TPU v7x, 32 devices: a whole 2x2x4 slice. The times are simulated.
32 devices in a mesh: groups: 2 (over x), tp: 16 (over z, y, core).
Axes of the slice: x: 2, y: 2, z: 4, core: 2. Of those that a mesh axis runs over, the one named last changes fastest.
Arguments:
- frames: bfloat16 [128, 1280], P(('groups', 'tp')), parts along dimension 0, may hold values from -6 to 6
- enc_gain: float32 [1280], replicated, may hold values from 0.1 to 1.9
- enc_shift: float32 [1280], replicated, may hold values from -1.75 to 1.75
- enc_up: bfloat16 [5120, 1280], P('tp'), may hold values from -0.15625 to 0.15625
- enc_up_bias: bfloat16 [5120], P('tp'), may hold values from -3 to 3
- enc_down: bfloat16 [5120, 1280], P('tp'), may hold values from -0.15625 to 0.15625
- enc_down_bias: float32 [1280], replicated, may hold values from -1.75 to 1.75
- post_gain: float32 [1280], replicated, may hold values from 0.1 to 1.9
- post_shift: float32 [1280], replicated, may hold values from -3 to 3
- proj_weight: bfloat16 [1280, 4096], P(None, 'tp'), may hold values from -0.15625 to 0.15625
- proj_bias: float32 [4096], P('tp'), may hold values from -1.75 to 1.75
- slot_source: int32 [128], P('groups'), parts along dimension 0, may hold values from -1 to 31, as said below
- prompt_embeds: bfloat16 [128, 4096], P(('groups', 'tp')), parts along dimension 0, may hold values from -6 to 6
- rms_gain: float32 [4096], replicated, may hold values from 0.1 to 1.9
- gate_weight: bfloat16 [4096, 11008], P(None, 'tp'), may hold values from -0.09375 to 0.09375
- up_weight: bfloat16 [4096, 11008], P(None, 'tp'), may hold values from -0.09375 to 0.09375
- down_weight: bfloat16 [11008, 4096], P('tp'), may hold values from -0.109375 to 0.109375
Outputs:
- prefill_out: bfloat16 [128, 4096], P(('groups', 'tp')), parts along dimension 0
There are 2 independent parts, one for each index of `groups`. A program takes and returns all parts, laid end to end along the dimension named above; an argument that names none is the same for every part. Nothing has to cross between parts.
Inputs may be any that keep to these rules, and one draw needn't show every extreme that they name: `slot_source`: each of the 32 pooled audio rows appears exactly once; the other 32 entries are -1. The same list is known to every device.
All inputs are finite; a program needn't handle non-finite values.
Results may differ from a plain program's by a relative error of at most 0.0072.
Values may be sent and summed in bfloat16 or wider, within the bound.
No kernel may reach another device: no remote copies, remote signals or barrier semaphores. Data moves between devices by JAX's collectives and lax.ppermute only.
A program may use at most 64 MiB of HBM per device.

v0:
```python
import jax
import jax.numpy as jnp
from jax import lax
from jax.sharding import PartitionSpec as P


def layer_norm(values, gain, shift):
    center = values - jnp.mean(values, axis=-1, keepdims=True)
    spread = jnp.mean(center * center, axis=-1, keepdims=True)
    return center * lax.rsqrt(spread + 1e-05) * gain + shift


def unit_block(normed, up_piece, bias_piece, down_piece):
    pre_act = lax.dot_general(
        normed, up_piece, (((1,), (1,)), ((), ())), preferred_element_type=jnp.float32
    )
    hidden_units = jax.nn.gelu(pre_act + bias_piece.astype(jnp.float32), approximate=False).astype(
        jnp.bfloat16
    )
    return jnp.dot(hidden_units, down_piece, preferred_element_type=jnp.float32)


def pool_norm(enc_out, post_gain, post_shift):
    paired = enc_out.reshape(enc_out.shape[0] // 2, 2, enc_out.shape[1])
    pooled = (paired[:, 0, :] + paired[:, 1, :]) * 0.5
    return layer_norm(pooled, post_gain, post_shift).astype(jnp.bfloat16)


def shards(
    frames,
    enc_gain,
    enc_shift,
    enc_up,
    enc_up_bias,
    enc_down,
    enc_down_bias,
    post_gain,
    post_shift,
    proj_weight,
    proj_bias,
    slot_source,
    prompt_embeds,
    rms_gain,
    gate_weight,
    up_weight,
    down_weight,
):
    resident = frames.astype(jnp.float32)
    gathered = lax.all_gather(frames, "tp", axis=0, tiled=True)
    normed = layer_norm(gathered.astype(jnp.float32), enc_gain, enc_shift).astype(jnp.bfloat16)
    partial_value = unit_block(normed, enc_up, enc_up_bias, enc_down)
    branch = lax.psum_scatter(partial_value, "tp", scatter_dimension=0, tiled=True)
    enc_out = resident + branch + enc_down_bias
    post_local = pool_norm(enc_out, post_gain, post_shift)
    post_every = lax.all_gather(post_local, "tp", axis=0, tiled=True)
    projected = (
        jnp.dot(post_every, proj_weight, preferred_element_type=jnp.float32) + proj_bias
    ).astype(jnp.bfloat16)
    clipped = jnp.maximum(slot_source, 0)
    outgoing = jnp.where(
        (slot_source >= 0)[:, None],
        jnp.take(projected, clipped, axis=0),
        jnp.zeros((), jnp.bfloat16),
    )
    arrived = lax.all_to_all(outgoing, "tp", split_axis=0, concat_axis=1, tiled=True)
    row_count = prompt_embeds.shape[0]
    owned = lax.dynamic_slice_in_dim(slot_source, lax.axis_index("tp") * row_count, row_count)
    packed = jnp.where((owned >= 0)[:, None], arrived, prompt_embeds)
    residual = packed.astype(jnp.float32)
    scale = lax.rsqrt(jnp.mean(residual * residual, axis=-1, keepdims=True) + 1e-06)
    lm_normed = (residual * scale * rms_gain).astype(jnp.bfloat16)
    piece = lax.all_gather(lm_normed, "tp", axis=0, tiled=True)
    gate = jnp.dot(piece, gate_weight, preferred_element_type=jnp.float32)
    lifted = jnp.dot(piece, up_weight, preferred_element_type=jnp.float32)
    lm_hidden = (jax.nn.silu(gate) * lifted).astype(jnp.bfloat16)
    summed = lax.psum_scatter(
        jnp.dot(lm_hidden, down_weight, preferred_element_type=jnp.float32),
        "tp",
        scatter_dimension=0,
        tiled=True,
    )
    return (residual + summed).astype(jnp.bfloat16)


def solution(mesh):
    placed = (
        P(("groups", "tp"), None),
        P(),
        P(),
        P("tp", None),
        P("tp"),
        P("tp", None),
        P(),
        P(),
        P(),
        P(None, "tp"),
        P("tp"),
        P("groups"),
        P(("groups", "tp"), None),
        P(),
        P(None, "tp"),
        P(None, "tp"),
        P("tp", None),
    )
    return jax.shard_map(
        shards, mesh=mesh, in_specs=placed, out_specs=P(("groups", "tp"), None), check_vma=False
    )
```

profile of v0, /device:TPU:0, one launch (start us, length us, event | category | flops | bytes accessed | tf_op | source)
XLA Modules:
  0.0 288.8 jit_solution(8041897194862616549)
XLA Ops:
  6.5 0.0 copy-start
  6.5 0.0 copy-start.5
  6.5 0.0 copy-start.4
  6.5 0.0 copy-start.1
  6.5 0.0 copy-start.2
  6.5 0.0 copy-start.3
  6.6 0.0 all-reduce.5.cloned.1.call-start
  6.6 23.9 %all-gather = bf16[16,4,1280]{2,1,0:T(4,128)(2,1)S(1)} all-gather(bf16[1,4,1280]{2,1,0:T(4,128)(2,1)} %bitcast.27), channel_id=1, replica_groups=mesh['groups'=2,'tp'=16] {'tp'}, dimensions={0}, use_global_device_ids=true | all-gather | bytes 174080 | tf_op jit(solution)/shard_map/all_gather | solution.py:49
  30.5 0.1 convert_reduce_fusion
  30.7 0.7 convert_element_type.36
  31.4 0.1 reshape.86
  31.5 0.2 multiply_reduce_fusion
  31.7 0.0 copy-done
  31.7 2.9 fusion.23
  34.6 0.0 all-reduce.5.cloned.1.call-update
  34.6 0.7 broadcast_compare_fusion.1
  35.3 0.7 broadcast_maximum_fusion
  35.9 0.1 broadcast_in_dim.52
  36.0 0.1 broadcast_in_dim.54
  36.1 1.2 dynamic-slice
  38.0 82.4 %all-reduce.5.cloned.1.call-done = f32[64,1280]{1,0:T(8,128)} async-done(((f32[64,1280]{1,0:T(8,128)}), f32[64,1280]{1,0:T(8,128)}) %all-reduce.5.cloned.1.call-update) | async-done | bytes 327696
  120.5 0.8 fusion.60
  121.3 0.1 fusion.94
  121.5 0.2 multiply_reduce_fusion.1
  121.7 0.8 fusion.62
  122.5 21.6 %all-gather.1 = bf16[16,2,1280]{2,1,0:T(2,128)(2,1)S(1)} all-gather(bf16[1,2,1280]{2,1,0:T(2,128)(2,1)S(1)} %fusion.62), channel_id=1, replica_groups=mesh['groups'=2,'tp'=16] {'tp'}, dimensions={0}, use_global_device_ids=true | all-gather | bytes 87040 | tf_op jit(solution)/shard_map/all_gather | solution.py:55
  144.1 0.0 copy-done.4
  144.1 0.0 copy-done.1
  144.2 0.2 fusion.2
  144.4 0.7 gather_fusion
  145.1 0.7 select_select_fusion
  145.8 3.5 %all-to-all-start = ((bf16[16,4,256]{2,1,0:T(4,128)(2,1)}), bf16[16,4,256]{2,1,0:T(4,128)(2,1)S(1)}, u32[]{:S(2)}, u32[]{:S(2)}) async-start(bf16[16,4,256]{2,1,0:T(4,128)(2,1)} %select_select_fusion), calls=%async_computation | async-start | bytes 65536 | tf_op jit(solution)/shard_map/all_to_all | solution.py:65
  149.4 0.0 all-reduce.7.cloned.1.call-start
  149.4 0.0 copy-done.5
  149.4 0.1 dynamic-slice_compare_fusion
  149.5 6.5 %all-to-all-done = bf16[16,4,256]{2,1,0:T(4,128)(2,1)S(1)} async-done(((bf16[16,4,256]{2,1,0:T(4,128)(2,1)}), bf16[16,4,256]{2,1,0:T(4,128)(2,1)S(1)}, u32[]{:S(2)}, u32[]{:S(2)}) %all-to-all-start) | async-done | bytes 32800 | tf_op jit(solution)/shard_map/all_to_all | solution.py:65
  156.0 0.0 copy-done.2
  156.0 0.2 fusion.24
  156.2 0.0 copy-done.3
  156.2 0.1 fusion.59
  156.3 19.0 %all-gather.2 = bf16[16,4,4096]{2,1,0:T(4,128)(2,1)S(1)} all-gather(bf16[1,4,4096]{2,1,0:T(4,128)(2,1)S(1)} %fusion.59), channel_id=1, replica_groups=mesh['groups'=2,'tp'=16] {'tp'}, dimensions={0}, use_global_device_ids=true | all-gather | bytes 557056 | tf_op jit(solution)/shard_map/all_gather | solution.py:72
  175.3 0.1 reshape.82
  175.4 4.4 %fusion.97 = f32[64,688]{1,0:T(8,128)S(1)} fusion(bf16[64,4096]{1,0:T(8,128)(2,1)S(1)} %reshape.82, bf16[4096,688]{0,1:T(8,128)(2,1)} %param.31), kind=kOutput, calls=%fused_computation.132 | convolution fusion | flops 360710144 | bytes 6336512 | tf_op jit(solution)/shard_map/dot_general | solution.py:73
  179.8 8.8 %fusion.1 = f32[64,4096]{1,0:T(8,128)} fusion(bf16[688,4096]{1,0:T(8,128)(2,1)} %param.33, bf16[64,4096]{1,0:T(8,128)(2,1)S(1)} %reshape.82, bf16[4096,688]{0,1:T(8,128)(2,1)} %param.32, f32[64,688]{1,0:T(8,128)S(1)} %fusion.97), kind=kOutput, calls=%fused_computation.3 | convolution fusion | flops 721684480 | bytes 13021184 | tf_op jit(solution)/shard_map/dot_general | solution.py:77
  188.6 0.0 all-reduce.7.cloned.1.call-update
  188.6 91.8 %all-reduce.7.cloned.1.call-done = f32[64,4096]{1,0:T(8,128)} async-done(((f32[64,4096]{1,0:T(8,128)}), f32[64,4096]{1,0:T(8,128)}) %all-reduce.7.cloned.1.call-update) | async-done | bytes 1048592
  280.4 1.5 fusion.27
  (11 shorter events, 0.2 us)
Async XLA Ops:
  6.5 25.2 %copy-start = (bf16[320,1280]{1,0:T(8,128)(2,1)S(1)}, bf16[320,1280]{1,0:T(8,128)(2,1)}, u32[]{:S(2)}) copy-start(bf16[320,1280]{1,0:T(8,128)(2,1)} %param.22) | copy-start | bytes 2457604
  6.5 142.9 %copy-start.5 = (s32[64]{0:T(128)S(1)}, s32[64]{0:T(128)}, u32[]{:S(2)}) copy-start(s32[64]{0:T(128)} %param.28) | copy-start | bytes 772
  6.5 137.6 %copy-start.4 = (f32[256]{0:T(256)S(1)}, f32[256]{0:T(256)}, u32[]{:S(2)}) copy-start(f32[256]{0:T(256)} %param.27) | copy-start | bytes 3076
  6.5 137.6 %copy-start.1 = (bf16[1280,256]{1,0:T(8,128)(2,1)S(1)}, bf16[1280,256]{1,0:T(8,128)(2,1)}, u32[]{:S(2)}) copy-start(bf16[1280,256]{1,0:T(8,128)(2,1)} %param.26) | copy-start | bytes 1966084
  6.5 149.4 %copy-start.2 = (bf16[4,4096]{1,0:T(4,128)(2,1)S(1)}, bf16[4,4096]{1,0:T(4,128)(2,1)}, u32[]{:S(2)}) copy-start(bf16[4,4096]{1,0:T(4,128)(2,1)} %param.29) | copy-start | bytes 98308
  6.5 149.6 %copy-start.3 = (f32[4096]{0:T(1024)S(1)}, f32[4096]{0:T(1024)}, u32[]{:S(2)}) copy-start(f32[4096]{0:T(1024)} %param.30) | copy-start | bytes 49156
  6.6 113.9 %all-reduce.5.cloned.1.call-start = ((), (), s32[]{:S(2)}) async-start(), calls=%async_computation.1 | async-start | bytes 655360
  145.8 10.1 %all-to-all-start = ((bf16[16,4,256]{2,1,0:T(4,128)(2,1)}), bf16[16,4,256]{2,1,0:T(4,128)(2,1)S(1)}, u32[]{:S(2)}, u32[]{:S(2)}) async-start(bf16[16,4,256]{2,1,0:T(4,128)(2,1)} %select_select_fusion), calls=%async_computation | async-start | bytes 65536 | tf_op jit(solution)/shard_map/all_to_all | solution.py:65
  149.4 131.0 %all-reduce.7.cloned.1.call-start = ((), (), s32[]{:S(2)}) async-start(), calls=%async_computation.2 | async-start | bytes 2097152
Sparse Core Ops, SparseCore 0:
  34.7 85.7 all-reduce.4
  188.7 91.6 all-reduce.6
where the time goes:
time: 289 us
  waiting for transfers between devices  181 us (63%)
  blocking collectives  64.6 us (22%)
  matrix products  16.2 us (6%)
  between operations  14.2 us (5%)
  other arithmetic  6.98 us (2%)
  starting transfers between devices  3.58 us (1%)
    unnamed x4, waiting for transfers between devices  174 us
    all_gather x1, blocking collectives, shards(): gathered = lax.all_gather(frames, 'tp', axis=0, tiled=True)  23.9 us
    all_gather x1, blocking collectives, shards(): post_every = lax.all_gather(post_local, 'tp', axis=0, tiled=True)  21.6 us
    all_gather x1, blocking collectives, shards(): piece = lax.all_gather(lm_normed, 'tp', axis=0, tiled=True)  19 us
    dot_general x1, matrix products, shards(): jnp.dot(lm_hidden, down_weight, preferred_element_type=jnp.float32)  8.76 us
    all_to_all x1, waiting for transfers between devices, shards(): lax.all_to_all(outgoing, 'tp', split_axis=0, concat_axis=1, tiled=True)  6.45 us
  transfers between devices with their start and end apart: 3, of which 3 were waited for; matrix products, arithmetic and copies ran while one was open for 1% of the time, Pallas kernels for 0%

commit v1 on v0

v1 whole, which is shorter than its diff:
```python
import jax
import jax.numpy as jnp
from jax import lax
from jax.sharding import PartitionSpec as P


def layer_norm(values, gain, shift):
    center = values - jnp.mean(values, axis=-1, keepdims=True)
    spread = jnp.mean(center * center, axis=-1, keepdims=True)
    return center * lax.rsqrt(spread + 1e-05) * gain + shift


def to_every(piece, count):
    spread = jnp.broadcast_to(piece[None], (count,) + piece.shape)
    return lax.all_to_all(spread, "tp", 0, 0)


def reduce_rows(partial_value, count):
    rows, width = partial_value.shape
    pieces = partial_value.astype(jnp.bfloat16).reshape(count, rows // count, width)
    return jnp.sum(lax.all_to_all(pieces, "tp", 0, 0).astype(jnp.float32), axis=0)


def pool(values):
    paired = values.reshape(values.shape[0] // 2, 2, values.shape[1])
    return (paired[:, 0, :] + paired[:, 1, :]) * 0.5


def shards(
    frames,
    enc_gain,
    enc_shift,
    enc_up,
    enc_up_bias,
    enc_down,
    enc_down_bias,
    post_gain,
    post_shift,
    proj_weight,
    proj_bias,
    slot_source,
    prompt_embeds,
    rms_gain,
    gate_weight,
    up_weight,
    down_weight,
):
    count = lax.axis_size("tp")
    me = lax.axis_index("tp")
    gathered = to_every(frames, count).reshape(-1, frames.shape[1])
    prompts = to_every(prompt_embeds, count).reshape(-1, prompt_embeds.shape[1])
    normed = layer_norm(gathered.astype(jnp.float32), enc_gain, enc_shift).astype(jnp.bfloat16)
    pre_act = lax.dot_general(
        normed, enc_up, (((1,), (1,)), ((), ())), preferred_element_type=jnp.float32
    )
    hidden = jax.nn.gelu(pre_act + enc_up_bias.astype(jnp.float32), approximate=False)
    partial_value = jnp.dot(
        hidden.astype(jnp.bfloat16), enc_down, preferred_element_type=jnp.float32
    )
    branch = reduce_rows(pool(partial_value), count)
    pooled = pool(frames.astype(jnp.float32)) + branch + enc_down_bias
    post = layer_norm(pooled, post_gain, post_shift).astype(jnp.bfloat16)
    post_every = to_every(post, count).reshape(-1, post.shape[1])
    projected = (
        jnp.dot(post_every, proj_weight, preferred_element_type=jnp.float32) + proj_bias
    ).astype(jnp.bfloat16)
    features = to_every(projected, count)
    features = jnp.transpose(features, (1, 0, 2)).reshape(projected.shape[0], -1)
    clipped = jnp.maximum(slot_source, 0)
    packed = jnp.where(
        (slot_source >= 0)[:, None], jnp.take(features, clipped, axis=0), prompts
    )
    residual = packed.astype(jnp.float32)
    scale = lax.rsqrt(jnp.mean(residual * residual, axis=-1, keepdims=True) + 1e-06)
    lm_normed = (residual * scale * rms_gain).astype(jnp.bfloat16)
    gate = jnp.dot(lm_normed, gate_weight, preferred_element_type=jnp.float32)
    lifted = jnp.dot(lm_normed, up_weight, preferred_element_type=jnp.float32)
    lm_hidden = (jax.nn.silu(gate) * lifted).astype(jnp.bfloat16)
    summed = reduce_rows(
        jnp.dot(lm_hidden, down_weight, preferred_element_type=jnp.float32), count
    )
    row_count = prompt_embeds.shape[0]
    own = lax.dynamic_slice_in_dim(packed, me * row_count, row_count).astype(jnp.float32)
    return (own + summed).astype(jnp.bfloat16)


def solution(mesh):
    placed = (
        P(("groups", "tp"), None),
        P(),
        P(),
        P("tp", None),
        P("tp"),
        P("tp", None),
        P(),
        P(),
        P(),
        P(None, "tp"),
        P("tp"),
        P("groups"),
        P(("groups", "tp"), None),
        P(),
        P(None, "tp"),
        P(None, "tp"),
        P("tp", None),
    )
    return jax.shard_map(
        shards, mesh=mesh, in_specs=placed, out_specs=P(("groups", "tp"), None), check_vma=False
    )
```

time: 289 us -> 111 us (0.38)
  waiting for transfers between devices: 181 us -> 52.4 us
  blocking collectives: 64.6 us -> 9.73 us
  starting transfers between devices: 3.58 us -> 22.1 us
  between operations: 14.2 us -> 0.3 us
  local copies, waits for them, and re-layouts: 2.5 us -> 7.8 us
  other arithmetic: 6.98 us -> 3.34 us
    unnamed x4 -> x0, waiting for transfers between devices: 174 us -> none
    all_gather x3 -> x0, blocking collectives: 64.6 us -> none  [the longest x1 23.9 us: shards(): gathered = lax.all_gather(frames, 'tp', axis=0, tiled=True)]
    all_to_all x1 -> x5, waiting for transfers between devices: 6.45 us -> 52.4 us  [the longest x3 30.9 us: to_every(): return lax.all_to_all(spread, 'tp', 0, 0)]
    all_to_all x1 -> x5, starting transfers between devices: 3.5 us -> 22.1 us  [the longest x3 15 us: to_every(): return lax.all_to_all(spread, 'tp', 0, 0)]
    all_to_all x0 -> x1, blocking collectives: none -> 9.73 us  [to_every(): return lax.all_to_all(spread, 'tp', 0, 0)]
    broadcast_in_dim x2 -> x6, local copies, waits for them, and re-layouts: 0.18 us -> 3.43 us  [the longest x4 3.25 us: to_every(): spread = jnp.broadcast_to(piece[None], (count,) + piece.shape)]
  transfers between devices with their start and end apart: 3 -> 5, of which waited for: 3 -> 5; matrix products, arithmetic and copies ran while one was open for 1% -> 2% of each run, Pallas kernels for 0% -> 0%
where the time goes in v1:
time: 111 us; the launch traced here: 110 us
  waiting for transfers between devices  52.4 us (47%)
  starting transfers between devices  22.1 us (20%)
  matrix products  14.5 us (13%)
  blocking collectives  9.73 us (9%)
  local copies, waits for them, and re-layouts  7.8 us (7%)
  other arithmetic  3.34 us (3%)
    all_to_all x3, waiting for transfers between devices, to_every(): return lax.all_to_all(spread, 'tp', 0, 0)  30.9 us
    all_to_all x2, waiting for transfers between devices, reduce_rows(): lax.all_to_all(pieces, 'tp', 0, 0).astype(jnp.float32)  21.5 us
    all_to_all x3, starting transfers between devices, to_every(): return lax.all_to_all(spread, 'tp', 0, 0)  15 us
    all_to_all x1, blocking collectives, to_every(): return lax.all_to_all(spread, 'tp', 0, 0)  9.73 us
    dot_general x1, matrix products, shards(): jnp.dot(lm_hidden, down_weight, preferred_element_type=jnp.float32)  7.74 us
    all_to_all x2, starting transfers between devices, reduce_rows(): lax.all_to_all(pieces, 'tp', 0, 0).astype(jnp.float32)  7.07 us
    dot_general x1, matrix products, shards(): gate = jnp.dot(lm_normed, gate_weight, preferred_element_type=jnp.float32)  4.4 us
    broadcast_in_dim x4, local copies, waits for them, and re-layouts, to_every(): spread = jnp.broadcast_to(piece[None], (count,) + piece.shape)  3.25 us
  transfers between devices with their start and end apart: 5, of which 5 were waited for; matrix products, arithmetic and copies ran while one was open for 2% of the time, Pallas kernels for 0%

profile of v1, /device:TPU:0, one launch (start us, length us, event | category | flops | bytes accessed | tf_op | source)
XLA Modules:
  0.0 110.1 jit_solution(6334944278081777460)
XLA Ops:
  0.0 0.0 copy-start
  0.0 0.0 copy-start.4
  0.0 0.0 copy-start.5
  0.0 0.0 copy-start.6
  0.0 0.0 copy-start.3
  0.0 0.0 copy-start.1
  0.0 0.0 copy-start.7
  0.0 0.0 copy-start.8
  0.1 1.5 %broadcast_in_dim.40 = bf16[16,4,1280]{2,1,0:T(4,128)(2,1)} broadcast(bf16[4,1280]{1,0:T(4,128)(2,1)} %param.17), dimensions={1,2} | broadcast | bytes 174080 | tf_op jit(solution)/shard_map/broadcast_in_dim | solution.py:14
  1.6 7.4 %all-to-all-start = ((bf16[16,4,1280]{2,1,0:T(4,128)(2,1)}), bf16[16,4,1280]{2,1,0:T(4,128)(2,1)S(1)}, u32[]{:S(2)}, u32[]{:S(2)}) async-start(bf16[16,4,1280]{2,1,0:T(4,128)(2,1)} %broadcast_in_dim.40), calls=%async_computation | async-start | bytes 327680 | tf_op jit(solution)/shard_map/all_to_all | solution.py:15
  9.0 0.7 reshape.214
  9.7 0.7 convert_element_type.68
  10.4 7.1 %all-to-all-done = bf16[16,4,1280]{2,1,0:T(4,128)(2,1)S(1)} async-done(((bf16[16,4,1280]{2,1,0:T(4,128)(2,1)}), bf16[16,4,1280]{2,1,0:T(4,128)(2,1)S(1)}, u32[]{:S(2)}, u32[]{:S(2)}) %all-to-all-start) | async-done | bytes 163872 | tf_op jit(solution)/shard_map/all_to_all | solution.py:15
  17.4 0.1 convert_reduce_fusion.1
  17.6 0.1 div.25
  17.7 0.2 multiply_reduce_fusion.1
  17.9 0.1 rsqrt.31
  18.0 0.0 copy-done
  18.1 2.2 %fusion.25 = f32[64,1280]{1,0:T(8,128)S(1)} fusion(bf16[320,1280]{1,0:T(8,128)(2,1)S(1)} %copy-done, bf16[320,1280]{1,0:T(8,128)(2,1)} %param.20, f32[64,1280]{1,0:T(8,128)S(1)} %reshape.215, f32[1280]{0:T(1024)} %param.19, f32[1280]{0:T(1024)} %param.18, f32[64]{0:T(128)S(1)} %rsqrt.31, f32[64]{0:T(128)S(1)} %div.25, f32[320]{0:T(512)S(1)} %convert_element_type.68), kind=kOutput, calls=%fused_computation.48 | convolution fusion | flops 106618880 | bytes 2305792 | tf_op jit(solution)/shard_map/dot_general | solution.py:57
  20.2 0.2 reshape.208
  20.4 0.3 fusion.92
  20.7 0.7 convert_element_type.71
  21.4 3.5 %all-to-all-start.1 = ((bf16[16,2,1280]{2,1,0:T(2,128)(2,1)}), bf16[16,2,1280]{2,1,0:T(2,128)(2,1)S(1)}, u32[]{:S(2)}, u32[]{:S(2)}) async-start(bf16[16,2,1280]{2,1,0:T(2,128)(2,1)} %convert_element_type.71), calls=%async_computation.1 | async-start | bytes 163840 | tf_op jit(solution)/shard_map/all_to_all | solution.py:21
  24.9 7.1 %all-to-all-done.1 = bf16[16,2,1280]{2,1,0:T(2,128)(2,1)S(1)} async-done(((bf16[16,2,1280]{2,1,0:T(2,128)(2,1)}), bf16[16,2,1280]{2,1,0:T(2,128)(2,1)S(1)}, u32[]{:S(2)}, u32[]{:S(2)}) %all-to-all-start.1) | async-done | bytes 81952 | tf_op jit(solution)/shard_map/all_to_all | solution.py:21
  32.0 0.1 convert_reduce_fusion.2
  32.1 0.0 copy-done.4
  32.1 0.1 fusion.90
  32.2 0.2 multiply_reduce_fusion.2
  32.4 0.0 copy-done.5
  32.4 0.0 copy-done.6
  32.4 0.1 add_convert_fusion.7
  32.6 9.7 %all_to_all.30 = bf16[16,2,1280]{2,1,0:T(2,128)(2,1)S(1)} all-to-all(bf16[16,2,1280]{2,1,0:T(2,128)(2,1)S(1)} %broadcast_in_dim.41), channel_id=1, replica_groups=mesh['groups'=2,'tp'=16] {'tp'}, dimensions={0} | all-to-all | bytes 163840 | tf_op jit(solution)/shard_map/all_to_all | solution.py:15
  42.3 0.0 copy-done.3
  42.3 1.0 broadcast_in_dim.75
  43.3 3.6 %all-to-all-start.4 = ((bf16[16,4,4096]{2,1,0:T(4,128)(2,1)}), bf16[16,4,4096]{2,1,0:T(4,128)(2,1)S(1)}, u32[]{:S(2)}, u32[]{:S(2)}) async-start(bf16[16,4,4096]{2,1,0:T(4,128)(2,1)} %broadcast_in_dim.75), calls=%async_computation.4 | async-start | bytes 1048576 | tf_op jit(solution)/shard_map/all_to_all | solution.py:15
  46.9 0.0 copy-done.1
  46.9 0.0 copy-done.7
  46.9 0.0 copy-start.2
  46.9 0.2 fusion.1
  47.1 14.1 %all-to-all-done.4 = bf16[16,4,4096]{2,1,0:T(4,128)(2,1)S(1)} async-done(((bf16[16,4,4096]{2,1,0:T(4,128)(2,1)}), bf16[16,4,4096]{2,1,0:T(4,128)(2,1)S(1)}, u32[]{:S(2)}, u32[]{:S(2)}) %all-to-all-start.4) | async-done | bytes 524320 | tf_op jit(solution)/shard_map/all_to_all | solution.py:15
  61.3 0.7 broadcast_in_dim.72
  62.0 4.0 %all-to-all-start.3 = ((bf16[16,32,256]{2,1,0:T(8,128)(2,1)}), bf16[16,32,256]{2,1,0:T(8,128)(2,1)S(1)}, u32[]{:S(2)}, u32[]{:S(2)}) async-start(bf16[16,32,256]{2,1,0:T(8,128)(2,1)} %broadcast_in_dim.72), calls=%async_computation.3 | async-start | bytes 524288 | tf_op jit(solution)/shard_map/all_to_all | solution.py:15
  66.0 0.0 copy-done.8
  66.0 0.1 broadcast_in_dim.78
  66.1 0.1 broadcast_in_dim.76
  66.3 0.1 reshape.211
  66.4 9.7 %all-to-all-done.3 = bf16[16,32,256]{2,1,0:T(8,128)(2,1)S(1)} async-done(((bf16[16,32,256]{2,1,0:T(8,128)(2,1)}), bf16[16,32,256]{2,1,0:T(8,128)(2,1)S(1)}, u32[]{:S(2)}, u32[]{:S(2)}) %all-to-all-start.3) | async-done | bytes 262176 | tf_op jit(solution)/shard_map/all_to_all | solution.py:15
  76.1 0.9 gather_fusion
  77.0 0.2 gather.7
  77.2 0.2 select_select_fusion
  77.3 0.7 multiply_reduce_fusion
  78.0 0.1 rsqrt.34
  78.1 0.0 copy-done.2
  78.1 4.4 %fusion.13 = f32[64,688]{1,0:T(8,128)S(1)} fusion(bf16[4096,688]{0,1:T(8,128)(2,1)} %param.31, bf16[64,4096]{1,0:T(8,128)(2,1)S(1)} %select_select_fusion, f32[4096]{0:T(1024)S(1)} %copy-done.2, f32[64]{0:T(128)S(1)} %rsqrt.34), kind=kOutput, calls=%fused_computation.28 | convolution fusion | flops 361758720 | bytes 6353152 | tf_op jit(solution)/shard_map/dot_general | solution.py:76
  82.5 7.7 %convolution_convert_fusion = bf16[64,4096]{1,0:T(8,128)(2,1)S(1)} fusion(bf16[688,4096]{1,0:T(8,128)(2,1)} %param.33, bf16[4096,688]{0,1:T(8,128)(2,1)} %param.32, f32[64,688]{1,0:T(8,128)S(1)} %fusion.13, bf16[64,4096]{1,0:T(8,128)(2,1)S(1)} %select_select_fusion, f32[4096]{0:T(1024)S(1)} %copy-done.2, f32[64]{0:T(128)S(1)} %rsqrt.34), kind=kOutput, calls=%fused_computation.1 | convolution fusion | flops 722995200 | bytes 12513536 | tf_op jit(solution)/shard_map/dot_general | solution.py:80
  90.3 1.0 reshape.212
  91.2 3.6 %all-to-all-start.5 = ((bf16[16,4,4096]{2,1,0:T(4,128)(2,1)}), bf16[16,4,4096]{2,1,0:T(4,128)(2,1)S(1)}, u32[]{:S(2)}, u32[]{:S(2)}) async-start(bf16[16,4,4096]{2,1,0:T(4,128)(2,1)} %reshape.212), calls=%async_computation.5 | async-start | bytes 1048576 | tf_op jit(solution)/shard_map/all_to_all | solution.py:21
  94.8 14.4 %all-to-all-done.5 = bf16[16,4,4096]{2,1,0:T(4,128)(2,1)S(1)} async-done(((bf16[16,4,4096]{2,1,0:T(4,128)(2,1)}), bf16[16,4,4096]{2,1,0:T(4,128)(2,1)S(1)}, u32[]{:S(2)}, u32[]{:S(2)}) %all-to-all-start.5) | async-done | bytes 524320 | tf_op jit(solution)/shard_map/all_to_all | solution.py:21
  109.2 0.2 convert_reduce_fusion
  109.5 0.6 add_convert_fusion.6
  (14 shorter events, 0.2 us)
Async XLA Ops:
  0.0 18.0 %copy-start = (bf16[320,1280]{1,0:T(8,128)(2,1)S(1)}, bf16[320,1280]{1,0:T(8,128)(2,1)}, u32[]{:S(2)}) copy-start(bf16[320,1280]{1,0:T(8,128)(2,1)} %param.22) | copy-start | bytes 2457604
  0.0 32.1 %copy-start.4 = (f32[1280]{0:T(1024)S(1)}, f32[1280]{0:T(1024)}, u32[]{:S(2)}) copy-start(f32[1280]{0:T(1024)} %param.23) | copy-start | bytes 15364
  0.0 32.4 %copy-start.5 = (f32[1280]{0:T(1024)S(1)}, f32[1280]{0:T(1024)}, u32[]{:S(2)}) copy-start(f32[1280]{0:T(1024)} %param.25) | copy-start | bytes 15364
  0.0 32.4 %copy-start.6 = (f32[1280]{0:T(1024)S(1)}, f32[1280]{0:T(1024)}, u32[]{:S(2)}) copy-start(f32[1280]{0:T(1024)} %param.24) | copy-start | bytes 15364
  0.0 42.3 %copy-start.3 = (bf16[4,4096]{1,0:T(4,128)(2,1)S(1)}, bf16[4,4096]{1,0:T(4,128)(2,1)}, u32[]{:S(2)}) copy-start(bf16[4,4096]{1,0:T(4,128)(2,1)} %param.29) | copy-start | bytes 98308
  0.0 46.9 %copy-start.1 = (bf16[1280,256]{1,0:T(8,128)(2,1)S(1)}, bf16[1280,256]{1,0:T(8,128)(2,1)}, u32[]{:S(2)}) copy-start(bf16[1280,256]{1,0:T(8,128)(2,1)} %param.26) | copy-start | bytes 1966084
  0.0 46.9 %copy-start.7 = (f32[256]{0:T(256)S(1)}, f32[256]{0:T(256)}, u32[]{:S(2)}) copy-start(f32[256]{0:T(256)} %param.27) | copy-start | bytes 3076
  0.0 66.0 %copy-start.8 = (s32[64]{0:T(128)S(1)}, s32[64]{0:T(128)}, u32[]{:S(2)}) copy-start(s32[64]{0:T(128)} %param.28) | copy-start | bytes 772
  1.6 15.9 %all-to-all-start = ((bf16[16,4,1280]{2,1,0:T(4,128)(2,1)}), bf16[16,4,1280]{2,1,0:T(4,128)(2,1)S(1)}, u32[]{:S(2)}, u32[]{:S(2)}) async-start(bf16[16,4,1280]{2,1,0:T(4,128)(2,1)} %broadcast_in_dim.40), calls=%async_computation | async-start | bytes 327680 | tf_op jit(solution)/shard_map/all_to_all | solution.py:15
  21.4 10.6 %all-to-all-start.1 = ((bf16[16,2,1280]{2,1,0:T(2,128)(2,1)}), bf16[16,2,1280]{2,1,0:T(2,128)(2,1)S(1)}, u32[]{:S(2)}, u32[]{:S(2)}) async-start(bf16[16,2,1280]{2,1,0:T(2,128)(2,1)} %convert_element_type.71), calls=%async_computation.1 | async-start | bytes 163840 | tf_op jit(solution)/shard_map/all_to_all | solution.py:21
  43.3 18.0 %all-to-all-start.4 = ((bf16[16,4,4096]{2,1,0:T(4,128)(2,1)}), bf16[16,4,4096]{2,1,0:T(4,128)(2,1)S(1)}, u32[]{:S(2)}, u32[]{:S(2)}) async-start(bf16[16,4,4096]{2,1,0:T(4,128)(2,1)} %broadcast_in_dim.75), calls=%async_computation.4 | async-start | bytes 1048576 | tf_op jit(solution)/shard_map/all_to_all | solution.py:15
  46.9 31.2 %copy-start.2 = (f32[4096]{0:T(1024)S(1)}, f32[4096]{0:T(1024)}, u32[]{:S(2)}) copy-start(f32[4096]{0:T(1024)} %param.30) | copy-start | bytes 49156
  62.0 14.1 %all-to-all-start.3 = ((bf16[16,32,256]{2,1,0:T(8,128)(2,1)}), bf16[16,32,256]{2,1,0:T(8,128)(2,1)S(1)}, u32[]{:S(2)}, u32[]{:S(2)}) async-start(bf16[16,32,256]{2,1,0:T(8,128)(2,1)} %broadcast_in_dim.72), calls=%async_computation.3 | async-start | bytes 524288 | tf_op jit(solution)/shard_map/all_to_all | solution.py:15
  91.2 18.0 %all-to-all-start.5 = ((bf16[16,4,4096]{2,1,0:T(4,128)(2,1)}), bf16[16,4,4096]{2,1,0:T(4,128)(2,1)S(1)}, u32[]{:S(2)}, u32[]{:S(2)}) async-start(bf16[16,4,4096]{2,1,0:T(4,128)(2,1)} %reshape.212), calls=%async_computation.5 | async-start | bytes 1048576 | tf_op jit(solution)/shard_map/all_to_all | solution.py:21

commit v2 on v1

--- a/solution.py
+++ b/solution.py
@@ -1,7 +1,217 @@
+import functools
+
 import jax
 import jax.numpy as jnp
 from jax import lax
+from jax.experimental import pallas as pl
+from jax.experimental.pallas import tpu as pltpu
 from jax.sharding import PartitionSpec as P
+
+
+def mask_of(bit):
+    return (1 << bit) | 1 if bit else 1
+
+
+def slot_of(offset, bits):
+    parity = offset & 1
+    slot = 0
+    for bit in range(1, bits):
+        one = (offset >> bit) & 1
+        parity = parity ^ one
+        slot = slot + (one << (bits - 1 - bit))
+    return slot + (parity << (bits - 1))
+
+
+def offset_of(slot, bits):
+    offset = (slot >> (bits - 1)) & 1
+    for bit in range(1, bits):
+        offset = offset ^ (((slot >> (bits - 1 - bit)) & 1) * mask_of(bit))
+    return offset
+
+
+def swap(value, bit, count):
+    pairs = [(i, i ^ mask_of(bit)) for i in range(count)]
+    return lax.ppermute(value, "tp", pairs)
+
+
+def gather_slots(value, bits):
+    for bit in list(range(bits - 1, 0, -1)) + [0]:
+        value = jnp.concatenate([value, swap(value, bit, 1 << bits)], axis=0)
+    return value
+
+
+def in_hbm(value):
+    return pltpu.with_memory_space_constraint(value, pltpu.HBM)
+
+
+def row(ref, part=slice(None)):
+    return ref[part].reshape(1, -1)
+
+
+def dot_last(left, right):
+    return lax.dot_general(
+        left, right, (((1,), (1,)), ((), ())), preferred_element_type=jnp.float32
+    )
+
+
+def encoder_kernel(
+    bits, me_ref, frames, gain, shift, bias, down_bias, up_hbm, down_hbm, gate_hbm,
+    send, keep, base, gate, up, down, sems,
+):
+    copies = [
+        pltpu.make_async_copy(source, target, sems.at[i])
+        for i, (source, target) in enumerate(((up_hbm, up), (down_hbm, down), (gate_hbm, gate)))
+    ]
+    for copy in copies:
+        copy.start()
+    me = me_ref[0]
+    rows, width = frames.shape
+    pooled = rows // 2
+    half = pooled // 2
+    own = rows >> bits
+    out_row = lax.broadcasted_iota(jnp.int32, (rows, rows), 0)
+    in_row = lax.broadcasted_iota(jnp.int32, (rows, rows), 1)
+    frame = jnp.where(out_row < pooled, 2 * out_row, 2 * (out_row - pooled) + 1)
+    place = slot_of((frame // own) ^ me, bits) * own + frame % own
+    order = jnp.where(place == in_row, 1.0, 0.0).astype(jnp.bfloat16)
+    values = jnp.dot(order, frames[...], preferred_element_type=jnp.float32)
+    both = (values[:pooled] + values[pooled:]) * 0.5 + row(down_bias)
+    center = values - jnp.mean(values, axis=-1, keepdims=True)
+    spread = jnp.mean(center * center, axis=-1, keepdims=True)
+    normed = (center * lax.rsqrt(spread + 1e-05) * row(gain) + row(shift)).astype(jnp.bfloat16)
+    copies[0].wait()
+    pre_act = dot_last(normed, up[...]) + row(bias).astype(jnp.float32)
+    hidden = (0.5 * pre_act * (1.0 + lax.erf(pre_act * 0.7071067811865476))).astype(jnp.bfloat16)
+    copies[1].wait()
+    result = jnp.dot(hidden, down[...], preferred_element_type=jnp.float32)
+    mine = (result[:pooled] + result[pooled:]) * 0.5
+    parity = me
+    for bit in range(1, bits):
+        parity = parity ^ (me >> bit)
+    upper = (parity & 1) == 1
+    keep[...] = jnp.where(upper, mine[half:], mine[:half])
+    send[...] = jnp.where(upper, mine[:half], mine[half:]).astype(jnp.bfloat16)
+    base[...] = jnp.where(upper, both[half:], both[:half])
+    copies[2].wait()
+
+
+def encoder(me, frames, gain, shift, bias, down_bias, up, down, gate, bits):
+    rows, width = frames.shape
+    half = rows // 4
+    vmem = pl.BlockSpec(memory_space=pltpu.VMEM)
+    hbm = pl.BlockSpec(memory_space=pltpu.HBM)
+    return pl.pallas_call(
+        functools.partial(encoder_kernel, bits),
+        out_shape=[
+            jax.ShapeDtypeStruct((half, width), jnp.bfloat16),
+            jax.ShapeDtypeStruct((half, width), jnp.float32),
+            jax.ShapeDtypeStruct((half, width), jnp.float32),
+            pltpu.VMEM(gate.shape, gate.dtype),
+        ],
+        in_specs=[pl.BlockSpec(memory_space=pltpu.SMEM)] + [vmem] * 5 + [hbm] * 3,
+        out_specs=[vmem] * 4,
+        scratch_shapes=[
+            pltpu.VMEM(up.shape, up.dtype),
+            pltpu.VMEM(down.shape, down.dtype),
+            pltpu.SemaphoreType.DMA((3,)),
+        ],
+        compiler_params=pltpu.CompilerParams(vmem_limit_bytes=12 * 2**20),
+        cost_estimate=pl.CostEstimate(
+            flops=4 * rows * up.size, bytes_accessed=4 * up.size + 2 * gate.size, transcendentals=0
+        ),
+    )(me, frames, gain, shift, bias, down_bias, in_hbm(up), in_hbm(down), in_hbm(gate))
+
+
+def language_kernel(
+    bits, pieces, me_ref, features, source, prompts, gain, gate, up_hbm, down_hbm,
+    send, keep, packed, up, down, sems,
+):
+    count, audio, columns = features.shape
+    rows, width = prompts.shape
+    half = rows // 2
+    own = rows >> bits
+    span = width // pieces
+    parts = [slice(i * span, (i + 1) * span) for i in range(pieces)]
+    ups = [
+        pltpu.make_async_copy(
+            up_hbm.at[:, pl.ds(i * span, span)], up.at[:, pl.ds(i * span, span)], sems.at[i]
+        )
+        for i in range(pieces)
+    ]
+    downs = [
+        pltpu.make_async_copy(
+            down_hbm.at[:, pl.ds(i * span, span)],
+            down.at[:, pl.ds(i * span, span)],
+            sems.at[pieces + i],
+        )
+        for i in range(pieces)
+    ]
+    for copy in ups + downs:
+        copy.start()
+    me = me_ref[0]
+    out_row = lax.broadcasted_iota(jnp.int32, (rows, rows), 0)
+    in_row = lax.broadcasted_iota(jnp.int32, (rows, rows), 1)
+    place = (offset_of(out_row // own, bits) ^ me) * own + out_row % own
+    order = jnp.where(place == in_row, 1.0, 0.0).astype(jnp.bfloat16)
+    wanted = lax.broadcasted_iota(jnp.int32, (audio, rows), 0)
+    chosen = jnp.where(row(source) == wanted, 1.0, 0.0).astype(jnp.bfloat16)
+    pick = dot_last(order, chosen)
+    audio_row = jnp.sum(pick, axis=1, keepdims=True) > 0.5
+    pick = pick.astype(jnp.bfloat16)
+    squares = jnp.zeros((rows, columns), jnp.float32)
+    for device in range(count):
+        part = slice(device * columns, (device + 1) * columns)
+        found = jnp.dot(
+            pick, features[slot_of(me ^ device, bits)], preferred_element_type=jnp.float32
+        )
+        value = jnp.where(audio_row, found, prompts[:, part].astype(jnp.float32))
+        squares += value * value
+        packed[:, part] = value.astype(jnp.bfloat16)
+    scale = lax.rsqrt(jnp.sum(squares, axis=1, keepdims=True) / width + 1e-06)
+
+    def normed(part):
+        return (packed[:, part].astype(jnp.float32) * scale * row(gain, part)).astype(jnp.bfloat16)
+
+    gated = sum(dot_last(normed(part), gate[:, part]) for part in parts)
+    lifted = 0.0
+    for part, copy in zip(parts, ups):
+        copy.wait()
+        lifted += dot_last(normed(part), up[:, part])
+    hidden = (gated * jax.nn.sigmoid(gated) * lifted).astype(jnp.bfloat16)
+    held = lax.broadcasted_iota(jnp.int32, (half, 1), 0) < own
+    for part, copy in zip(parts, downs):
+        copy.wait()
+        result = jnp.dot(hidden, down[:, part], preferred_element_type=jnp.float32)
+        send[:, part] = result[half:].astype(jnp.bfloat16)
+        keep[:, part] = result[:half] + jnp.where(
+            held, packed[:half, part].astype(jnp.float32), 0.0
+        )
+
+
+def language(me, features, source, prompts, gain, gate, up, down, bits):
+    rows, width = prompts.shape
+    pieces = 4
+    vmem = pl.BlockSpec(memory_space=pltpu.VMEM)
+    hbm = pl.BlockSpec(memory_space=pltpu.HBM)
+    return pl.pallas_call(
+        functools.partial(language_kernel, bits, pieces),
+        out_shape=[
+            jax.ShapeDtypeStruct((rows // 2, width), jnp.bfloat16),
+            jax.ShapeDtypeStruct((rows // 2, width), jnp.float32),
+        ],
+        in_specs=[pl.BlockSpec(memory_space=pltpu.SMEM)] + [vmem] * 5 + [hbm] * 2,
+        out_specs=[vmem] * 2,
+        scratch_shapes=[
+            pltpu.VMEM((rows, width), jnp.bfloat16),
+            pltpu.VMEM(up.shape, up.dtype),
+            pltpu.VMEM(down.shape, down.dtype),
+            pltpu.SemaphoreType.DMA((2 * pieces,)),
+        ],
+        compiler_params=pltpu.CompilerParams(vmem_limit_bytes=24 * 2**20),
+        cost_estimate=pl.CostEstimate(
+            flops=6 * rows * up.size, bytes_accessed=4 * up.size, transcendentals=0
+        ),
+    )(me, features, source, prompts, gain, gate, in_hbm(up), in_hbm(down))
 
 
 def layer_norm(values, gain, shift):
@@ -84,6 +294,91 @@
     return (own + summed).astype(jnp.bfloat16)
 
 
+def fused_shards(
+    bits,
+    frames,
+    enc_gain,
+    enc_shift,
+    enc_up,
+    enc_up_bias,
+    enc_down,
+    enc_down_bias,
+    post_gain,
+    post_shift,
+    proj_weight,
+    proj_bias,
+    slot_source,
+    prompt_embeds,
+    rms_gain,
+    gate_weight,
+    up_weight,
+    down_weight,
+):
+    count = 1 << bits
+    index = lax.axis_index("tp")
+    me = index.reshape(1).astype(jnp.int32)
+    gathered = gather_slots(frames, bits)
+    prompts = gather_slots(prompt_embeds, bits)
+    send, total, base, gate = encoder(
+        me,
+        gathered,
+        enc_gain,
+        enc_shift,
+        enc_up_bias,
+        enc_down_bias,
+        enc_up,
+        enc_down,
+        gate_weight.T,
+        bits,
+    )
+    total = total + swap(send, 0, count).astype(jnp.float32)
+    for bit in range(1, bits):
+        total = total + swap(total.astype(jnp.bfloat16), bit, count).astype(jnp.float32)
+    post = layer_norm(total + base, post_gain, post_shift).astype(jnp.bfloat16)
+    other = swap(post, 0, count)
+    parity = index
+    for bit in range(1, bits):
+        parity = parity ^ (index >> bit)
+    upper = (parity & 1) == 1
+    post_every = jnp.where(
+        upper, jnp.concatenate([other, post]), jnp.concatenate([post, other])
+    )
+    projected = (
+        jnp.dot(post_every, proj_weight, preferred_element_type=jnp.float32) + proj_bias
+    ).astype(jnp.bfloat16)
+    features = gather_slots(projected[None], bits)
+    send, total = language(
+        me,
+        features,
+        slot_source,
+        prompts,
+        rms_gain,
+        gate,
+        up_weight.T,
+        down_weight,
+        bits,
+    )
+    total = total + swap(send, 0, count).astype(jnp.float32)
+    for bit in range(1, bits):
+        half = total.shape[0] // 2
+        arrived = swap(total[half:].astype(jnp.bfloat16), bit, count)
+        total = total[:half] + arrived.astype(jnp.float32)
+    return total.astype(jnp.bfloat16)
+
+
+def any_shards(*arrays):
+    count = lax.axis_size("tp")
+    bits = count.bit_length() - 1
+    whole_tiles = (
+        arrays[9].shape[1] % 128 == 0
+        and arrays[3].shape[0] % 16 == 0
+        and arrays[16].shape[0] % 16 == 0
+    )
+    if count == 1 << bits and bits > 1 and whole_tiles:
+        return fused_shards(bits, *arrays)
+    return shards(*arrays)
+
+
 def solution(mesh):
     placed = (
         P(("groups", "tp"), None),
@@ -105,5 +400,5 @@
         P("tp", None),
     )
     return jax.shard_map(
-        shards, mesh=mesh, in_specs=placed, out_specs=P(("groups", "tp"), None), check_vma=False
-    )
+        any_shards, mesh=mesh, in_specs=placed, out_specs=P(("groups", "tp"), None), check_vma=False
+    )

time: 111 us -> 86 us (0.77)
  waiting for transfers between devices: 52.4 us -> 32.2 us
  matrix products: 14.5 us -> 0.21 us
  Pallas kernels: 0 us -> 13.3 us
  blocking collectives: 9.73 us -> 0 us
  starting transfers between devices: 22.1 us -> 26.7 us
    all_to_all x5 -> x0, waiting for transfers between devices: 52.4 us -> none  [the longest x3 30.9 us: to_every(): return lax.all_to_all(spread, 'tp', 0, 0)]
    ppermute x0 -> x21, waiting for transfers between devices: none -> 32.2 us  [swap(): return lax.ppermute(value, 'tp', pairs)]
    ppermute x0 -> x21, starting transfers between devices: none -> 26.7 us  [swap(): return lax.ppermute(value, 'tp', pairs)]
    all_to_all x5 -> x0, starting transfers between devices: 22.1 us -> none  [the longest x3 15 us: to_every(): return lax.all_to_all(spread, 'tp', 0, 0)]
    dot_general x4 -> x1, matrix products: 14.5 us -> 0.21 us  [fused_shards(): jnp.dot(post_every, proj_weight, preferred_element_type=jnp.float32)]
    pallas_call x0 -> x2, Pallas kernels: none -> 13.3 us  [the longest x1 9.94 us: language(): pl.pallas_call(functools.partial(language_kernel, bits, pieces), out_shap...]
    all_to_all x1 -> x0, blocking collectives: 9.73 us -> none  [to_every(): return lax.all_to_all(spread, 'tp', 0, 0)]
    unnamed x18 -> x29, local copies, waits for them, and re-layouts: 0.04 us -> 7.83 us
  transfers between devices with their start and end apart: 5 -> 21, of which waited for: 5 -> 16; matrix products, arithmetic and copies ran while one was open for 2% -> 1% of each run, Pallas kernels for 0% -> 0%
where the time goes in v2:
time: 86 us; the launch traced here: 84.9 us
  waiting for transfers between devices  32.2 us (37%)
  starting transfers between devices  26.7 us (31%)
  Pallas kernels  13.3 us (15%)
  local copies, waits for them, and re-layouts  8.77 us (10%)
  other arithmetic  3.56 us (4%)
    ppermute x21, waiting for transfers between devices, swap(): return lax.ppermute(value, 'tp', pairs)  32.2 us
    ppermute x21, starting transfers between devices, swap(): return lax.ppermute(value, 'tp', pairs)  26.7 us
    pallas_call x1, Pallas kernels, language(): pl.pallas_call(functools.partial(language_kernel, bits, pieces), out_shap...  9.94 us
    unnamed x29, local copies, waits for them, and re-layouts  7.83 us
    pallas_call x1, Pallas kernels, encoder(): pl.pallas_call(functools.partial(encoder_kernel, bits), out_shape=[jax.Sh...  3.35 us
    concatenate x9, other arithmetic, gather_slots(): value = jnp.concatenate([value, swap(value, bit, 1 << bits)], axis=0)  2.34 us
  transfers between devices with their start and end apart: 21, of which 16 were waited for; matrix products, arithmetic and copies ran while one was open for 1% of the time, Pallas kernels for 0%

profile of v2, /device:TPU:0, one launch (start us, length us, event | category | flops | bytes accessed | tf_op | source)
XLA Modules:
  0.0 84.9 jit_solution(5906275313417880983)
XLA Ops:
  0.0 3.5 %collective-permute-start = (bf16[4,1280]{1,0:T(4,128)(2,1)}, bf16[4,1280]{1,0:T(4,128)(2,1)S(1)}, u32[]{:S(2)}, u32[]{:S(2)}) collective-permute-start(bf16[4,1280]{1,0:T(4,128)(2,1)} %param.17), channel_id=1, source_target_pairs={{0,9},{1,8},{2,11},{3,10},{4,13},{5,12},{6,15},{7,14},{8,1},{9,0},... | collective-permute-start | bytes 30728 | tf_op jit(solution)/shard_map/ppermute | solution.py:34
  3.6 1.6 %collective-permute-done = bf16[4,1280]{1,0:T(4,128)(2,1)S(1)} collective-permute-done((bf16[4,1280]{1,0:T(4,128)(2,1)}, bf16[4,1280]{1,0:T(4,128)(2,1)S(1)}, u32[]{:S(2)}, u32[]{:S(2)}) %collective-permute-start) | collective-permute-done | bytes 10272 | tf_op jit(solution)/shard_map/ppermute | solution.py:34
  5.2 0.7 pad_maximum_fusion.8
  5.9 1.9 %collective-permute-start.1 = (bf16[8,1280]{1,0:T(8,128)(2,1)S(1)}, bf16[8,1280]{1,0:T(8,128)(2,1)S(1)}, u32[]{:S(2)}, u32[]{:S(2)}) collective-permute-start(bf16[8,1280]{1,0:T(8,128)(2,1)S(1)} %pad_maximum_fusion.8), channel_id=1, source_target_pairs={{0,5},{1,4},{2,7},{3,6},{4,1},{5,0},{6,3},{7,2},{8,13},{9,12},{10,... | collective-permute-start | bytes 61448 | tf_op jit(solution)/shard_map/ppermute | solution.py:34
  7.8 1.5 %collective-permute-done.1 = bf16[8,1280]{1,0:T(8,128)(2,1)S(1)} collective-permute-done((bf16[8,1280]{1,0:T(8,128)(2,1)S(1)}, bf16[8,1280]{1,0:T(8,128)(2,1)S(1)}, u32[]{:S(2)}, u32[]{:S(2)}) %collective-permute-start.1) | collective-permute-done | bytes 20512 | tf_op jit(solution)/shard_map/ppermute | solution.py:34
  9.3 0.7 pad_maximum_fusion.6
  10.0 1.7 %collective-permute-start.2 = (bf16[16,1280]{1,0:T(8,128)(2,1)S(1)}, bf16[16,1280]{1,0:T(8,128)(2,1)S(1)}, u32[]{:S(2)}, u32[]{:S(2)}) collective-permute-start(bf16[16,1280]{1,0:T(8,128)(2,1)S(1)} %pad_maximum_fusion.6), channel_id=1, source_target_pairs={{0,3},{1,2},{2,1},{3,0},{4,7},{5,6},{6,5},{7,4},{8,11},{9,10},{10,... | collective-permute-start | bytes 122888 | tf_op jit(solution)/shard_map/ppermute | solution.py:34
  11.8 1.8 %collective-permute-done.2 = bf16[16,1280]{1,0:T(8,128)(2,1)S(1)} collective-permute-done((bf16[16,1280]{1,0:T(8,128)(2,1)S(1)}, bf16[16,1280]{1,0:T(8,128)(2,1)S(1)}, u32[]{:S(2)}, u32[]{:S(2)}) %collective-permute-start.2) | collective-permute-done | bytes 40992 | tf_op jit(solution)/shard_map/ppermute | solution.py:34
  13.5 0.7 pad_maximum_fusion.3
  14.3 0.6 collective-permute-start.3
  14.8 0.9 %collective-permute-done.3 = bf16[32,1280]{1,0:T(8,128)(2,1)S(1)} collective-permute-done((bf16[32,1280]{1,0:T(8,128)(2,1)S(1)}, bf16[32,1280]{1,0:T(8,128)(2,1)S(1)}, u32[]{:S(2)}, u32[]{:S(2)}) %collective-permute-start.3) | collective-permute-done | bytes 81952 | tf_op jit(solution)/shard_map/ppermute | solution.py:34
  15.7 0.7 concatenate.54.frames
  16.5 0.0 copy-start.4
  16.5 0.7 copy-done.4
  17.2 0.7 copy-done.5
  17.9 0.7 copy-done.6
  18.6 0.7 copy-done.7
  19.3 3.3 %shard_map.163 = (bf16[16,1280]{1,0:T(8,128)(2,1)S(1)}, f32[16,1280]{1,0:T(8,128)S(1)}, f32[16,1280]{1,0:T(8,128)S(1)}, bf16[688,4096]{1,0:T(8,128)(2,1)S(1)}) custom-call(s32[1]{0:T(128)} %bitcast.me_ref, bf16[64,1280]{1,0:T(8,128)(2,1)S(1)} %concatenate.54.frames, f32[1280]{0:T(1024)S(1)} %copy-done.4, f32[1280]{0:T(1024)S(1)} %copy-done.5, ...), custom_call_target="tpu_custom_call" | custom-call | flops 104857600 | bytes 7274496 | tf_op jit(solution)/shard_map/pallas_call | solution.py:103
  22.6 2.4 %copy-done.1 = bf16[688,4096]{1,0:T(8,128)(2,1)} copy-done((bf16[688,4096]{1,0:T(8,128)(2,1)}, bf16[688,4096]{1,0:T(8,128)(2,1)S(1)}, u32[]{:S(2)}) %copy-start.1) | copy-done | bytes 5636120
  25.1 0.4 collective-permute-start.4
  25.4 0.9 %collective-permute-done.4 = bf16[16,1280]{1,0:T(8,128)(2,1)S(1)} collective-permute-done((bf16[16,1280]{1,0:T(8,128)(2,1)S(1)}, bf16[16,1280]{1,0:T(8,128)(2,1)S(1)}, u32[]{:S(2)}, u32[]{:S(2)}) %collective-permute-start.4) | collective-permute-done | bytes 40992 | tf_op jit(solution)/shard_map/ppermute | solution.py:34
  26.3 1.8 %collective-permute-start.5 = (bf16[16,1280]{1,0:T(8,128)(2,1)S(1)}, bf16[16,1280]{1,0:T(8,128)(2,1)S(1)}, u32[]{:S(2)}, u32[]{:S(2)}) collective-permute-start(bf16[16,1280]{1,0:T(8,128)(2,1)S(1)} %fusion.9), channel_id=1, source_target_pairs={{0,3},{1,2},{2,1},{3,0},{4,7},{5,6},{6,5},{7,4},{8,11},{9,10},{10,... | collective-permute-start | bytes 122888 | tf_op jit(solution)/shard_map/ppermute | solution.py:34
  28.1 1.7 %collective-permute-done.5 = bf16[16,1280]{1,0:T(8,128)(2,1)S(1)} collective-permute-done((bf16[16,1280]{1,0:T(8,128)(2,1)S(1)}, bf16[16,1280]{1,0:T(8,128)(2,1)S(1)}, u32[]{:S(2)}, u32[]{:S(2)}) %collective-permute-start.5) | collective-permute-done | bytes 40992 | tf_op jit(solution)/shard_map/ppermute | solution.py:34
  29.8 1.9 %collective-permute-start.6 = (bf16[16,1280]{1,0:T(8,128)(2,1)S(1)}, bf16[16,1280]{1,0:T(8,128)(2,1)S(1)}, u32[]{:S(2)}, u32[]{:S(2)}) collective-permute-start(bf16[16,1280]{1,0:T(8,128)(2,1)S(1)} %fusion.12), channel_id=1, source_target_pairs={{0,5},{1,4},{2,7},{3,6},{4,1},{5,0},{6,3},{7,2},{8,13},{9,12},{10,... | collective-permute-start | bytes 122888 | tf_op jit(solution)/shard_map/ppermute | solution.py:34
  31.7 2.8 %collective-permute-start.13 = (bf16[4,4096]{1,0:T(4,128)(2,1)S(1)}, bf16[4,4096]{1,0:T(4,128)(2,1)S(1)}, u32[]{:S(2)}, u32[]{:S(2)}) collective-permute-start(bf16[4,4096]{1,0:T(4,128)(2,1)S(1)} %copy-done.9), channel_id=1, source_target_pairs={{0,9},{1,8},{2,11},{3,10},{4,13},{5,12},{6,15},{7,14},{8,1},{9,0},... | collective-permute-start | bytes 98312 | tf_op jit(solution)/shard_map/ppermute | solution.py:34
  34.5 0.0 collective-permute-done.6
  34.5 2.3 %collective-permute-start.7 = (bf16[16,1280]{1,0:T(8,128)(2,1)S(1)}, bf16[16,1280]{1,0:T(8,128)(2,1)S(1)}, u32[]{:S(2)}, u32[]{:S(2)}) collective-permute-start(bf16[16,1280]{1,0:T(8,128)(2,1)S(1)} %fusion.10), channel_id=1, source_target_pairs={{0,9},{1,8},{2,11},{3,10},{4,13},{5,12},{6,15},{7,14},{8,1},{9,0},... | collective-permute-start | bytes 122888 | tf_op jit(solution)/shard_map/ppermute | solution.py:34
  36.8 0.0 collective-permute-done.13
  36.9 1.4 %collective-permute-start.14 = (bf16[8,4096]{1,0:T(8,128)(2,1)S(1)}, bf16[8,4096]{1,0:T(8,128)(2,1)S(1)}, u32[]{:S(2)}, u32[]{:S(2)}) collective-permute-start(bf16[8,4096]{1,0:T(8,128)(2,1)S(1)} %pad_maximum_fusion.5), channel_id=1, source_target_pairs={{0,5},{1,4},{2,7},{3,6},{4,1},{5,0},{6,3},{7,2},{8,13},{9,12},{10,... | collective-permute-start | bytes 196616 | tf_op jit(solution)/shard_map/ppermute | solution.py:34
  38.2 1.7 %collective-permute-done.7 = bf16[16,1280]{1,0:T(8,128)(2,1)S(1)} collective-permute-done((bf16[16,1280]{1,0:T(8,128)(2,1)S(1)}, bf16[16,1280]{1,0:T(8,128)(2,1)S(1)}, u32[]{:S(2)}, u32[]{:S(2)}) %collective-permute-start.7) | collective-permute-done | bytes 40992 | tf_op jit(solution)/shard_map/ppermute | solution.py:34
  39.9 0.1 fusion.13
  40.0 0.2 multiply_reduce_fusion
  40.3 0.1 add_convert_fusion
  40.4 0.3 collective-permute-start.8
  40.6 1.0 %collective-permute-done.14 = bf16[8,4096]{1,0:T(8,128)(2,1)S(1)} collective-permute-done((bf16[8,4096]{1,0:T(8,128)(2,1)S(1)}, bf16[8,4096]{1,0:T(8,128)(2,1)S(1)}, u32[]{:S(2)}, u32[]{:S(2)}) %collective-permute-start.14) | collective-permute-done | bytes 65568 | tf_op jit(solution)/shard_map/ppermute | solution.py:34
  41.6 0.1 pad_maximum_fusion.2
  41.7 1.3 %collective-permute-start.15 = (bf16[16,4096]{1,0:T(8,128)(2,1)S(1)}, bf16[16,4096]{1,0:T(8,128)(2,1)S(1)}, u32[]{:S(2)}, u32[]{:S(2)}) collective-permute-start(bf16[16,4096]{1,0:T(8,128)(2,1)S(1)} %pad_maximum_fusion.2), channel_id=1, source_target_pairs={{0,3},{1,2},{2,1},{3,0},{4,7},{5,6},{6,5},{7,4},{8,11},{9,10},{10,... | collective-permute-start | bytes 393224 | tf_op jit(solution)/shard_map/ppermute | solution.py:34
  43.0 0.0 collective-permute-done.8
  43.0 0.2 constant_dynamic-update-slice_fusion.4
  43.2 1.3 %collective-permute-start.9 = (bf16[1,32,256]{2,1,0:T(8,128)(2,1)S(1)}, bf16[1,32,256]{2,1,0:T(8,128)(2,1)S(1)}, u32[]{:S(2)}, u32[]{:S(2)}) collective-permute-start(bf16[1,32,256]{2,1,0:T(8,128)(2,1)S(1)} %get-tuple-element.20), channel_id=1, source_target_pairs={{0,9},{1,8},{2,11},{3,10},{4,13},{5,12},{6,15},{7,14},{8,1},{9,0},... | collective-permute-start | bytes 49160 | tf_op jit(solution)/shard_map/ppermute | solution.py:34
  44.5 2.9 %collective-permute-done.9 = bf16[1,32,256]{2,1,0:T(8,128)(2,1)S(1)} collective-permute-done((bf16[1,32,256]{2,1,0:T(8,128)(2,1)S(1)}, bf16[1,32,256]{2,1,0:T(8,128)(2,1)S(1)}, u32[]{:S(2)}, u32[]{:S(2)}) %collective-permute-start.9) | collective-permute-done | bytes 16416 | tf_op jit(solution)/shard_map/ppermute | solution.py:34
  47.4 0.6 collective-permute-start.10
  48.0 0.0 collective-permute-done.15
  48.0 0.1 pad_maximum_fusion
  48.0 0.3 collective-permute-start.16
  48.3 2.4 %collective-permute-done.10 = bf16[2,32,256]{2,1,0:T(8,128)(2,1)S(1)} collective-permute-done((bf16[2,32,256]{2,1,0:T(8,128)(2,1)S(1)}, bf16[2,32,256]{2,1,0:T(8,128)(2,1)S(1)}, u32[]{:S(2)}, u32[]{:S(2)}) %collective-permute-start.10) | collective-permute-done | bytes 32800 | tf_op jit(solution)/shard_map/ppermute | solution.py:34
  50.7 0.8 collective-permute-start.11
  51.5 3.0 %collective-permute-done.11 = bf16[4,32,256]{2,1,0:T(8,128)(2,1)S(1)} collective-permute-done((bf16[4,32,256]{2,1,0:T(8,128)(2,1)S(1)}, bf16[4,32,256]{2,1,0:T(8,128)(2,1)S(1)}, u32[]{:S(2)}, u32[]{:S(2)}) %collective-permute-start.11) | collective-permute-done | bytes 65568 | tf_op jit(solution)/shard_map/ppermute | solution.py:34
  54.5 0.7 collective-permute-start.12
  55.2 0.0 collective-permute-done.16
  55.2 0.2 concatenate.64.prompts
  55.3 0.8 collective-permute-done.12
  56.2 2.6 %copy-done.2 = bf16[688,4096]{1,0:T(8,128)(2,1)S(1)} copy-done((bf16[688,4096]{1,0:T(8,128)(2,1)S(1)}, bf16[688,4096]{1,0:T(8,128)(2,1)}, u32[]{:S(2)}) %copy-start.2) | copy-done | bytes 5636120
  58.8 9.9 %shard_map.164 = (bf16[32,4096]{1,0:T(8,128)(2,1)S(1)}, f32[32,4096]{1,0:T(8,128)S(1)}) custom-call(s32[1]{0:T(128)} %bitcast.me_ref, bf16[16,32,256]{2,1,0:T(8,128)(2,1)S(1)} %constant_dynamic-update-slice_fusion.features, s32[64]{0:T(128)S(1)} %copy-done.8, bf16[64,4096]{1,0:T(8,128)(2,1)S(1)} %concatenate.64.prompts, f32[4096]{0:T(1024)S(1)} %copy-done.3, ...), custom_call_target="tpu_custom_call" | custom-call | flops 1082130432 | bytes 11272192 | tf_op jit(solution)/shard_map/pallas_call | solution.py:196
  68.7 0.4 collective-permute-start.17
  69.1 1.2 %collective-permute-done.17 = bf16[32,4096]{1,0:T(8,128)(2,1)S(1)} collective-permute-done((bf16[32,4096]{1,0:T(8,128)(2,1)S(1)}, bf16[32,4096]{1,0:T(8,128)(2,1)S(1)}, u32[]{:S(2)}, u32[]{:S(2)}) %collective-permute-start.17) | collective-permute-done | bytes 262176 | tf_op jit(solution)/shard_map/ppermute | solution.py:34
  70.3 0.1 convert_add_fusion
  70.4 0.5 collective-permute-start.18
  70.9 4.9 %collective-permute-done.18 = bf16[16,4096]{1,0:T(8,128)(2,1)S(1)} collective-permute-done((bf16[16,4096]{1,0:T(8,128)(2,1)S(1)}, bf16[16,4096]{1,0:T(8,128)(2,1)S(1)}, u32[]{:S(2)}, u32[]{:S(2)}) %collective-permute-start.18) | collective-permute-done | bytes 131104 | tf_op jit(solution)/shard_map/ppermute | solution.py:34
  75.9 0.8 collective-permute-start.19
  76.7 3.3 %collective-permute-done.19 = bf16[8,4096]{1,0:T(8,128)(2,1)S(1)} collective-permute-done((bf16[8,4096]{1,0:T(8,128)(2,1)S(1)}, bf16[8,4096]{1,0:T(8,128)(2,1)S(1)}, u32[]{:S(2)}, u32[]{:S(2)}) %collective-permute-start.19) | collective-permute-done | bytes 65568 | tf_op jit(solution)/shard_map/ppermute | solution.py:34
  80.0 1.5 %collective-permute-start.20 = (bf16[4,4096]{1,0:T(4,128)(2,1)S(1)}, bf16[4,4096]{1,0:T(4,128)(2,1)S(1)}, u32[]{:S(2)}, u32[]{:S(2)}) collective-permute-start(bf16[4,4096]{1,0:T(4,128)(2,1)S(1)} %slice.43), channel_id=1, source_target_pairs={{0,9},{1,8},{2,11},{3,10},{4,13},{5,12},{6,15},{7,14},{8,1},{9,0},... | collective-permute-start | bytes 98312 | tf_op jit(solution)/shard_map/ppermute | solution.py:34
  81.5 2.8 %collective-permute-done.20 = bf16[4,4096]{1,0:T(4,128)(2,1)S(1)} collective-permute-done((bf16[4,4096]{1,0:T(4,128)(2,1)S(1)}, bf16[4,4096]{1,0:T(4,128)(2,1)S(1)}, u32[]{:S(2)}, u32[]{:S(2)}) %collective-permute-start.20) | collective-permute-done | bytes 32800 | tf_op jit(solution)/shard_map/ppermute | solution.py:34
  84.3 0.6 fusion.8
  (37 shorter events, 0.3 us)
Async XLA Ops:
  0.0 43.0 %copy-start = (bf16[1280,256]{1,0:T(8,128)(2,1)S(1)}, bf16[1280,256]{1,0:T(8,128)(2,1)}, u32[]{:S(2)}) copy-start(bf16[1280,256]{1,0:T(8,128)(2,1)} %param.26) | copy-start | bytes 1966084
  0.0 31.7 %copy-start.9 = (bf16[4,4096]{1,0:T(4,128)(2,1)S(1)}, bf16[4,4096]{1,0:T(4,128)(2,1)}, u32[]{:S(2)}) copy-start(bf16[4,4096]{1,0:T(4,128)(2,1)} %param.29) | copy-start | bytes 98308
  0.0 40.2 %copy-start.10 = (f32[1280]{0:T(1024)S(1)}, f32[1280]{0:T(1024)}, u32[]{:S(2)}) copy-start(f32[1280]{0:T(1024)} %param.25) | copy-start | bytes 15364
  0.0 40.3 %copy-start.11 = (f32[1280]{0:T(1024)S(1)}, f32[1280]{0:T(1024)}, u32[]{:S(2)}) copy-start(f32[1280]{0:T(1024)} %param.24) | copy-start | bytes 15364
  0.0 43.0 %copy-start.12 = (f32[256]{0:T(256)S(1)}, f32[256]{0:T(256)}, u32[]{:S(2)}) copy-start(f32[256]{0:T(256)} %param.27) | copy-start | bytes 3076
  0.0 5.1 %collective-permute-start = (bf16[4,1280]{1,0:T(4,128)(2,1)}, bf16[4,1280]{1,0:T(4,128)(2,1)S(1)}, u32[]{:S(2)}, u32[]{:S(2)}) collective-permute-start(bf16[4,1280]{1,0:T(4,128)(2,1)} %param.17), channel_id=1, source_target_pairs={{0,9},{1,8},{2,11},{3,10},{4,13},{5,12},{6,15},{7,14},{8,1},{9,0},... | collective-permute-start | bytes 30728 | tf_op jit(solution)/shard_map/ppermute | solution.py:34
  5.9 3.4 %collective-permute-start.1 = (bf16[8,1280]{1,0:T(8,128)(2,1)S(1)}, bf16[8,1280]{1,0:T(8,128)(2,1)S(1)}, u32[]{:S(2)}, u32[]{:S(2)}) collective-permute-start(bf16[8,1280]{1,0:T(8,128)(2,1)S(1)} %pad_maximum_fusion.8), channel_id=1, source_target_pairs={{0,5},{1,4},{2,7},{3,6},{4,1},{5,0},{6,3},{7,2},{8,13},{9,12},{10,... | collective-permute-start | bytes 61448 | tf_op jit(solution)/shard_map/ppermute | solution.py:34
  10.0 3.5 %collective-permute-start.2 = (bf16[16,1280]{1,0:T(8,128)(2,1)S(1)}, bf16[16,1280]{1,0:T(8,128)(2,1)S(1)}, u32[]{:S(2)}, u32[]{:S(2)}) collective-permute-start(bf16[16,1280]{1,0:T(8,128)(2,1)S(1)} %pad_maximum_fusion.6), channel_id=1, source_target_pairs={{0,3},{1,2},{2,1},{3,0},{4,7},{5,6},{6,5},{7,4},{8,11},{9,10},{10,... | collective-permute-start | bytes 122888 | tf_op jit(solution)/shard_map/ppermute | solution.py:34
  14.3 1.5 %collective-permute-start.3 = (bf16[32,1280]{1,0:T(8,128)(2,1)S(1)}, bf16[32,1280]{1,0:T(8,128)(2,1)S(1)}, u32[]{:S(2)}, u32[]{:S(2)}) collective-permute-start(bf16[32,1280]{1,0:T(8,128)(2,1)S(1)} %pad_maximum_fusion.3), channel_id=1, source_target_pairs={{0,1},{1,0},{2,3},{3,2},{4,5},{5,4},{6,7},{7,6},{8,9},{9,8},{10,11... | collective-permute-start | bytes 245768 | tf_op jit(solution)/shard_map/ppermute | solution.py:34
  16.5 0.7 copy-start.4
  17.2 0.7 copy-start.5
  17.9 0.7 copy-start.6
  18.6 0.7 copy-start.7
  19.3 36.9 %copy-start.3 = (f32[4096]{0:T(1024)S(1)}, f32[4096]{0:T(1024)}, u32[]{:S(2)}) copy-start(f32[4096]{0:T(1024)} %gain.3) | copy-start | bytes 49156
  19.3 36.9 %copy-start.8 = (s32[64]{0:T(128)S(1)}, s32[64]{0:T(128)}, u32[]{:S(2)}) copy-start(s32[64]{0:T(128)} %source.1) | copy-start | bytes 772
  22.6 2.4 %copy-start.1 = (bf16[688,4096]{1,0:T(8,128)(2,1)}, bf16[688,4096]{1,0:T(8,128)(2,1)S(1)}, u32[]{:S(2)}) copy-start(bf16[688,4096]{1,0:T(8,128)(2,1)S(1)} %get-tuple-element.14.gate) | copy-start | bytes 16908292
  25.1 1.2 %collective-permute-start.4 = (bf16[16,1280]{1,0:T(8,128)(2,1)S(1)}, bf16[16,1280]{1,0:T(8,128)(2,1)S(1)}, u32[]{:S(2)}, u32[]{:S(2)}) collective-permute-start(bf16[16,1280]{1,0:T(8,128)(2,1)S(1)} %get-tuple-element.12), channel_id=1, source_target_pairs={{0,1},{1,0},{2,3},{3,2},{4,5},{5,4},{6,7},{7,6},{8,9},{9,8},{10,11... | collective-permute-start | bytes 122888 | tf_op jit(solution)/shard_map/ppermute | solution.py:34
  26.3 3.5 %collective-permute-start.5 = (bf16[16,1280]{1,0:T(8,128)(2,1)S(1)}, bf16[16,1280]{1,0:T(8,128)(2,1)S(1)}, u32[]{:S(2)}, u32[]{:S(2)}) collective-permute-start(bf16[16,1280]{1,0:T(8,128)(2,1)S(1)} %fusion.9), channel_id=1, source_target_pairs={{0,3},{1,2},{2,1},{3,0},{4,7},{5,6},{6,5},{7,4},{8,11},{9,10},{10,... | collective-permute-start | bytes 122888 | tf_op jit(solution)/shard_map/ppermute | solution.py:34
  29.8 4.7 %collective-permute-start.6 = (bf16[16,1280]{1,0:T(8,128)(2,1)S(1)}, bf16[16,1280]{1,0:T(8,128)(2,1)S(1)}, u32[]{:S(2)}, u32[]{:S(2)}) collective-permute-start(bf16[16,1280]{1,0:T(8,128)(2,1)S(1)} %fusion.12), channel_id=1, source_target_pairs={{0,5},{1,4},{2,7},{3,6},{4,1},{5,0},{6,3},{7,2},{8,13},{9,12},{10,... | collective-permute-start | bytes 122888 | tf_op jit(solution)/shard_map/ppermute | solution.py:34
  31.7 5.1 %collective-permute-start.13 = (bf16[4,4096]{1,0:T(4,128)(2,1)S(1)}, bf16[4,4096]{1,0:T(4,128)(2,1)S(1)}, u32[]{:S(2)}, u32[]{:S(2)}) collective-permute-start(bf16[4,4096]{1,0:T(4,128)(2,1)S(1)} %copy-done.9), channel_id=1, source_target_pairs={{0,9},{1,8},{2,11},{3,10},{4,13},{5,12},{6,15},{7,14},{8,1},{9,0},... | collective-permute-start | bytes 98312 | tf_op jit(solution)/shard_map/ppermute | solution.py:34
  34.5 5.4 %collective-permute-start.7 = (bf16[16,1280]{1,0:T(8,128)(2,1)S(1)}, bf16[16,1280]{1,0:T(8,128)(2,1)S(1)}, u32[]{:S(2)}, u32[]{:S(2)}) collective-permute-start(bf16[16,1280]{1,0:T(8,128)(2,1)S(1)} %fusion.10), channel_id=1, source_target_pairs={{0,9},{1,8},{2,11},{3,10},{4,13},{5,12},{6,15},{7,14},{8,1},{9,0},... | collective-permute-start | bytes 122888 | tf_op jit(solution)/shard_map/ppermute | solution.py:34
  36.9 4.8 %collective-permute-start.14 = (bf16[8,4096]{1,0:T(8,128)(2,1)S(1)}, bf16[8,4096]{1,0:T(8,128)(2,1)S(1)}, u32[]{:S(2)}, u32[]{:S(2)}) collective-permute-start(bf16[8,4096]{1,0:T(8,128)(2,1)S(1)} %pad_maximum_fusion.5), channel_id=1, source_target_pairs={{0,5},{1,4},{2,7},{3,6},{4,1},{5,0},{6,3},{7,2},{8,13},{9,12},{10,... | collective-permute-start | bytes 196616 | tf_op jit(solution)/shard_map/ppermute | solution.py:34
  40.4 2.6 %collective-permute-start.8 = (bf16[16,1280]{1,0:T(8,128)(2,1)S(1)}, bf16[16,1280]{1,0:T(8,128)(2,1)S(1)}, u32[]{:S(2)}, u32[]{:S(2)}) collective-permute-start(bf16[16,1280]{1,0:T(8,128)(2,1)S(1)} %add_convert_fusion), channel_id=1, source_target_pairs={{0,1},{1,0},{2,3},{3,2},{4,5},{5,4},{6,7},{7,6},{8,9},{9,8},{10,11... | collective-permute-start | bytes 122888 | tf_op jit(solution)/shard_map/ppermute | solution.py:34
  41.7 6.3 %collective-permute-start.15 = (bf16[16,4096]{1,0:T(8,128)(2,1)S(1)}, bf16[16,4096]{1,0:T(8,128)(2,1)S(1)}, u32[]{:S(2)}, u32[]{:S(2)}) collective-permute-start(bf16[16,4096]{1,0:T(8,128)(2,1)S(1)} %pad_maximum_fusion.2), channel_id=1, source_target_pairs={{0,3},{1,2},{2,1},{3,0},{4,7},{5,6},{6,5},{7,4},{8,11},{9,10},{10,... | collective-permute-start | bytes 393224 | tf_op jit(solution)/shard_map/ppermute | solution.py:34
  43.2 4.1 %collective-permute-start.9 = (bf16[1,32,256]{2,1,0:T(8,128)(2,1)S(1)}, bf16[1,32,256]{2,1,0:T(8,128)(2,1)S(1)}, u32[]{:S(2)}, u32[]{:S(2)}) collective-permute-start(bf16[1,32,256]{2,1,0:T(8,128)(2,1)S(1)} %get-tuple-element.20), channel_id=1, source_target_pairs={{0,9},{1,8},{2,11},{3,10},{4,13},{5,12},{6,15},{7,14},{8,1},{9,0},... | collective-permute-start | bytes 49160 | tf_op jit(solution)/shard_map/ppermute | solution.py:34
  47.4 3.3 %collective-permute-start.10 = (bf16[2,32,256]{2,1,0:T(8,128)(2,1)S(1)}, bf16[2,32,256]{2,1,0:T(8,128)(2,1)S(1)}, u32[]{:S(2)}, u32[]{:S(2)}) collective-permute-start(bf16[2,32,256]{2,1,0:T(8,128)(2,1)S(1)} %pad_maximum_fusion.7), channel_id=1, source_target_pairs={{0,5},{1,4},{2,7},{3,6},{4,1},{5,0},{6,3},{7,2},{8,13},{9,12},{10,... | collective-permute-start | bytes 98312 | tf_op jit(solution)/shard_map/ppermute | solution.py:34
  48.0 7.1 %collective-permute-start.16 = (bf16[32,4096]{1,0:T(8,128)(2,1)S(1)}, bf16[32,4096]{1,0:T(8,128)(2,1)S(1)}, u32[]{:S(2)}, u32[]{:S(2)}) collective-permute-start(bf16[32,4096]{1,0:T(8,128)(2,1)S(1)} %pad_maximum_fusion), channel_id=1, source_target_pairs={{0,1},{1,0},{2,3},{3,2},{4,5},{5,4},{6,7},{7,6},{8,9},{9,8},{10,11... | collective-permute-start | bytes 786440 | tf_op jit(solution)/shard_map/ppermute | solution.py:34
  50.7 3.8 %collective-permute-start.11 = (bf16[4,32,256]{2,1,0:T(8,128)(2,1)S(1)}, bf16[4,32,256]{2,1,0:T(8,128)(2,1)S(1)}, u32[]{:S(2)}, u32[]{:S(2)}) collective-permute-start(bf16[4,32,256]{2,1,0:T(8,128)(2,1)S(1)} %pad_maximum_fusion.4), channel_id=1, source_target_pairs={{0,3},{1,2},{2,1},{3,0},{4,7},{5,6},{6,5},{7,4},{8,11},{9,10},{10,... | collective-permute-start | bytes 196616 | tf_op jit(solution)/shard_map/ppermute | solution.py:34
  54.5 1.6 %collective-permute-start.12 = (bf16[8,32,256]{2,1,0:T(8,128)(2,1)S(1)}, bf16[8,32,256]{2,1,0:T(8,128)(2,1)S(1)}, u32[]{:S(2)}, u32[]{:S(2)}) collective-permute-start(bf16[8,32,256]{2,1,0:T(8,128)(2,1)S(1)} %pad_maximum_fusion.1), channel_id=1, source_target_pairs={{0,1},{1,0},{2,3},{3,2},{4,5},{5,4},{6,7},{7,6},{8,9},{9,8},{10,11... | collective-permute-start | bytes 393224 | tf_op jit(solution)/shard_map/ppermute | solution.py:34
  56.2 2.6 %copy-start.2 = (bf16[688,4096]{1,0:T(8,128)(2,1)S(1)}, bf16[688,4096]{1,0:T(8,128)(2,1)}, u32[]{:S(2)}) copy-start(bf16[688,4096]{1,0:T(8,128)(2,1)} %copy-done.1) | copy-start | bytes 16908292
  68.7 1.6 %collective-permute-start.17 = (bf16[32,4096]{1,0:T(8,128)(2,1)S(1)}, bf16[32,4096]{1,0:T(8,128)(2,1)S(1)}, u32[]{:S(2)}, u32[]{:S(2)}) collective-permute-start(bf16[32,4096]{1,0:T(8,128)(2,1)S(1)} %get-tuple-element.16), channel_id=1, source_target_pairs={{0,1},{1,0},{2,3},{3,2},{4,5},{5,4},{6,7},{7,6},{8,9},{9,8},{10,11... | collective-permute-start | bytes 786440 | tf_op jit(solution)/shard_map/ppermute | solution.py:34
  70.4 5.4 %collective-permute-start.18 = (bf16[16,4096]{1,0:T(8,128)(2,1)S(1)}, bf16[16,4096]{1,0:T(8,128)(2,1)S(1)}, u32[]{:S(2)}, u32[]{:S(2)}) collective-permute-start(bf16[16,4096]{1,0:T(8,128)(2,1)S(1)} %slice.41), channel_id=1, source_target_pairs={{0,3},{1,2},{2,1},{3,0},{4,7},{5,6},{6,5},{7,4},{8,11},{9,10},{10,... | collective-permute-start | bytes 393224 | tf_op jit(solution)/shard_map/ppermute | solution.py:34
  75.9 4.1 %collective-permute-start.19 = (bf16[8,4096]{1,0:T(8,128)(2,1)S(1)}, bf16[8,4096]{1,0:T(8,128)(2,1)S(1)}, u32[]{:S(2)}, u32[]{:S(2)}) collective-permute-start(bf16[8,4096]{1,0:T(8,128)(2,1)S(1)} %slice.42), channel_id=1, source_target_pairs={{0,5},{1,4},{2,7},{3,6},{4,1},{5,0},{6,3},{7,2},{8,13},{9,12},{10,... | collective-permute-start | bytes 196616 | tf_op jit(solution)/shard_map/ppermute | solution.py:34
  80.0 4.3 %collective-permute-start.20 = (bf16[4,4096]{1,0:T(4,128)(2,1)S(1)}, bf16[4,4096]{1,0:T(4,128)(2,1)S(1)}, u32[]{:S(2)}, u32[]{:S(2)}) collective-permute-start(bf16[4,4096]{1,0:T(4,128)(2,1)S(1)} %slice.43), channel_id=1, source_target_pairs={{0,9},{1,8},{2,11},{3,10},{4,13},{5,12},{6,15},{7,14},{8,1},{9,0},... | collective-permute-start | bytes 98312 | tf_op jit(solution)/shard_map/ppermute | solution.py:34

commit v3 on v2

v3 whole, which is shorter than its diff:
```python
import functools

import jax
import jax.numpy as jnp
from jax import lax
from jax.experimental import pallas as pl
from jax.experimental.pallas import tpu as pltpu
from jax.sharding import PartitionSpec as P


def mask_of(bit):
    return (1 << bit) | 1 if bit else 1


def slot_of(offset, bits):
    parity = offset & 1
    slot = 0
    for bit in range(1, bits):
        one = (offset >> bit) & 1
        parity = parity ^ one
        slot = slot + (one << (bits - 1 - bit))
    return slot + (parity << (bits - 1))


def offset_of(slot, bits):
    offset = (slot >> (bits - 1)) & 1
    for bit in range(1, bits):
        offset = offset ^ (((slot >> (bits - 1 - bit)) & 1) * mask_of(bit))
    return offset


def swap(value, bit, count):
    pairs = [(i, i ^ mask_of(bit)) for i in range(count)]
    return lax.ppermute(value, "tp", pairs)


def parity_of(index, bits):
    parity = index
    for bit in range(1, bits):
        parity = parity ^ (index >> bit)
    return parity & 1


def in_hbm(value):
    return pltpu.with_memory_space_constraint(value, pltpu.HBM)


def row(ref, part=slice(None)):
    return ref[part].reshape(1, -1)


def dot_last(left, right):
    return lax.dot_general(
        left, right, (((1,), (1,)), ((), ())), preferred_element_type=jnp.float32
    )


def encoder_kernel(
    bits, frames, others, gain, shift, down_bias, bias, up, down, send, keep, base
):
    me = lax.axis_index("tp")
    first = frames.shape[0]
    rows = 2 * first
    pooled = rows // 2
    half = pooled // 2
    own = rows >> bits
    out_row = lax.broadcasted_iota(jnp.int32, (rows, rows), 0)
    in_row = lax.broadcasted_iota(jnp.int32, (rows, rows), 1)
    frame = jnp.where(out_row < pooled, 2 * out_row, 2 * (out_row - pooled) + 1)
    place = slot_of((frame // own) ^ me, bits) * own + frame % own
    order = jnp.where(place == in_row, 1.0, 0.0).astype(jnp.bfloat16)
    values = jnp.dot(
        order, jnp.concatenate([frames[...], others[...]]), preferred_element_type=jnp.float32
    )
    center = values - jnp.mean(values, axis=-1, keepdims=True)
    spread = jnp.mean(center * center, axis=-1, keepdims=True)
    both = (values[:pooled] + values[pooled:]) * 0.5 + row(down_bias)
    normed = (center * lax.rsqrt(spread + 1e-05) * row(gain) + row(shift)).astype(jnp.bfloat16)
    pre_act = dot_last(normed, up[...]) + row(bias).astype(jnp.float32)
    hidden = (0.5 * pre_act * (1.0 + lax.erf(pre_act * 0.7071067811865476))).astype(jnp.bfloat16)
    result = jnp.dot(hidden, down[...], preferred_element_type=jnp.float32)
    mine = (result[:pooled] + result[pooled:]) * 0.5
    upper = parity_of(me, bits) == 1
    keep[...] = jnp.where(upper, mine[half:], mine[:half])
    send[...] = jnp.where(upper, mine[:half], mine[half:]).astype(jnp.bfloat16)
    base[...] = jnp.where(upper, both[half:], both[:half])


def encoder(halves, vectors, up, down, bits):
    first, width = halves[0].shape
    half = first // 2
    vmem = pl.BlockSpec(memory_space=pltpu.VMEM)
    return pl.pallas_call(
        functools.partial(encoder_kernel, bits),
        out_shape=[
            jax.ShapeDtypeStruct((half, width), jnp.bfloat16),
            jax.ShapeDtypeStruct((half, width), jnp.float32),
            jax.ShapeDtypeStruct((half, width), jnp.float32),
        ],
        in_specs=[vmem] * 8,
        out_specs=[vmem] * 3,
        compiler_params=pltpu.CompilerParams(vmem_limit_bytes=8 * 2**20),
        cost_estimate=pl.CostEstimate(
            flops=8 * first * up.size, bytes_accessed=4 * up.size, transcendentals=0
        ),
    )(*halves, *vectors, up, down)


def post_kernel(total, arrived, base, gain, shift, after, post):
    values = total[...] + arrived[...].astype(jnp.float32) + base[...]
    center = values - jnp.mean(values, axis=-1, keepdims=True)
    spread = jnp.mean(center * center, axis=-1, keepdims=True)
    normed = center * lax.rsqrt(spread + 1e-05) * row(gain) + row(shift)
    post[...] = normed.astype(post.dtype)


def post_norm(total, arrived, base, gain, shift, after):
    vmem = pl.BlockSpec(memory_space=pltpu.VMEM)
    return pl.pallas_call(
        post_kernel,
        out_shape=jax.ShapeDtypeStruct(total.shape, jnp.bfloat16),
        in_specs=[vmem] * 5 + [pl.BlockSpec(memory_space=pl.ANY)],
        out_specs=vmem,
        compiler_params=pltpu.CompilerParams(vmem_limit_bytes=4 * 2**20),
    )(total, arrived, base, gain, shift, after)


def project_kernel(bits, post, other, weight, bias, out):
    upper = parity_of(lax.axis_index("tp"), bits) == 1
    low = jnp.where(upper, other[...], post[...])
    high = jnp.where(upper, post[...], other[...])
    every = jnp.concatenate([low, high])
    result = jnp.dot(every, weight[...], preferred_element_type=jnp.float32) + row(bias)
    out[0] = result.astype(out.dtype)


def project(post, other, weight, bias, bits):
    vmem = pl.BlockSpec(memory_space=pltpu.VMEM)
    return pl.pallas_call(
        functools.partial(project_kernel, bits),
        out_shape=jax.ShapeDtypeStruct((1, 2 * post.shape[0], weight.shape[1]), jnp.bfloat16),
        in_specs=[vmem] * 4,
        out_specs=vmem,
        compiler_params=pltpu.CompilerParams(vmem_limit_bytes=4 * 2**20),
    )(post, other, weight, bias)


def stage_kernel(count, *refs):
    sems = refs[2 * count]
    copies = [
        pltpu.make_async_copy(refs[i], refs[count + i], sems.at[i]) for i in range(count)
    ]
    for copy in copies:
        copy.start()
    for copy in copies:
        copy.wait()


def stage(*values):
    count = len(values)
    return pl.pallas_call(
        functools.partial(stage_kernel, count),
        out_shape=[pltpu.VMEM(value.shape, value.dtype) for value in values],
        in_specs=[pl.BlockSpec(memory_space=pltpu.HBM)] * count,
        out_specs=[pl.BlockSpec(memory_space=pltpu.VMEM)] * count,
        scratch_shapes=[pltpu.SemaphoreType.DMA((count,))],
        compiler_params=pltpu.CompilerParams(vmem_limit_bytes=2 * 2**20),
    )(*[in_hbm(value) for value in values])


def fetch_kernel(start, carried, after, source, target, passed, sem):
    width = target.shape[1]
    copy = pltpu.make_async_copy(source.at[:, pl.ds(start, width)], target, sem)
    copy.start()
    passed[...] = carried[...]
    copy.wait()


def fetch(carried, after, weight, start, width):
    vmem = pl.BlockSpec(memory_space=pltpu.VMEM)
    return pl.pallas_call(
        functools.partial(fetch_kernel, start),
        out_shape=[
            pltpu.VMEM((weight.shape[0], width), weight.dtype),
            jax.ShapeDtypeStruct(carried.shape, carried.dtype),
        ],
        in_specs=[
            vmem,
            pl.BlockSpec(memory_space=pl.ANY),
            pl.BlockSpec(memory_space=pltpu.HBM),
        ],
        out_specs=[vmem] * 2,
        scratch_shapes=[pltpu.SemaphoreType.DMA],
        compiler_params=pltpu.CompilerParams(vmem_limit_bytes=2 * 2**20),
        cost_estimate=pl.CostEstimate(
            flops=0, bytes_accessed=2 * weight.shape[0] * width, transcendentals=0
        ),
    )(carried, after, in_hbm(weight))


def language_kernel(
    bits, near, far, source, prompts, others, gain, gate, rest, up, down,
    send, keep, packed, normed,
):
    count, audio, columns = near.shape
    count = 2 * count
    half, width = prompts.shape
    rows = 2 * half
    own = rows >> bits
    me = lax.axis_index("tp")
    out_row = lax.broadcasted_iota(jnp.int32, (rows, rows), 0)
    in_row = lax.broadcasted_iota(jnp.int32, (rows, rows), 1)
    place = (offset_of(out_row // own, bits) ^ me) * own + out_row % own
    order = jnp.where(place == in_row, 1.0, 0.0).astype(jnp.bfloat16)
    wanted = lax.broadcasted_iota(jnp.int32, (audio, rows), 0)
    chosen = jnp.where(row(source) == wanted, 1.0, 0.0).astype(jnp.bfloat16)
    pick = dot_last(order, chosen)
    audio_row = jnp.sum(pick, axis=1, keepdims=True) > 0.5
    pick = pick.astype(jnp.bfloat16)
    squares = jnp.zeros((rows, columns), jnp.float32)
    for device in range(count):
        part = slice(device * columns, (device + 1) * columns)
        slot = slot_of(me ^ device, bits)
        place = slot & (count // 2 - 1)
        piece = jnp.where(slot < count // 2, near[place], far[place])
        found = jnp.dot(pick, piece, preferred_element_type=jnp.float32)
        prompt = jnp.concatenate([prompts[:, part], others[:, part]])
        value = jnp.where(audio_row, found, prompt.astype(jnp.float32))
        squares += value * value
        packed[:, part] = value.astype(jnp.bfloat16)
    scale = lax.rsqrt(jnp.sum(squares, axis=1, keepdims=True) / width + 1e-06)
    for device in range(count):
        part = slice(device * columns, (device + 1) * columns)
        value = packed[:, part].astype(jnp.float32) * scale * row(gain, part)
        normed[:, part] = value.astype(jnp.bfloat16)
    cut = width // 2
    gated = dot_last(normed[:, :cut], gate[...]) + dot_last(normed[:, cut:], rest[...])
    lifted = dot_last(normed[...], up[...])
    hidden = (gated * jax.nn.sigmoid(gated) * lifted).astype(jnp.bfloat16)
    held = lax.broadcasted_iota(jnp.int32, (half, 1), 0) < own
    pieces = 4
    for piece in range(pieces):
        part = slice(piece * width // pieces, (piece + 1) * width // pieces)
        result = jnp.dot(hidden, down[:, part], preferred_element_type=jnp.float32)
        send[:, part] = result[half:].astype(jnp.bfloat16)
        keep[:, part] = result[:half] + jnp.where(
            held, packed[:half, part].astype(jnp.float32), 0.0
        )


def language(features, source, prompts, gain, gate, rest, up, down, bits):
    half, width = prompts[0].shape
    vmem = pl.BlockSpec(memory_space=pltpu.VMEM)
    return pl.pallas_call(
        functools.partial(language_kernel, bits),
        out_shape=[
            jax.ShapeDtypeStruct((half, width), jnp.bfloat16),
            jax.ShapeDtypeStruct((half, width), jnp.float32),
        ],
        in_specs=[vmem] * 10,
        out_specs=[vmem] * 2,
        scratch_shapes=[pltpu.VMEM((2 * half, width), jnp.bfloat16)] * 2,
        compiler_params=pltpu.CompilerParams(vmem_limit_bytes=12 * 2**20),
        cost_estimate=pl.CostEstimate(
            flops=12 * half * up.size, bytes_accessed=4 * up.size, transcendentals=0
        ),
    )(*features, source, *prompts, gain, gate, rest, up, down)


def layer_norm(values, gain, shift):
    center = values - jnp.mean(values, axis=-1, keepdims=True)
    spread = jnp.mean(center * center, axis=-1, keepdims=True)
    return center * lax.rsqrt(spread + 1e-05) * gain + shift


def to_every(piece, count):
    spread = jnp.broadcast_to(piece[None], (count,) + piece.shape)
    return lax.all_to_all(spread, "tp", 0, 0)


def reduce_rows(partial_value, count):
    rows, width = partial_value.shape
    pieces = partial_value.astype(jnp.bfloat16).reshape(count, rows // count, width)
    return jnp.sum(lax.all_to_all(pieces, "tp", 0, 0).astype(jnp.float32), axis=0)


def pool(values):
    paired = values.reshape(values.shape[0] // 2, 2, values.shape[1])
    return (paired[:, 0, :] + paired[:, 1, :]) * 0.5


def shards(
    frames,
    enc_gain,
    enc_shift,
    enc_up,
    enc_up_bias,
    enc_down,
    enc_down_bias,
    post_gain,
    post_shift,
    proj_weight,
    proj_bias,
    slot_source,
    prompt_embeds,
    rms_gain,
    gate_weight,
    up_weight,
    down_weight,
):
    count = lax.axis_size("tp")
    me = lax.axis_index("tp")
    gathered = to_every(frames, count).reshape(-1, frames.shape[1])
    prompts = to_every(prompt_embeds, count).reshape(-1, prompt_embeds.shape[1])
    normed = layer_norm(gathered.astype(jnp.float32), enc_gain, enc_shift).astype(jnp.bfloat16)
    pre_act = lax.dot_general(
        normed, enc_up, (((1,), (1,)), ((), ())), preferred_element_type=jnp.float32
    )
    hidden = jax.nn.gelu(pre_act + enc_up_bias.astype(jnp.float32), approximate=False)
    partial_value = jnp.dot(
        hidden.astype(jnp.bfloat16), enc_down, preferred_element_type=jnp.float32
    )
    branch = reduce_rows(pool(partial_value), count)
    pooled = pool(frames.astype(jnp.float32)) + branch + enc_down_bias
    post = layer_norm(pooled, post_gain, post_shift).astype(jnp.bfloat16)
    post_every = to_every(post, count).reshape(-1, post.shape[1])
    projected = (
        jnp.dot(post_every, proj_weight, preferred_element_type=jnp.float32) + proj_bias
    ).astype(jnp.bfloat16)
    features = to_every(projected, count)
    features = jnp.transpose(features, (1, 0, 2)).reshape(projected.shape[0], -1)
    clipped = jnp.maximum(slot_source, 0)
    packed = jnp.where(
        (slot_source >= 0)[:, None], jnp.take(features, clipped, axis=0), prompts
    )
    residual = packed.astype(jnp.float32)
    scale = lax.rsqrt(jnp.mean(residual * residual, axis=-1, keepdims=True) + 1e-06)
    lm_normed = (residual * scale * rms_gain).astype(jnp.bfloat16)
    gate = jnp.dot(lm_normed, gate_weight, preferred_element_type=jnp.float32)
    lifted = jnp.dot(lm_normed, up_weight, preferred_element_type=jnp.float32)
    lm_hidden = (jax.nn.silu(gate) * lifted).astype(jnp.bfloat16)
    summed = reduce_rows(
        jnp.dot(lm_hidden, down_weight, preferred_element_type=jnp.float32), count
    )
    row_count = prompt_embeds.shape[0]
    own = lax.dynamic_slice_in_dim(packed, me * row_count, row_count).astype(jnp.float32)
    return (own + summed).astype(jnp.bfloat16)


def fused_shards(
    bits,
    frames,
    enc_gain,
    enc_shift,
    enc_up,
    enc_up_bias,
    enc_down,
    enc_down_bias,
    post_gain,
    post_shift,
    proj_weight,
    proj_bias,
    slot_source,
    prompt_embeds,
    rms_gain,
    gate_weight,
    up_weight,
    down_weight,
):
    count = 1 << bits
    width = prompt_embeds.shape[1]
    steps = range(bits - 1, 0, -1)
    gate_rows, up_rows = gate_weight.T, up_weight.T
    arrived = swap(frames, bits - 1, count)
    (
        block, prompts, enc_gain, enc_shift, enc_down_bias, enc_up_bias, enc_up, enc_down,
        post_gain, post_shift, proj_weight, proj_bias, rms_gain, slot_source,
    ) = stage(
        frames, prompt_embeds, enc_gain, enc_shift, enc_down_bias, enc_up_bias, enc_up, enc_down,
        post_gain, post_shift, proj_weight, proj_bias, rms_gain, slot_source,
    )
    gate = []
    block = jnp.concatenate([block, arrived])
    for step, bit in enumerate(steps[1:]):
        arrived = swap(block, bit, count)
        if step < 2:
            piece, block = fetch(block, block, gate_rows, step * width // 2, width // 2)
            gate.append(piece)
        block = jnp.concatenate([block, arrived])
    send, total, base = encoder(
        (block, swap(block, 0, count)),
        (enc_gain, enc_shift, enc_down_bias, enc_up_bias),
        enc_up,
        enc_down,
        bits,
    )
    arrived = swap(send, 0, count)
    for step, bit in enumerate(range(1, bits)):
        total = total + arrived.astype(jnp.float32)
        arrived = swap(total.astype(jnp.bfloat16), bit, count)
        if step < 2:
            prompts = jnp.concatenate([prompts, swap(prompts, steps[step], count)])
    post = post_norm(total, arrived, base, post_gain, post_shift, prompts)
    features = project(post, swap(post, 0, count), proj_weight, proj_bias, bits)
    for bit in steps[2:]:
        prompts = jnp.concatenate([prompts, swap(prompts, bit, count)])
    for step, bit in enumerate(steps):
        arrived = swap(features, bit, count)
        if step == 0:
            up, features = fetch(features, features, up_rows, 0, width)
        if step == 2:
            down, features = fetch(features, prompts, down_weight, 0, width)
        features = jnp.concatenate([features, arrived])
    features = features, swap(features, 0, count)
    prompts = prompts, swap(prompts, 0, count)
    send, total = language(features, slot_source, prompts, rms_gain, *gate, up, down, bits)
    total = total + swap(send, 0, count).astype(jnp.float32)
    for bit in range(1, bits):
        half = total.shape[0] // 2
        arrived = swap(total[half:].astype(jnp.bfloat16), bit, count)
        total = total[:half] + arrived.astype(jnp.float32)
    return total.astype(jnp.bfloat16)


def any_shards(*arrays):
    count = lax.axis_size("tp")
    bits = count.bit_length() - 1
    whole_tiles = (
        arrays[9].shape[1] % 128 == 0
        and arrays[3].shape[0] % 16 == 0
        and arrays[16].shape[0] % 16 == 0
    )
    if count == 1 << bits and bits > 3 and whole_tiles:
        return fused_shards(bits, *arrays)
    return shards(*arrays)


def solution(mesh):
    placed = (
        P(("groups", "tp"), None),
        P(),
        P(),
        P("tp", None),
        P("tp"),
        P("tp", None),
        P(),
        P(),
        P(),
        P(None, "tp"),
        P("tp"),
        P("groups"),
        P(("groups", "tp"), None),
        P(),
        P(None, "tp"),
        P(None, "tp"),
        P("tp", None),
    )
    return jax.shard_map(
        any_shards, mesh=mesh, in_specs=placed, out_specs=P(("groups", "tp"), None), check_vma=False
    )
```

time: 86 us -> 68.8 us (0.80)
  waiting for transfers between devices: 32.2 us -> 21.2 us
  local copies, waits for them, and re-layouts: 8.77 us -> 0.08 us
  Pallas kernels: 13.3 us -> 17.4 us
  other arithmetic: 3.56 us -> 0.95 us
  starting transfers between devices: 26.7 us -> 28.8 us
    ppermute x21, waiting for transfers between devices: 32.2 us -> 21.2 us  [swap(): return lax.ppermute(value, 'tp', pairs)]
    unnamed x29 -> x5, local copies, waits for them, and re-layouts: 7.83 us -> 0.02 us
    pallas_call x1 -> x8, Pallas kernels: 9.94 us -> 16.2 us  [the longest x4 8.82 us: fetch(): pl.pallas_call(functools.partial(fetch_kernel, start), out_shape=[pltpu.V...]
    concatenate x9 -> x5, other arithmetic: 2.34 us -> 0.17 us  [the longest x2 0.09 us: fused_shards(): prompts = jnp.concatenate([prompts, swap(prompts, steps[step], count)])]
    pallas_call x1, Pallas kernels: 3.35 us -> 1.2 us  [encoder(): pl.pallas_call(functools.partial(encoder_kernel, bits), out_shape=[jax.Sh...]
    ppermute x21, starting transfers between devices: 26.7 us -> 28.8 us  [swap(): return lax.ppermute(value, 'tp', pairs)]
    concatenate x3 -> x4, local copies, waits for them, and re-layouts: 0.9 us -> 0.02 us  [the longest x2 0.01 us: fused_shards(): features = jnp.concatenate([features, arrived])]
  transfers between devices with their start and end apart: 21 -> 21, of which waited for: 16 -> 14; matrix products, arithmetic and copies ran while one was open for 1% -> 0% of each run, Pallas kernels for 0% -> 16%
where the time goes in v3:
time: 68.8 us; the launch traced here: 68.5 us
  starting transfers between devices  28.8 us (42%)
  waiting for transfers between devices  21.2 us (31%)
  Pallas kernels  17.4 us (25%)
  other arithmetic  0.95 us (1%)
    ppermute x21, starting transfers between devices, swap(): return lax.ppermute(value, 'tp', pairs)  28.8 us
    ppermute x21, waiting for transfers between devices, swap(): return lax.ppermute(value, 'tp', pairs)  21.2 us
    pallas_call x4, Pallas kernels, fetch(): pl.pallas_call(functools.partial(fetch_kernel, start), out_shape=[pltpu.V...  8.82 us
    pallas_call x1, Pallas kernels, language(): pl.pallas_call(functools.partial(language_kernel, bits), out_shape=[jax.S...  5.08 us
    pallas_call x1, Pallas kernels, stage(): pl.pallas_call(functools.partial(stage_kernel, count), out_shape=[pltpu.V...  1.82 us
  transfers between devices with their start and end apart: 21, of which 14 were waited for; matrix products, arithmetic and copies ran while one was open for 0% of the time, Pallas kernels for 16%

profile of v3, /device:TPU:0, one launch (start us, length us, event | category | flops | bytes accessed | tf_op | source)
XLA Modules:
  0.0 68.5 jit_solution(1999252418873608083)
XLA Ops:
  0.0 3.5 %collective-permute-start = (bf16[4,1280]{1,0:T(4,128)(2,1)}, bf16[4,1280]{1,0:T(4,128)(2,1)S(1)}, u32[]{:S(2)}, u32[]{:S(2)}) collective-permute-start(bf16[4,1280]{1,0:T(4,128)(2,1)} %refs_0_.1), channel_id=1, source_target_pairs={{0,9},{1,8},{2,11},{3,10},{4,13},{5,12},{6,15},{7,14},{8,1},{9,0},... | collective-permute-start | bytes 30728 | tf_op jit(solution)/shard_map/ppermute | solution.py:34
  3.5 1.8 %shard_map.163 = (bf16[4,1280]{1,0:T(4,128)(2,1)S(1)}, bf16[4,4096]{1,0:T(4,128)(2,1)S(1)}, f32[1280]{0:T(1024)S(1)}, f32[1280]{0:T(1024)S(1)}, f32[1280]{0:T(10...) custom-call(bf16[4,1280]{1,0:T(4,128)(2,1)} %refs_0_.1, ...), custom_call_target="tpu_custom_call" | custom-call | tf_op jit(solution)/shard_map/pallas_call | solution.py:161
  5.3 0.0 collective-permute-done
  5.3 1.9 %collective-permute-start.1 = (bf16[8,1280]{1,0:T(8,128)(2,1)S(1)}, bf16[8,1280]{1,0:T(8,128)(2,1)S(1)}, u32[]{:S(2)}, u32[]{:S(2)}) collective-permute-start(bf16[8,1280]{1,0:T(8,128)(2,1)S(1)} %pad_maximum_fusion.4.carried.after), channel_id=1, source_target_pairs={{0,5},{1,4},{2,7},{3,6},{4,1},{5,0},{6,3},{7,2},{8,13},{9,12},{10,... | collective-permute-start | bytes 61448 | tf_op jit(solution)/shard_map/ppermute | solution.py:34
  7.3 1.8 %shard_map.164 = (bf16[688,2048]{1,0:T(8,128)(2,1)S(1)}, bf16[8,1280]{1,0:T(8,128)(2,1)S(1)}) custom-call(bf16[8,1280]{1,0:T(8,128)(2,1)S(1)} %pad_maximum_fusion.4.carried.after, bf16[8,1280]{1,0:T(8,128)(2,1)S(1)} %pad_maximum_fusion.4.carried.after, bf16[688,4096]{1,0:T(8,128)(2,1)} %bitcast.2), custom_call_target="tpu_custom_call" | custom-call | bytes 2818048 | tf_op jit(solution)/shard_map/pallas_call | solution.py:181
  9.1 0.0 collective-permute-done.1
  9.1 1.4 %collective-permute-start.2 = (bf16[16,1280]{1,0:T(8,128)(2,1)S(1)}, bf16[16,1280]{1,0:T(8,128)(2,1)S(1)}, u32[]{:S(2)}, u32[]{:S(2)}) collective-permute-start(bf16[16,1280]{1,0:T(8,128)(2,1)S(1)} %constant_dynamic-update-slice_fusion.carried.after), channel_id=1, source_target_pairs={{0,3},{1,2},{2,1},{3,0},{4,7},{5,6},{6,5},{7,4},{8,11},{9,10},{10,... | collective-permute-start | bytes 122888 | tf_op jit(solution)/shard_map/ppermute | solution.py:34
  10.5 1.8 %shard_map.165 = (bf16[688,2048]{1,0:T(8,128)(2,1)S(1)}, bf16[16,1280]{1,0:T(8,128)(2,1)S(1)}) custom-call(bf16[16,1280]{1,0:T(8,128)(2,1)S(1)} %constant_dynamic-update-slice_fusion.carried.after, bf16[16,1280]{1,0:T(8,128)(2,1)S(1)} %constant_dynamic-update-slice_fusion.carried.after, bf16[688,4096]{1,0:T(8,128)(2,1)} %bitcast.3), custom_call_target="tpu_custom_call" | custom-call | bytes 2818048 | tf_op jit(solution)/shard_map/pallas_call | solution.py:181
  12.3 0.5 collective-permute-done.2
  12.8 0.1 collective-permute-start.3
  12.9 1.2 %collective-permute-done.3.others = bf16[32,1280]{1,0:T(8,128)(2,1)S(1)} collective-permute-done((bf16[32,1280]{1,0:T(8,128)(2,1)S(1)}, bf16[32,1280]{1,0:T(8,128)(2,1)S(1)}, u32[]{:S(2)}, u32[]{:S(2)}) %collective-permute-start.3) | collective-permute-done | bytes 81952 | tf_op jit(solution)/shard_map/ppermute | solution.py:34
  14.1 1.2 %shard_map.166 = (bf16[16,1280]{1,0:T(8,128)(2,1)S(1)}, f32[16,1280]{1,0:T(8,128)S(1)}, f32[16,1280]{1,0:T(8,128)S(1)}) custom-call(bf16[32,1280]{1,0:T(8,128)(2,1)S(1)} %constant_dynamic-update-slice_fusion.2.frames, bf16[32,1280]{1,0:T(8,128)(2,1)S(1)} %collective-permute-done.3.others, f32[1280]{0:T(1024)S(1)} %get-tuple-element.35.gain, ...), custom_call_target="tpu_custom_call" | custom-call | flops 104857600 | bytes 1638400 | tf_op jit(solution)/shard_map/pallas_call | solution.py:93
  15.3 0.2 collective-permute-start.4
  15.4 2.4 %collective-permute-start.8 = (bf16[4,4096]{1,0:T(4,128)(2,1)S(1)}, bf16[4,4096]{1,0:T(4,128)(2,1)S(1)}, u32[]{:S(2)}, u32[]{:S(2)}) collective-permute-start(bf16[4,4096]{1,0:T(4,128)(2,1)S(1)} %get-tuple-element.46), channel_id=1, source_target_pairs={{0,9},{1,8},{2,11},{3,10},{4,13},{5,12},{6,15},{7,14},{8,1},{9,0},... | collective-permute-start | bytes 98312 | tf_op jit(solution)/shard_map/ppermute | solution.py:34
  17.9 0.0 collective-permute-done.4
  17.9 1.5 %collective-permute-start.5 = (bf16[16,1280]{1,0:T(8,128)(2,1)S(1)}, bf16[16,1280]{1,0:T(8,128)(2,1)S(1)}, u32[]{:S(2)}, u32[]{:S(2)}) collective-permute-start(bf16[16,1280]{1,0:T(8,128)(2,1)S(1)} %fusion.1), channel_id=1, source_target_pairs={{0,3},{1,2},{2,1},{3,0},{4,7},{5,6},{6,5},{7,4},{8,11},{9,10},{10,... | collective-permute-start | bytes 122888 | tf_op jit(solution)/shard_map/ppermute | solution.py:34
  19.4 0.2 collective-permute-done.8
  19.7 1.3 %collective-permute-start.9 = (bf16[8,4096]{1,0:T(8,128)(2,1)S(1)}, bf16[8,4096]{1,0:T(8,128)(2,1)S(1)}, u32[]{:S(2)}, u32[]{:S(2)}) collective-permute-start(bf16[8,4096]{1,0:T(8,128)(2,1)S(1)} %pad_maximum_fusion.2), channel_id=1, source_target_pairs={{0,5},{1,4},{2,7},{3,6},{4,1},{5,0},{6,3},{7,2},{8,13},{9,12},{10,... | collective-permute-start | bytes 196616 | tf_op jit(solution)/shard_map/ppermute | solution.py:34
  21.1 0.3 collective-permute-done.5
  21.4 1.6 %collective-permute-start.6 = (bf16[16,1280]{1,0:T(8,128)(2,1)S(1)}, bf16[16,1280]{1,0:T(8,128)(2,1)S(1)}, u32[]{:S(2)}, u32[]{:S(2)}) collective-permute-start(bf16[16,1280]{1,0:T(8,128)(2,1)S(1)} %fusion.2), channel_id=1, source_target_pairs={{0,5},{1,4},{2,7},{3,6},{4,1},{5,0},{6,3},{7,2},{8,13},{9,12},{10,... | collective-permute-start | bytes 122888 | tf_op jit(solution)/shard_map/ppermute | solution.py:34
  23.0 0.7 %collective-permute-done.9 = bf16[8,4096]{1,0:T(8,128)(2,1)S(1)} collective-permute-done((bf16[8,4096]{1,0:T(8,128)(2,1)S(1)}, bf16[8,4096]{1,0:T(8,128)(2,1)S(1)}, u32[]{:S(2)}, u32[]{:S(2)}) %collective-permute-start.9) | collective-permute-done | bytes 65568 | tf_op jit(solution)/shard_map/ppermute | solution.py:34
  23.7 0.1 pad_maximum_fusion.1.after
  23.8 1.5 %collective-permute-start.13 = (bf16[16,4096]{1,0:T(8,128)(2,1)S(1)}, bf16[16,4096]{1,0:T(8,128)(2,1)S(1)}, u32[]{:S(2)}, u32[]{:S(2)}) collective-permute-start(bf16[16,4096]{1,0:T(8,128)(2,1)S(1)} %pad_maximum_fusion.1.after), channel_id=1, source_target_pairs={{0,3},{1,2},{2,1},{3,0},{4,7},{5,6},{6,5},{7,4},{8,11},{9,10},{10,... | collective-permute-start | bytes 393224 | tf_op jit(solution)/shard_map/ppermute | solution.py:34
  25.2 0.0 collective-permute-done.6
  25.3 3.2 %collective-permute-start.7 = (bf16[16,1280]{1,0:T(8,128)(2,1)S(1)}, bf16[16,1280]{1,0:T(8,128)(2,1)S(1)}, u32[]{:S(2)}, u32[]{:S(2)}) collective-permute-start(bf16[16,1280]{1,0:T(8,128)(2,1)S(1)} %get-tuple-element.59), channel_id=1, source_target_pairs={{0,9},{1,8},{2,11},{3,10},{4,13},{5,12},{6,15},{7,14},{8,1},{9,0},... | collective-permute-start | bytes 122888 | tf_op jit(solution)/shard_map/ppermute | solution.py:34
  28.5 2.0 %collective-permute-done.7.arrived = bf16[16,1280]{1,0:T(8,128)(2,1)S(1)} collective-permute-done((bf16[16,1280]{1,0:T(8,128)(2,1)S(1)}, bf16[16,1280]{1,0:T(8,128)(2,1)S(1)}, u32[]{:S(2)}, u32[]{:S(2)}) %collective-permute-start.7) | collective-permute-done | bytes 40992 | tf_op jit(solution)/shard_map/ppermute | solution.py:34
  30.5 0.2 shard_map.167.post
  30.7 0.2 collective-permute-start.10
  30.9 0.0 collective-permute-done.13
  30.9 0.1 pad_maximum_fusion.after.prompts
  30.9 0.5 collective-permute-start.16
  31.4 0.6 collective-permute-done.10.other
  32.0 0.2 shard_map.168.carried.after
  32.2 2.4 %collective-permute-start.11 = (bf16[1,32,256]{2,1,0:T(8,128)(2,1)S(1)}, bf16[1,32,256]{2,1,0:T(8,128)(2,1)S(1)}, u32[]{:S(2)}, u32[]{:S(2)}) collective-permute-start(bf16[1,32,256]{2,1,0:T(8,128)(2,1)S(1)} %shard_map.168.carried.after), channel_id=1, source_target_pairs={{0,9},{1,8},{2,11},{3,10},{4,13},{5,12},{6,15},{7,14},{8,1},{9,0},... | collective-permute-start | bytes 49160 | tf_op jit(solution)/shard_map/ppermute | solution.py:34
  34.6 2.6 %shard_map.169 = (bf16[688,4096]{1,0:T(8,128)(2,1)S(1)}, bf16[1,32,256]{2,1,0:T(8,128)(2,1)S(1)}) custom-call(bf16[1,32,256]{2,1,0:T(8,128)(2,1)S(1)} %shard_map.168.carried.after, bf16[1,32,256]{2,1,0:T(8,128)(2,1)S(1)} %shard_map.168.carried.after, bf16[688,4096]{1,0:T(8,128)(2,1)} %bitcast.4), custom_call_target="tpu_custom_call" | custom-call | bytes 5636096 | tf_op jit(solution)/shard_map/pallas_call | solution.py:181
  37.2 0.0 collective-permute-done.11
  37.3 2.7 %collective-permute-start.12 = (bf16[2,32,256]{2,1,0:T(8,128)(2,1)S(1)}, bf16[2,32,256]{2,1,0:T(8,128)(2,1)S(1)}, u32[]{:S(2)}, u32[]{:S(2)}) collective-permute-start(bf16[2,32,256]{2,1,0:T(8,128)(2,1)S(1)} %pad_maximum_fusion.3), channel_id=1, source_target_pairs={{0,5},{1,4},{2,7},{3,6},{4,1},{5,0},{6,3},{7,2},{8,13},{9,12},{10,... | collective-permute-start | bytes 98312 | tf_op jit(solution)/shard_map/ppermute | solution.py:34
  40.0 1.6 %collective-permute-done.12 = bf16[2,32,256]{2,1,0:T(8,128)(2,1)S(1)} collective-permute-done((bf16[2,32,256]{2,1,0:T(8,128)(2,1)S(1)}, bf16[2,32,256]{2,1,0:T(8,128)(2,1)S(1)}, u32[]{:S(2)}, u32[]{:S(2)}) %collective-permute-start.12) | collective-permute-done | bytes 32800 | tf_op jit(solution)/shard_map/ppermute | solution.py:34
  41.6 0.7 collective-permute-start.14
  42.3 2.6 %shard_map.170 = (bf16[688,4096]{1,0:T(8,128)(2,1)S(1)}, bf16[4,32,256]{2,1,0:T(8,128)(2,1)S(1)}) custom-call(bf16[4,32,256]{2,1,0:T(8,128)(2,1)S(1)} %constant_dynamic-update-slice_fusion.4.carried, bf16[32,4096]{1,0:T(8,128)(2,1)S(1)} %pad_maximum_fusion.after.prompts, bf16[688,4096]{1,0:T(8,128)(2,1)} %source.1), custom_call_target="tpu_custom_call" | custom-call | bytes 5636096 | tf_op jit(solution)/shard_map/pallas_call | solution.py:181
  44.9 0.8 %collective-permute-done.14 = bf16[4,32,256]{2,1,0:T(8,128)(2,1)S(1)} collective-permute-done((bf16[4,32,256]{2,1,0:T(8,128)(2,1)S(1)}, bf16[4,32,256]{2,1,0:T(8,128)(2,1)S(1)}, u32[]{:S(2)}, u32[]{:S(2)}) %collective-permute-start.14) | collective-permute-done | bytes 65568 | tf_op jit(solution)/shard_map/ppermute | solution.py:34
  45.7 0.1 collective-permute-start.15
  45.8 0.0 collective-permute-done.16.others
  45.8 1.2 %collective-permute-done.15.far = bf16[8,32,256]{2,1,0:T(8,128)(2,1)S(1)} collective-permute-done((bf16[8,32,256]{2,1,0:T(8,128)(2,1)S(1)}, bf16[8,32,256]{2,1,0:T(8,128)(2,1)S(1)}, u32[]{:S(2)}, u32[]{:S(2)}) %collective-permute-start.15) | collective-permute-done | bytes 131104 | tf_op jit(solution)/shard_map/ppermute | solution.py:34
  47.1 5.1 %shard_map.171 = (bf16[32,4096]{1,0:T(8,128)(2,1)S(1)}, f32[32,4096]{1,0:T(8,128)S(1)}) custom-call(bf16[8,32,256]{2,1,0:T(8,128)(2,1)S(1)} %constant_dynamic-update-slice_fusion.7.near, bf16[8,32,256]{2,1,0:T(8,128)(2,1)S(1)} %collective-permute-done.15.far, s32[64]{0:T(128)S(1)} %get-tuple-element.51.source, ...), custom_call_target="tpu_custom_call" | custom-call | flops 1082130432 | bytes 11272192 | tf_op jit(solution)/shard_map/pallas_call | solution.py:254
  52.1 0.2 collective-permute-start.17
  52.4 1.4 %collective-permute-done.17 = bf16[32,4096]{1,0:T(8,128)(2,1)S(1)} collective-permute-done((bf16[32,4096]{1,0:T(8,128)(2,1)S(1)}, bf16[32,4096]{1,0:T(8,128)(2,1)S(1)}, u32[]{:S(2)}, u32[]{:S(2)}) %collective-permute-start.17) | collective-permute-done | bytes 262176 | tf_op jit(solution)/shard_map/ppermute | solution.py:34
  53.8 0.1 convert_add_fusion
  53.8 0.7 %collective-permute-start.18 = (bf16[16,4096]{1,0:T(8,128)(2,1)S(1)}, bf16[16,4096]{1,0:T(8,128)(2,1)S(1)}, u32[]{:S(2)}, u32[]{:S(2)}) collective-permute-start(bf16[16,4096]{1,0:T(8,128)(2,1)S(1)} %slice.41), channel_id=1, source_target_pairs={{0,3},{1,2},{2,1},{3,0},{4,7},{5,6},{6,5},{7,4},{8,11},{9,10},{10,... | collective-permute-start | bytes 393224 | tf_op jit(solution)/shard_map/ppermute | solution.py:34
  54.6 4.8 %collective-permute-done.18 = bf16[16,4096]{1,0:T(8,128)(2,1)S(1)} collective-permute-done((bf16[16,4096]{1,0:T(8,128)(2,1)S(1)}, bf16[16,4096]{1,0:T(8,128)(2,1)S(1)}, u32[]{:S(2)}, u32[]{:S(2)}) %collective-permute-start.18) | collective-permute-done | bytes 131104 | tf_op jit(solution)/shard_map/ppermute | solution.py:34
  59.4 1.4 %collective-permute-start.19 = (bf16[8,4096]{1,0:T(8,128)(2,1)S(1)}, bf16[8,4096]{1,0:T(8,128)(2,1)S(1)}, u32[]{:S(2)}, u32[]{:S(2)}) collective-permute-start(bf16[8,4096]{1,0:T(8,128)(2,1)S(1)} %slice.42), channel_id=1, source_target_pairs={{0,5},{1,4},{2,7},{3,6},{4,1},{5,0},{6,3},{7,2},{8,13},{9,12},{10,... | collective-permute-start | bytes 196616 | tf_op jit(solution)/shard_map/ppermute | solution.py:34
  60.8 2.8 %collective-permute-done.19 = bf16[8,4096]{1,0:T(8,128)(2,1)S(1)} collective-permute-done((bf16[8,4096]{1,0:T(8,128)(2,1)S(1)}, bf16[8,4096]{1,0:T(8,128)(2,1)S(1)}, u32[]{:S(2)}, u32[]{:S(2)}) %collective-permute-start.19) | collective-permute-done | bytes 65568 | tf_op jit(solution)/shard_map/ppermute | solution.py:34
  63.6 1.2 %collective-permute-start.20 = (bf16[4,4096]{1,0:T(4,128)(2,1)S(1)}, bf16[4,4096]{1,0:T(4,128)(2,1)S(1)}, u32[]{:S(2)}, u32[]{:S(2)}) collective-permute-start(bf16[4,4096]{1,0:T(4,128)(2,1)S(1)} %slice.43), channel_id=1, source_target_pairs={{0,9},{1,8},{2,11},{3,10},{4,13},{5,12},{6,15},{7,14},{8,1},{9,0},... | collective-permute-start | bytes 98312 | tf_op jit(solution)/shard_map/ppermute | solution.py:34
  64.8 3.1 %collective-permute-done.20 = bf16[4,4096]{1,0:T(4,128)(2,1)S(1)} collective-permute-done((bf16[4,4096]{1,0:T(4,128)(2,1)S(1)}, bf16[4,4096]{1,0:T(4,128)(2,1)S(1)}, u32[]{:S(2)}, u32[]{:S(2)}) %collective-permute-start.20) | collective-permute-done | bytes 32800 | tf_op jit(solution)/shard_map/ppermute | solution.py:34
  67.9 0.6 fusion
  (20 shorter events, 0.2 us)
Async XLA Ops:
  0.0 5.3 %collective-permute-start = (bf16[4,1280]{1,0:T(4,128)(2,1)}, bf16[4,1280]{1,0:T(4,128)(2,1)S(1)}, u32[]{:S(2)}, u32[]{:S(2)}) collective-permute-start(bf16[4,1280]{1,0:T(4,128)(2,1)} %refs_0_.1), channel_id=1, source_target_pairs={{0,9},{1,8},{2,11},{3,10},{4,13},{5,12},{6,15},{7,14},{8,1},{9,0},... | collective-permute-start | bytes 30728 | tf_op jit(solution)/shard_map/ppermute | solution.py:34
  5.3 3.7 %collective-permute-start.1 = (bf16[8,1280]{1,0:T(8,128)(2,1)S(1)}, bf16[8,1280]{1,0:T(8,128)(2,1)S(1)}, u32[]{:S(2)}, u32[]{:S(2)}) collective-permute-start(bf16[8,1280]{1,0:T(8,128)(2,1)S(1)} %pad_maximum_fusion.4.carried.after), channel_id=1, source_target_pairs={{0,5},{1,4},{2,7},{3,6},{4,1},{5,0},{6,3},{7,2},{8,13},{9,12},{10,... | collective-permute-start | bytes 61448 | tf_op jit(solution)/shard_map/ppermute | solution.py:34
  9.1 3.7 %collective-permute-start.2 = (bf16[16,1280]{1,0:T(8,128)(2,1)S(1)}, bf16[16,1280]{1,0:T(8,128)(2,1)S(1)}, u32[]{:S(2)}, u32[]{:S(2)}) collective-permute-start(bf16[16,1280]{1,0:T(8,128)(2,1)S(1)} %constant_dynamic-update-slice_fusion.carried.after), channel_id=1, source_target_pairs={{0,3},{1,2},{2,1},{3,0},{4,7},{5,6},{6,5},{7,4},{8,11},{9,10},{10,... | collective-permute-start | bytes 122888 | tf_op jit(solution)/shard_map/ppermute | solution.py:34
  12.8 1.3 %collective-permute-start.3 = (bf16[32,1280]{1,0:T(8,128)(2,1)S(1)}, bf16[32,1280]{1,0:T(8,128)(2,1)S(1)}, u32[]{:S(2)}, u32[]{:S(2)}) collective-permute-start(bf16[32,1280]{1,0:T(8,128)(2,1)S(1)} %constant_dynamic-update-slice_fusion.2.frames), channel_id=1, source_target_pairs={{0,1},{1,0},{2,3},{3,2},{4,5},{5,4},{6,7},{7,6},{8,9},{9,8},{10,11... | collective-permute-start | bytes 245768 | tf_op jit(solution)/shard_map/ppermute | solution.py:34
  15.3 2.6 %collective-permute-start.4 = (bf16[16,1280]{1,0:T(8,128)(2,1)S(1)}, bf16[16,1280]{1,0:T(8,128)(2,1)S(1)}, u32[]{:S(2)}, u32[]{:S(2)}) collective-permute-start(bf16[16,1280]{1,0:T(8,128)(2,1)S(1)} %get-tuple-element.42), channel_id=1, source_target_pairs={{0,1},{1,0},{2,3},{3,2},{4,5},{5,4},{6,7},{7,6},{8,9},{9,8},{10,11... | collective-permute-start | bytes 122888 | tf_op jit(solution)/shard_map/ppermute | solution.py:34
  15.4 4.2 %collective-permute-start.8 = (bf16[4,4096]{1,0:T(4,128)(2,1)S(1)}, bf16[4,4096]{1,0:T(4,128)(2,1)S(1)}, u32[]{:S(2)}, u32[]{:S(2)}) collective-permute-start(bf16[4,4096]{1,0:T(4,128)(2,1)S(1)} %get-tuple-element.46), channel_id=1, source_target_pairs={{0,9},{1,8},{2,11},{3,10},{4,13},{5,12},{6,15},{7,14},{8,1},{9,0},... | collective-permute-start | bytes 98312 | tf_op jit(solution)/shard_map/ppermute | solution.py:34
  17.9 3.5 %collective-permute-start.5 = (bf16[16,1280]{1,0:T(8,128)(2,1)S(1)}, bf16[16,1280]{1,0:T(8,128)(2,1)S(1)}, u32[]{:S(2)}, u32[]{:S(2)}) collective-permute-start(bf16[16,1280]{1,0:T(8,128)(2,1)S(1)} %fusion.1), channel_id=1, source_target_pairs={{0,3},{1,2},{2,1},{3,0},{4,7},{5,6},{6,5},{7,4},{8,11},{9,10},{10,... | collective-permute-start | bytes 122888 | tf_op jit(solution)/shard_map/ppermute | solution.py:34
  19.7 4.0 %collective-permute-start.9 = (bf16[8,4096]{1,0:T(8,128)(2,1)S(1)}, bf16[8,4096]{1,0:T(8,128)(2,1)S(1)}, u32[]{:S(2)}, u32[]{:S(2)}) collective-permute-start(bf16[8,4096]{1,0:T(8,128)(2,1)S(1)} %pad_maximum_fusion.2), channel_id=1, source_target_pairs={{0,5},{1,4},{2,7},{3,6},{4,1},{5,0},{6,3},{7,2},{8,13},{9,12},{10,... | collective-permute-start | bytes 196616 | tf_op jit(solution)/shard_map/ppermute | solution.py:34
  21.4 3.8 %collective-permute-start.6 = (bf16[16,1280]{1,0:T(8,128)(2,1)S(1)}, bf16[16,1280]{1,0:T(8,128)(2,1)S(1)}, u32[]{:S(2)}, u32[]{:S(2)}) collective-permute-start(bf16[16,1280]{1,0:T(8,128)(2,1)S(1)} %fusion.2), channel_id=1, source_target_pairs={{0,5},{1,4},{2,7},{3,6},{4,1},{5,0},{6,3},{7,2},{8,13},{9,12},{10,... | collective-permute-start | bytes 122888 | tf_op jit(solution)/shard_map/ppermute | solution.py:34
  23.8 7.1 %collective-permute-start.13 = (bf16[16,4096]{1,0:T(8,128)(2,1)S(1)}, bf16[16,4096]{1,0:T(8,128)(2,1)S(1)}, u32[]{:S(2)}, u32[]{:S(2)}) collective-permute-start(bf16[16,4096]{1,0:T(8,128)(2,1)S(1)} %pad_maximum_fusion.1.after), channel_id=1, source_target_pairs={{0,3},{1,2},{2,1},{3,0},{4,7},{5,6},{6,5},{7,4},{8,11},{9,10},{10,... | collective-permute-start | bytes 393224 | tf_op jit(solution)/shard_map/ppermute | solution.py:34
  25.3 5.2 %collective-permute-start.7 = (bf16[16,1280]{1,0:T(8,128)(2,1)S(1)}, bf16[16,1280]{1,0:T(8,128)(2,1)S(1)}, u32[]{:S(2)}, u32[]{:S(2)}) collective-permute-start(bf16[16,1280]{1,0:T(8,128)(2,1)S(1)} %get-tuple-element.59), channel_id=1, source_target_pairs={{0,9},{1,8},{2,11},{3,10},{4,13},{5,12},{6,15},{7,14},{8,1},{9,0},... | collective-permute-start | bytes 122888 | tf_op jit(solution)/shard_map/ppermute | solution.py:34
  30.7 1.3 %collective-permute-start.10 = (bf16[16,1280]{1,0:T(8,128)(2,1)S(1)}, bf16[16,1280]{1,0:T(8,128)(2,1)S(1)}, u32[]{:S(2)}, u32[]{:S(2)}) collective-permute-start(bf16[16,1280]{1,0:T(8,128)(2,1)S(1)} %shard_map.167.post), channel_id=1, source_target_pairs={{0,1},{1,0},{2,3},{3,2},{4,5},{5,4},{6,7},{7,6},{8,9},{9,8},{10,11... | collective-permute-start | bytes 122888 | tf_op jit(solution)/shard_map/ppermute | solution.py:34
  30.9 14.9 %collective-permute-start.16 = (bf16[32,4096]{1,0:T(8,128)(2,1)S(1)}, bf16[32,4096]{1,0:T(8,128)(2,1)S(1)}, u32[]{:S(2)}, u32[]{:S(2)}) collective-permute-start(bf16[32,4096]{1,0:T(8,128)(2,1)S(1)} %pad_maximum_fusion.after.prompts), channel_id=1, source_target_pairs={{0,1},{1,0},{2,3},{3,2},{4,5},{5,4},{6,7},{7,6},{8,9},{9,8},{10,11... | collective-permute-start | bytes 786440 | tf_op jit(solution)/shard_map/ppermute | solution.py:34
  32.2 5.0 %collective-permute-start.11 = (bf16[1,32,256]{2,1,0:T(8,128)(2,1)S(1)}, bf16[1,32,256]{2,1,0:T(8,128)(2,1)S(1)}, u32[]{:S(2)}, u32[]{:S(2)}) collective-permute-start(bf16[1,32,256]{2,1,0:T(8,128)(2,1)S(1)} %shard_map.168.carried.after), channel_id=1, source_target_pairs={{0,9},{1,8},{2,11},{3,10},{4,13},{5,12},{6,15},{7,14},{8,1},{9,0},... | collective-permute-start | bytes 49160 | tf_op jit(solution)/shard_map/ppermute | solution.py:34
  37.3 4.3 %collective-permute-start.12 = (bf16[2,32,256]{2,1,0:T(8,128)(2,1)S(1)}, bf16[2,32,256]{2,1,0:T(8,128)(2,1)S(1)}, u32[]{:S(2)}, u32[]{:S(2)}) collective-permute-start(bf16[2,32,256]{2,1,0:T(8,128)(2,1)S(1)} %pad_maximum_fusion.3), channel_id=1, source_target_pairs={{0,5},{1,4},{2,7},{3,6},{4,1},{5,0},{6,3},{7,2},{8,13},{9,12},{10,... | collective-permute-start | bytes 98312 | tf_op jit(solution)/shard_map/ppermute | solution.py:34
  41.6 4.1 %collective-permute-start.14 = (bf16[4,32,256]{2,1,0:T(8,128)(2,1)S(1)}, bf16[4,32,256]{2,1,0:T(8,128)(2,1)S(1)}, u32[]{:S(2)}, u32[]{:S(2)}) collective-permute-start(bf16[4,32,256]{2,1,0:T(8,128)(2,1)S(1)} %constant_dynamic-update-slice_fusion.4.carried), channel_id=1, source_target_pairs={{0,3},{1,2},{2,1},{3,0},{4,7},{5,6},{6,5},{7,4},{8,11},{9,10},{10,... | collective-permute-start | bytes 196616 | tf_op jit(solution)/shard_map/ppermute | solution.py:34
  45.7 1.3 %collective-permute-start.15 = (bf16[8,32,256]{2,1,0:T(8,128)(2,1)S(1)}, bf16[8,32,256]{2,1,0:T(8,128)(2,1)S(1)}, u32[]{:S(2)}, u32[]{:S(2)}) collective-permute-start(bf16[8,32,256]{2,1,0:T(8,128)(2,1)S(1)} %constant_dynamic-update-slice_fusion.7.near), channel_id=1, source_target_pairs={{0,1},{1,0},{2,3},{3,2},{4,5},{5,4},{6,7},{7,6},{8,9},{9,8},{10,11... | collective-permute-start | bytes 393224 | tf_op jit(solution)/shard_map/ppermute | solution.py:34
  52.1 1.6 %collective-permute-start.17 = (bf16[32,4096]{1,0:T(8,128)(2,1)S(1)}, bf16[32,4096]{1,0:T(8,128)(2,1)S(1)}, u32[]{:S(2)}, u32[]{:S(2)}) collective-permute-start(bf16[32,4096]{1,0:T(8,128)(2,1)S(1)} %get-tuple-element.58), channel_id=1, source_target_pairs={{0,1},{1,0},{2,3},{3,2},{4,5},{5,4},{6,7},{7,6},{8,9},{9,8},{10,11... | collective-permute-start | bytes 786440 | tf_op jit(solution)/shard_map/ppermute | solution.py:34
  53.8 5.5 %collective-permute-start.18 = (bf16[16,4096]{1,0:T(8,128)(2,1)S(1)}, bf16[16,4096]{1,0:T(8,128)(2,1)S(1)}, u32[]{:S(2)}, u32[]{:S(2)}) collective-permute-start(bf16[16,4096]{1,0:T(8,128)(2,1)S(1)} %slice.41), channel_id=1, source_target_pairs={{0,3},{1,2},{2,1},{3,0},{4,7},{5,6},{6,5},{7,4},{8,11},{9,10},{10,... | collective-permute-start | bytes 393224 | tf_op jit(solution)/shard_map/ppermute | solution.py:34
  59.4 4.1 %collective-permute-start.19 = (bf16[8,4096]{1,0:T(8,128)(2,1)S(1)}, bf16[8,4096]{1,0:T(8,128)(2,1)S(1)}, u32[]{:S(2)}, u32[]{:S(2)}) collective-permute-start(bf16[8,4096]{1,0:T(8,128)(2,1)S(1)} %slice.42), channel_id=1, source_target_pairs={{0,5},{1,4},{2,7},{3,6},{4,1},{5,0},{6,3},{7,2},{8,13},{9,12},{10,... | collective-permute-start | bytes 196616 | tf_op jit(solution)/shard_map/ppermute | solution.py:34
  63.6 4.3 %collective-permute-start.20 = (bf16[4,4096]{1,0:T(4,128)(2,1)S(1)}, bf16[4,4096]{1,0:T(4,128)(2,1)S(1)}, u32[]{:S(2)}, u32[]{:S(2)}) collective-permute-start(bf16[4,4096]{1,0:T(4,128)(2,1)S(1)} %slice.43), channel_id=1, source_target_pairs={{0,9},{1,8},{2,11},{3,10},{4,13},{5,12},{6,15},{7,14},{8,1},{9,0},... | collective-permute-start | bytes 98312 | tf_op jit(solution)/shard_map/ppermute | solution.py:34

commit v4 on v3

--- a/solution.py
+++ b/solution.py
@@ -168,38 +168,42 @@
     )(*[in_hbm(value) for value in values])
 
 
-def fetch_kernel(start, carried, after, source, target, passed, sem):
-    width = target.shape[1]
-    copy = pltpu.make_async_copy(source.at[:, pl.ds(start, width)], target, sem)
+def fetch_kernel(start, width, carried, after, source, *refs):
+    target, passed, sem = refs[-3:]
+    part = (slice(None), pl.ds(start, width))
+    copy = pltpu.make_async_copy(source.at[part], target.at[part], sem)
     copy.start()
     passed[...] = carried[...]
     copy.wait()
 
 
-def fetch(carried, after, weight, start, width):
+def fetch(carried, after, weight, held, start, width):
     vmem = pl.BlockSpec(memory_space=pltpu.VMEM)
-    return pl.pallas_call(
-        functools.partial(fetch_kernel, start),
+    held = [] if held is None else [held]
+    return pl.pallas_call(
+        functools.partial(fetch_kernel, start, width),
         out_shape=[
-            pltpu.VMEM((weight.shape[0], width), weight.dtype),
+            pltpu.VMEM(weight.shape, weight.dtype),
             jax.ShapeDtypeStruct(carried.shape, carried.dtype),
         ],
         in_specs=[
             vmem,
             pl.BlockSpec(memory_space=pl.ANY),
             pl.BlockSpec(memory_space=pltpu.HBM),
-        ],
+        ]
+        + [vmem] * len(held),
         out_specs=[vmem] * 2,
         scratch_shapes=[pltpu.SemaphoreType.DMA],
+        input_output_aliases={3: 0} if held else {},
         compiler_params=pltpu.CompilerParams(vmem_limit_bytes=2 * 2**20),
         cost_estimate=pl.CostEstimate(
             flops=0, bytes_accessed=2 * weight.shape[0] * width, transcendentals=0
         ),
-    )(carried, after, in_hbm(weight))
+    )(carried, after, in_hbm(weight), *held)
 
 
 def language_kernel(
-    bits, near, far, source, prompts, others, gain, gate, rest, up, down,
+    bits, near, far, source, prompts, others, gain, gate, up, down,
     send, keep, packed, normed,
 ):
     count, audio, columns = near.shape
@@ -233,10 +237,8 @@
         part = slice(device * columns, (device + 1) * columns)
         value = packed[:, part].astype(jnp.float32) * scale * row(gain, part)
         normed[:, part] = value.astype(jnp.bfloat16)
-    cut = width // 2
-    gated = dot_last(normed[:, :cut], gate[...]) + dot_last(normed[:, cut:], rest[...])
-    lifted = dot_last(normed[...], up[...])
-    hidden = (gated * jax.nn.sigmoid(gated) * lifted).astype(jnp.bfloat16)
+    gated, lifted = dot_last(gate[...], normed[...]), dot_last(up[...], normed[...])
+    hidden = (gated * jax.nn.sigmoid(gated) * lifted).T.astype(jnp.bfloat16)
     held = lax.broadcasted_iota(jnp.int32, (half, 1), 0) < own
     pieces = 4
     for piece in range(pieces):
@@ -248,7 +250,7 @@
         )
 
 
-def language(features, source, prompts, gain, gate, rest, up, down, bits):
+def language(features, source, prompts, gain, gate, up, down, bits):
     half, width = prompts[0].shape
     vmem = pl.BlockSpec(memory_space=pltpu.VMEM)
     return pl.pallas_call(
@@ -257,14 +259,14 @@
             jax.ShapeDtypeStruct((half, width), jnp.bfloat16),
             jax.ShapeDtypeStruct((half, width), jnp.float32),
         ],
-        in_specs=[vmem] * 10,
+        in_specs=[vmem] * 9,
         out_specs=[vmem] * 2,
         scratch_shapes=[pltpu.VMEM((2 * half, width), jnp.bfloat16)] * 2,
         compiler_params=pltpu.CompilerParams(vmem_limit_bytes=12 * 2**20),
         cost_estimate=pl.CostEstimate(
             flops=12 * half * up.size, bytes_accessed=4 * up.size, transcendentals=0
         ),
-    )(*features, source, *prompts, gain, gate, rest, up, down)
+    )(*features, source, *prompts, gain, gate, up, down)
 
 
 def layer_norm(values, gain, shift):
@@ -372,6 +374,7 @@
     steps = range(bits - 1, 0, -1)
     gate_rows, up_rows = gate_weight.T, up_weight.T
     arrived = swap(frames, bits - 1, count)
+    prompts_arrived = swap(prompt_embeds, bits - 1, count)
     (
         block, prompts, enc_gain, enc_shift, enc_down_bias, enc_up_bias, enc_up, enc_down,
         post_gain, post_shift, proj_weight, proj_bias, rms_gain, slot_source,
@@ -379,13 +382,16 @@
         frames, prompt_embeds, enc_gain, enc_shift, enc_down_bias, enc_up_bias, enc_up, enc_down,
         post_gain, post_shift, proj_weight, proj_bias, rms_gain, slot_source,
     )
-    gate = []
+    gate = up = down = None
+    part = width // 4
+    large = width // 2 - width // 8
     block = jnp.concatenate([block, arrived])
+    prompts = jnp.concatenate([prompts, prompts_arrived])
     for step, bit in enumerate(steps[1:]):
         arrived = swap(block, bit, count)
         if step < 2:
-            piece, block = fetch(block, block, gate_rows, step * width // 2, width // 2)
-            gate.append(piece)
+            after = prompts if step else block
+            gate, block = fetch(block, after, gate_rows, gate, step * part, part)
         block = jnp.concatenate([block, arrived])
     send, total, base = encoder(
         (block, swap(block, 0, count)),
@@ -395,25 +401,33 @@
         bits,
     )
     arrived = swap(send, 0, count)
-    for step, bit in enumerate(range(1, bits)):
+    for step, bit in enumerate((steps[1], steps[0], *steps[2:])):
         total = total + arrived.astype(jnp.float32)
-        arrived = swap(total.astype(jnp.bfloat16), bit, count)
-        if step < 2:
-            prompts = jnp.concatenate([prompts, swap(prompts, steps[step], count)])
-    post = post_norm(total, arrived, base, post_gain, post_shift, prompts)
+        outgoing = total.astype(jnp.bfloat16)
+        if step != 1:
+            outgoing, prompts = lax.optimization_barrier((outgoing, prompts))
+        arrived = swap(outgoing, bit, count)
+        if step != 1:
+            early = prompts
+            prompts = jnp.concatenate([prompts, swap(prompts, bit, count)])
+        if step == 1:
+            gate, total = fetch(total, total, gate_rows, gate, 2 * part, 2 * part)
+        elif step < 3:
+            up, total = fetch(total, total, up_rows, up, step // 2 * large, large)
+    post = post_norm(total, arrived, base, post_gain, post_shift, early)
     features = project(post, swap(post, 0, count), proj_weight, proj_bias, bits)
-    for bit in steps[2:]:
-        prompts = jnp.concatenate([prompts, swap(prompts, bit, count)])
     for step, bit in enumerate(steps):
         arrived = swap(features, bit, count)
-        if step == 0:
-            up, features = fetch(features, features, up_rows, 0, width)
-        if step == 2:
-            down, features = fetch(features, prompts, down_weight, 0, width)
+        if step == 1:
+            left = width - 2 * large
+            up, features = fetch(features, features, up_rows, up, 2 * large, left)
+        elif step < 3:
+            after = features if step else prompts
+            down, features = fetch(features, after, down_weight, down, step * part, 2 * part)
         features = jnp.concatenate([features, arrived])
     features = features, swap(features, 0, count)
     prompts = prompts, swap(prompts, 0, count)
-    send, total = language(features, slot_source, prompts, rms_gain, *gate, up, down, bits)
+    send, total = language(features, slot_source, prompts, rms_gain, gate, up, down, bits)
     total = total + swap(send, 0, count).astype(jnp.float32)
     for bit in range(1, bits):
         half = total.shape[0] // 2

time: 68.8 us -> 65.6 us (0.953)
  waiting for transfers between devices: 21.2 us -> 14.7 us
  Pallas kernels: 17.4 us -> 20.8 us
    ppermute x21, waiting for transfers between devices: 21.2 us -> 14.7 us  [swap(): return lax.ppermute(value, 'tp', pairs)]
    pallas_call x4 -> x8, Pallas kernels: 8.82 us -> 12.7 us  [fetch(): pl.pallas_call(functools.partial(fetch_kernel, start, width), out_shape=[...]
  transfers between devices with their start and end apart: 21 -> 21, of which waited for: 14 -> 14; matrix products, arithmetic and copies ran while one was open for 0% -> 0% of each run, Pallas kernels for 16% -> 23%
where the time goes in v4:
time: 65.6 us; the launch traced here: 65.2 us
  starting transfers between devices  28.6 us (44%)
  Pallas kernels  20.8 us (32%)
  waiting for transfers between devices  14.7 us (22%)
  other arithmetic  0.82 us (1%)
    ppermute x21, starting transfers between devices, swap(): return lax.ppermute(value, 'tp', pairs)  28.6 us
    ppermute x21, waiting for transfers between devices, swap(): return lax.ppermute(value, 'tp', pairs)  14.7 us
    pallas_call x8, Pallas kernels, fetch(): pl.pallas_call(functools.partial(fetch_kernel, start, width), out_shape=[...  12.7 us
    pallas_call x1, Pallas kernels, language(): pl.pallas_call(functools.partial(language_kernel, bits), out_shape=[jax.S...  4.66 us
    pallas_call x1, Pallas kernels, stage(): pl.pallas_call(functools.partial(stage_kernel, count), out_shape=[pltpu.V...  1.82 us
  transfers between devices with their start and end apart: 21, of which 14 were waited for; matrix products, arithmetic and copies ran while one was open for 0% of the time, Pallas kernels for 23%

profile of v4, /device:TPU:0, one launch (start us, length us, event | category | flops | bytes accessed | tf_op | source)
XLA Modules:
  0.0 65.2 jit_solution(12218965263818617408)
XLA Ops:
  0.0 3.5 %collective-permute-start = (bf16[4,1280]{1,0:T(4,128)(2,1)}, bf16[4,1280]{1,0:T(4,128)(2,1)S(1)}, u32[]{:S(2)}, u32[]{:S(2)}) collective-permute-start(bf16[4,1280]{1,0:T(4,128)(2,1)} %refs_0_.1), channel_id=1, source_target_pairs={{0,9},{1,8},{2,11},{3,10},{4,13},{5,12},{6,15},{7,14},{8,1},{9,0},... | collective-permute-start | bytes 30728 | tf_op jit(solution)/shard_map/ppermute | solution.py:34
  3.5 0.0 collective-permute-start.2
  3.5 1.8 %shard_map.163 = (bf16[4,1280]{1,0:T(4,128)(2,1)S(1)}, bf16[4,4096]{1,0:T(4,128)(2,1)S(1)}, f32[1280]{0:T(1024)S(1)}, f32[1280]{0:T(1024)S(1)}, f32[1280]{0:T(10...) custom-call(bf16[4,1280]{1,0:T(4,128)(2,1)} %refs_0_.1, ...), custom_call_target="tpu_custom_call" | custom-call | tf_op jit(solution)/shard_map/pallas_call | solution.py:161
  5.3 0.0 collective-permute-done
  5.4 1.9 %collective-permute-start.1 = (bf16[8,1280]{1,0:T(8,128)(2,1)S(1)}, bf16[8,1280]{1,0:T(8,128)(2,1)S(1)}, u32[]{:S(2)}, u32[]{:S(2)}) collective-permute-start(bf16[8,1280]{1,0:T(8,128)(2,1)S(1)} %pad_maximum_fusion.2.carried.after), channel_id=1, source_target_pairs={{0,5},{1,4},{2,7},{3,6},{4,1},{5,0},{6,3},{7,2},{8,13},{9,12},{10,... | collective-permute-start | bytes 61448 | tf_op jit(solution)/shard_map/ppermute | solution.py:34
  7.3 1.4 %shard_map.164 = (bf16[688,4096]{1,0:T(8,128)(2,1)S(1)}, bf16[8,1280]{1,0:T(8,128)(2,1)S(1)}) custom-call(bf16[8,1280]{1,0:T(8,128)(2,1)S(1)} %pad_maximum_fusion.2.carried.after, bf16[8,1280]{1,0:T(8,128)(2,1)S(1)} %pad_maximum_fusion.2.carried.after, bf16[688,4096]{1,0:T(8,128)(2,1)} %bitcast.2), custom_call_target="tpu_custom_call" | custom-call | bytes 1409024 | tf_op jit(solution)/shard_map/pallas_call | solution.py:183
  8.7 0.2 collective-permute-done.1
  8.9 1.7 %collective-permute-start.3 = (bf16[16,1280]{1,0:T(8,128)(2,1)S(1)}, bf16[16,1280]{1,0:T(8,128)(2,1)S(1)}, u32[]{:S(2)}, u32[]{:S(2)}) collective-permute-start(bf16[16,1280]{1,0:T(8,128)(2,1)S(1)} %constant_dynamic-update-slice_fusion.carried), channel_id=1, source_target_pairs={{0,3},{1,2},{2,1},{3,0},{4,7},{5,6},{6,5},{7,4},{8,11},{9,10},{10,... | collective-permute-start | bytes 122888 | tf_op jit(solution)/shard_map/ppermute | solution.py:34
  10.6 0.0 collective-permute-done.2
  10.7 1.4 %shard_map.165 = (bf16[688,4096]{1,0:T(8,128)(2,1)S(1)}, bf16[16,1280]{1,0:T(8,128)(2,1)S(1)}) custom-call(bf16[16,1280]{1,0:T(8,128)(2,1)S(1)} %constant_dynamic-update-slice_fusion.carried, bf16[8,4096]{1,0:T(8,128)(2,1)S(1)} %pad_maximum_fusion.1.after, bf16[688,4096]{1,0:T(8,128)(2,1)} %bitcast.3, ...), custom_call_target="tpu_custom_call", output_to_operand_aliasing={{0}: (3, {})} | custom-call | bytes 1409024 | tf_op jit(solution)/shard_map/pallas_call | solution.py:183
  12.1 0.3 collective-permute-done.3
  12.3 0.4 collective-permute-start.4
  12.8 0.9 %collective-permute-done.4.others = bf16[32,1280]{1,0:T(8,128)(2,1)S(1)} collective-permute-done((bf16[32,1280]{1,0:T(8,128)(2,1)S(1)}, bf16[32,1280]{1,0:T(8,128)(2,1)S(1)}, u32[]{:S(2)}, u32[]{:S(2)}) %collective-permute-start.4) | collective-permute-done | bytes 81952 | tf_op jit(solution)/shard_map/ppermute | solution.py:34
  13.7 1.2 %shard_map.166 = (bf16[16,1280]{1,0:T(8,128)(2,1)S(1)}, f32[16,1280]{1,0:T(8,128)S(1)}, f32[16,1280]{1,0:T(8,128)S(1)}) custom-call(bf16[32,1280]{1,0:T(8,128)(2,1)S(1)} %constant_dynamic-update-slice_fusion.2.frames, bf16[32,1280]{1,0:T(8,128)(2,1)S(1)} %collective-permute-done.4.others, f32[1280]{0:T(1024)S(1)} %get-tuple-element.49.gain, ...), custom_call_target="tpu_custom_call" | custom-call | flops 104857600 | bytes 1638400 | tf_op jit(solution)/shard_map/pallas_call | solution.py:93
  14.9 0.4 collective-permute-start.5
  15.3 0.9 %collective-permute-done.5 = bf16[16,1280]{1,0:T(8,128)(2,1)S(1)} collective-permute-done((bf16[16,1280]{1,0:T(8,128)(2,1)S(1)}, bf16[16,1280]{1,0:T(8,128)(2,1)S(1)}, u32[]{:S(2)}, u32[]{:S(2)}) %collective-permute-start.5) | collective-permute-done | bytes 40992 | tf_op jit(solution)/shard_map/ppermute | solution.py:34
  16.2 1.8 %collective-permute-start.6 = (bf16[16,1280]{1,0:T(8,128)(2,1)S(1)}, bf16[16,1280]{1,0:T(8,128)(2,1)S(1)}, u32[]{:S(2)}, u32[]{:S(2)}) collective-permute-start(bf16[16,1280]{1,0:T(8,128)(2,1)S(1)} %get-tuple-element.58), channel_id=1, source_target_pairs={{0,5},{1,4},{2,7},{3,6},{4,1},{5,0},{6,3},{7,2},{8,13},{9,12},{10,... | collective-permute-start | bytes 122888 | tf_op jit(solution)/shard_map/ppermute | solution.py:34
  18.0 0.1 collective-permute-start.8
  18.0 1.6 %shard_map.167 = (bf16[688,4096]{1,0:T(8,128)(2,1)S(1)}, f32[16,1280]{1,0:T(8,128)S(1)}) custom-call(f32[16,1280]{1,0:T(8,128)S(1)} %get-tuple-element.88.carried.after, f32[16,1280]{1,0:T(8,128)S(1)} %get-tuple-element.88.carried.after, bf16[688,4096]{1,0:T(8,128)(2,1)} %bitcast.5), custom_call_target="tpu_custom_call" | custom-call | bytes 2113536 | tf_op jit(solution)/shard_map/pallas_call | solution.py:183
  19.7 0.3 collective-permute-done.6
  19.9 3.0 %collective-permute-start.7 = (bf16[16,1280]{1,0:T(8,128)(2,1)S(1)}, bf16[16,1280]{1,0:T(8,128)(2,1)S(1)}, u32[]{:S(2)}, u32[]{:S(2)}) collective-permute-start(bf16[16,1280]{1,0:T(8,128)(2,1)S(1)} %get-tuple-element.85), channel_id=1, source_target_pairs={{0,9},{1,8},{2,11},{3,10},{4,13},{5,12},{6,15},{7,14},{8,1},{9,0},... | collective-permute-start | bytes 122888 | tf_op jit(solution)/shard_map/ppermute | solution.py:34
  22.9 1.8 %shard_map.168 = (bf16[688,4096]{1,0:T(8,128)(2,1)S(1)}, f32[16,1280]{1,0:T(8,128)S(1)}) custom-call(f32[16,1280]{1,0:T(8,128)S(1)} %get-tuple-element.86.carried.after, f32[16,1280]{1,0:T(8,128)S(1)} %get-tuple-element.86.carried.after, bf16[688,4096]{1,0:T(8,128)(2,1)} %bitcast.4, ...), custom_call_target="tpu_custom_call", output_to_operand_aliasing={{0}: (3, {})} | custom-call | bytes 2818048 | tf_op jit(solution)/shard_map/pallas_call | solution.py:183
  24.7 0.0 collective-permute-done.8
  24.8 0.0 collective-permute-done.7
  24.8 1.6 %collective-permute-start.9 = (bf16[16,1280]{1,0:T(8,128)(2,1)S(1)}, bf16[16,1280]{1,0:T(8,128)(2,1)S(1)}, u32[]{:S(2)}, u32[]{:S(2)}) collective-permute-start(bf16[16,1280]{1,0:T(8,128)(2,1)S(1)} %get-tuple-element.64), channel_id=1, source_target_pairs={{0,3},{1,2},{2,1},{3,0},{4,7},{5,6},{6,5},{7,4},{8,11},{9,10},{10,... | collective-permute-start | bytes 122888 | tf_op jit(solution)/shard_map/ppermute | solution.py:34
  26.4 0.2 collective-permute-start.11
  26.6 1.6 %shard_map.169 = (bf16[688,4096]{1,0:T(8,128)(2,1)S(1)}, f32[16,1280]{1,0:T(8,128)S(1)}) custom-call(f32[16,1280]{1,0:T(8,128)S(1)} %get-tuple-element.84.carried.after, f32[16,1280]{1,0:T(8,128)S(1)} %get-tuple-element.84.carried.after, bf16[688,4096]{1,0:T(8,128)(2,1)} %bitcast.6, ...), custom_call_target="tpu_custom_call", output_to_operand_aliasing={{0}: (3, {})} | custom-call | bytes 2113536 | tf_op jit(solution)/shard_map/pallas_call | solution.py:183
  28.2 0.2 collective-permute-done.9.arrived
  28.4 0.2 shard_map.170.post
  28.6 0.4 collective-permute-start.10
  29.0 0.9 %collective-permute-done.10.other = bf16[16,1280]{1,0:T(8,128)(2,1)S(1)} collective-permute-done((bf16[16,1280]{1,0:T(8,128)(2,1)S(1)}, bf16[16,1280]{1,0:T(8,128)(2,1)S(1)}, u32[]{:S(2)}, u32[]{:S(2)}) %collective-permute-start.10) | collective-permute-done | bytes 40992 | tf_op jit(solution)/shard_map/ppermute | solution.py:34
  29.9 0.2 shard_map.171.carried
  30.1 2.8 %collective-permute-start.12 = (bf16[1,32,256]{2,1,0:T(8,128)(2,1)S(1)}, bf16[1,32,256]{2,1,0:T(8,128)(2,1)S(1)}, u32[]{:S(2)}, u32[]{:S(2)}) collective-permute-start(bf16[1,32,256]{2,1,0:T(8,128)(2,1)S(1)} %shard_map.171.carried), channel_id=1, source_target_pairs={{0,9},{1,8},{2,11},{3,10},{4,13},{5,12},{6,15},{7,14},{8,1},{9,0},... | collective-permute-start | bytes 49160 | tf_op jit(solution)/shard_map/ppermute | solution.py:34
  32.9 0.0 collective-permute-done.11
  32.9 0.4 collective-permute-start.16
  33.3 1.8 %shard_map.172 = (bf16[688,4096]{1,0:T(8,128)(2,1)S(1)}, bf16[1,32,256]{2,1,0:T(8,128)(2,1)S(1)}) custom-call(bf16[1,32,256]{2,1,0:T(8,128)(2,1)S(1)} %shard_map.171.carried, bf16[32,4096]{1,0:T(8,128)(2,1)S(1)} %constant_dynamic-update-slice_fusion.4.after.prompts, bf16[688,4096]{1,0:T(8,128)(2,1)} %source.3), custom_call_target="tpu_custom_call" | custom-call | bytes 2818048 | tf_op jit(solution)/shard_map/pallas_call | solution.py:183
  35.2 0.0 collective-permute-done.12
  35.2 2.0 %collective-permute-start.13 = (bf16[2,32,256]{2,1,0:T(8,128)(2,1)S(1)}, bf16[2,32,256]{2,1,0:T(8,128)(2,1)S(1)}, u32[]{:S(2)}, u32[]{:S(2)}) collective-permute-start(bf16[2,32,256]{2,1,0:T(8,128)(2,1)S(1)} %constant_dynamic-update-slice_fusion.6.carried.after), channel_id=1, source_target_pairs={{0,5},{1,4},{2,7},{3,6},{4,1},{5,0},{6,3},{7,2},{8,13},{9,12},{10,... | collective-permute-start | bytes 98312 | tf_op jit(solution)/shard_map/ppermute | solution.py:34
  37.1 1.4 %shard_map.173 = (bf16[688,4096]{1,0:T(8,128)(2,1)S(1)}, bf16[2,32,256]{2,1,0:T(8,128)(2,1)S(1)}) custom-call(bf16[2,32,256]{2,1,0:T(8,128)(2,1)S(1)} %constant_dynamic-update-slice_fusion.6.carried.after, bf16[2,32,256]{2,1,0:T(8,128)(2,1)S(1)} %constant_dynamic-update-slice_fusion.6.carried.after, ...), custom_call_target="tpu_custom_call", output_to_operand_aliasing={{0}: (3, {})} | custom-call | bytes 1409024 | tf_op jit(solution)/shard_map/pallas_call | solution.py:183
  38.5 0.2 collective-permute-done.13
  38.7 2.0 %collective-permute-start.14 = (bf16[4,32,256]{2,1,0:T(8,128)(2,1)S(1)}, bf16[4,32,256]{2,1,0:T(8,128)(2,1)S(1)}, u32[]{:S(2)}, u32[]{:S(2)}) collective-permute-start(bf16[4,32,256]{2,1,0:T(8,128)(2,1)S(1)} %constant_dynamic-update-slice_fusion.8.carried.after), channel_id=1, source_target_pairs={{0,3},{1,2},{2,1},{3,0},{4,7},{5,6},{6,5},{7,4},{8,11},{9,10},{10,... | collective-permute-start | bytes 196616 | tf_op jit(solution)/shard_map/ppermute | solution.py:34
  40.7 1.8 %shard_map.174 = (bf16[688,4096]{1,0:T(8,128)(2,1)S(1)}, bf16[4,32,256]{2,1,0:T(8,128)(2,1)S(1)}) custom-call(bf16[4,32,256]{2,1,0:T(8,128)(2,1)S(1)} %constant_dynamic-update-slice_fusion.8.carried.after, bf16[4,32,256]{2,1,0:T(8,128)(2,1)S(1)} %constant_dynamic-update-slice_fusion.8.carried.after, ...), custom_call_target="tpu_custom_call", output_to_operand_aliasing={{0}: (3, {})} | custom-call | bytes 2818048 | tf_op jit(solution)/shard_map/pallas_call | solution.py:183
  42.5 0.4 collective-permute-done.14
  42.9 0.3 collective-permute-start.15
  43.2 1.1 %collective-permute-done.15.far = bf16[8,32,256]{2,1,0:T(8,128)(2,1)S(1)} collective-permute-done((bf16[8,32,256]{2,1,0:T(8,128)(2,1)S(1)}, bf16[8,32,256]{2,1,0:T(8,128)(2,1)S(1)}, u32[]{:S(2)}, u32[]{:S(2)}) %collective-permute-start.15) | collective-permute-done | bytes 131104 | tf_op jit(solution)/shard_map/ppermute | solution.py:34
  44.2 0.0 collective-permute-done.16.others
  44.2 4.7 %shard_map.175 = (bf16[32,4096]{1,0:T(8,128)(2,1)S(1)}, f32[32,4096]{1,0:T(8,128)S(1)}) custom-call(bf16[8,32,256]{2,1,0:T(8,128)(2,1)S(1)} %constant_dynamic-update-slice_fusion.10.near, bf16[8,32,256]{2,1,0:T(8,128)(2,1)S(1)} %collective-permute-done.15.far, s32[64]{0:T(128)S(1)} %get-tuple-element.76.source, ...), custom_call_target="tpu_custom_call" | custom-call | flops 1082130432 | bytes 11272192 | tf_op jit(solution)/shard_map/pallas_call | solution.py:256
  48.9 0.3 collective-permute-start.17
  49.2 1.3 %collective-permute-done.17 = bf16[32,4096]{1,0:T(8,128)(2,1)S(1)} collective-permute-done((bf16[32,4096]{1,0:T(8,128)(2,1)S(1)}, bf16[32,4096]{1,0:T(8,128)(2,1)S(1)}, u32[]{:S(2)}, u32[]{:S(2)}) %collective-permute-start.17) | collective-permute-done | bytes 262176 | tf_op jit(solution)/shard_map/ppermute | solution.py:34
  50.6 2.0 %collective-permute-start.18 = (bf16[16,4096]{1,0:T(8,128)(2,1)S(1)}, bf16[16,4096]{1,0:T(8,128)(2,1)S(1)}, u32[]{:S(2)}, u32[]{:S(2)}) collective-permute-start(bf16[16,4096]{1,0:T(8,128)(2,1)S(1)} %slice.41), channel_id=1, source_target_pairs={{0,3},{1,2},{2,1},{3,0},{4,7},{5,6},{6,5},{7,4},{8,11},{9,10},{10,... | collective-permute-start | bytes 393224 | tf_op jit(solution)/shard_map/ppermute | solution.py:34
  52.6 3.6 %collective-permute-done.18 = bf16[16,4096]{1,0:T(8,128)(2,1)S(1)} collective-permute-done((bf16[16,4096]{1,0:T(8,128)(2,1)S(1)}, bf16[16,4096]{1,0:T(8,128)(2,1)S(1)}, u32[]{:S(2)}, u32[]{:S(2)}) %collective-permute-start.18) | collective-permute-done | bytes 131104 | tf_op jit(solution)/shard_map/ppermute | solution.py:34
  56.2 1.9 %collective-permute-start.19 = (bf16[8,4096]{1,0:T(8,128)(2,1)S(1)}, bf16[8,4096]{1,0:T(8,128)(2,1)S(1)}, u32[]{:S(2)}, u32[]{:S(2)}) collective-permute-start(bf16[8,4096]{1,0:T(8,128)(2,1)S(1)} %slice.42), channel_id=1, source_target_pairs={{0,5},{1,4},{2,7},{3,6},{4,1},{5,0},{6,3},{7,2},{8,13},{9,12},{10,... | collective-permute-start | bytes 196616 | tf_op jit(solution)/shard_map/ppermute | solution.py:34
  58.1 2.2 %collective-permute-done.19 = bf16[8,4096]{1,0:T(8,128)(2,1)S(1)} collective-permute-done((bf16[8,4096]{1,0:T(8,128)(2,1)S(1)}, bf16[8,4096]{1,0:T(8,128)(2,1)S(1)}, u32[]{:S(2)}, u32[]{:S(2)}) %collective-permute-start.19) | collective-permute-done | bytes 65568 | tf_op jit(solution)/shard_map/ppermute | solution.py:34
  60.3 1.9 %collective-permute-start.20 = (bf16[4,4096]{1,0:T(4,128)(2,1)S(1)}, bf16[4,4096]{1,0:T(4,128)(2,1)S(1)}, u32[]{:S(2)}, u32[]{:S(2)}) collective-permute-start(bf16[4,4096]{1,0:T(4,128)(2,1)S(1)} %slice.43), channel_id=1, source_target_pairs={{0,9},{1,8},{2,11},{3,10},{4,13},{5,12},{6,15},{7,14},{8,1},{9,0},... | collective-permute-start | bytes 98312 | tf_op jit(solution)/shard_map/ppermute | solution.py:34
  62.2 2.4 %collective-permute-done.20 = bf16[4,4096]{1,0:T(4,128)(2,1)S(1)} collective-permute-done((bf16[4,4096]{1,0:T(4,128)(2,1)S(1)}, bf16[4,4096]{1,0:T(4,128)(2,1)S(1)}, u32[]{:S(2)}, u32[]{:S(2)}) %collective-permute-start.20) | collective-permute-done | bytes 32800 | tf_op jit(solution)/shard_map/ppermute | solution.py:34
  64.6 0.6 fusion
  (24 shorter events, 0.3 us)
Async XLA Ops:
  0.0 5.3 %collective-permute-start = (bf16[4,1280]{1,0:T(4,128)(2,1)}, bf16[4,1280]{1,0:T(4,128)(2,1)S(1)}, u32[]{:S(2)}, u32[]{:S(2)}) collective-permute-start(bf16[4,1280]{1,0:T(4,128)(2,1)} %refs_0_.1), channel_id=1, source_target_pairs={{0,9},{1,8},{2,11},{3,10},{4,13},{5,12},{6,15},{7,14},{8,1},{9,0},... | collective-permute-start | bytes 30728 | tf_op jit(solution)/shard_map/ppermute | solution.py:34
  3.5 7.2 %collective-permute-start.2 = (bf16[4,4096]{1,0:T(4,128)(2,1)}, bf16[4,4096]{1,0:T(4,128)(2,1)S(1)}, u32[]{:S(2)}, u32[]{:S(2)}) collective-permute-start(bf16[4,4096]{1,0:T(4,128)(2,1)} %refs_1_.1), channel_id=1, source_target_pairs={{0,9},{1,8},{2,11},{3,10},{4,13},{5,12},{6,15},{7,14},{8,1},{9,0},... | collective-permute-start | bytes 98312 | tf_op jit(solution)/shard_map/ppermute | solution.py:34
  5.4 3.5 %collective-permute-start.1 = (bf16[8,1280]{1,0:T(8,128)(2,1)S(1)}, bf16[8,1280]{1,0:T(8,128)(2,1)S(1)}, u32[]{:S(2)}, u32[]{:S(2)}) collective-permute-start(bf16[8,1280]{1,0:T(8,128)(2,1)S(1)} %pad_maximum_fusion.2.carried.after), channel_id=1, source_target_pairs={{0,5},{1,4},{2,7},{3,6},{4,1},{5,0},{6,3},{7,2},{8,13},{9,12},{10,... | collective-permute-start | bytes 61448 | tf_op jit(solution)/shard_map/ppermute | solution.py:34
  8.9 3.4 %collective-permute-start.3 = (bf16[16,1280]{1,0:T(8,128)(2,1)S(1)}, bf16[16,1280]{1,0:T(8,128)(2,1)S(1)}, u32[]{:S(2)}, u32[]{:S(2)}) collective-permute-start(bf16[16,1280]{1,0:T(8,128)(2,1)S(1)} %constant_dynamic-update-slice_fusion.carried), channel_id=1, source_target_pairs={{0,3},{1,2},{2,1},{3,0},{4,7},{5,6},{6,5},{7,4},{8,11},{9,10},{10,... | collective-permute-start | bytes 122888 | tf_op jit(solution)/shard_map/ppermute | solution.py:34
  12.3 1.4 %collective-permute-start.4 = (bf16[32,1280]{1,0:T(8,128)(2,1)S(1)}, bf16[32,1280]{1,0:T(8,128)(2,1)S(1)}, u32[]{:S(2)}, u32[]{:S(2)}) collective-permute-start(bf16[32,1280]{1,0:T(8,128)(2,1)S(1)} %constant_dynamic-update-slice_fusion.2.frames), channel_id=1, source_target_pairs={{0,1},{1,0},{2,3},{3,2},{4,5},{5,4},{6,7},{7,6},{8,9},{9,8},{10,11... | collective-permute-start | bytes 245768 | tf_op jit(solution)/shard_map/ppermute | solution.py:34
  14.9 1.3 %collective-permute-start.5 = (bf16[16,1280]{1,0:T(8,128)(2,1)S(1)}, bf16[16,1280]{1,0:T(8,128)(2,1)S(1)}, u32[]{:S(2)}, u32[]{:S(2)}) collective-permute-start(bf16[16,1280]{1,0:T(8,128)(2,1)S(1)} %get-tuple-element.56), channel_id=1, source_target_pairs={{0,1},{1,0},{2,3},{3,2},{4,5},{5,4},{6,7},{7,6},{8,9},{9,8},{10,11... | collective-permute-start | bytes 122888 | tf_op jit(solution)/shard_map/ppermute | solution.py:34
  16.2 3.8 %collective-permute-start.6 = (bf16[16,1280]{1,0:T(8,128)(2,1)S(1)}, bf16[16,1280]{1,0:T(8,128)(2,1)S(1)}, u32[]{:S(2)}, u32[]{:S(2)}) collective-permute-start(bf16[16,1280]{1,0:T(8,128)(2,1)S(1)} %get-tuple-element.58), channel_id=1, source_target_pairs={{0,5},{1,4},{2,7},{3,6},{4,1},{5,0},{6,3},{7,2},{8,13},{9,12},{10,... | collective-permute-start | bytes 122888 | tf_op jit(solution)/shard_map/ppermute | solution.py:34
  18.0 6.8 %collective-permute-start.8 = (bf16[8,4096]{1,0:T(8,128)(2,1)S(1)}, bf16[8,4096]{1,0:T(8,128)(2,1)S(1)}, u32[]{:S(2)}, u32[]{:S(2)}) collective-permute-start(bf16[8,4096]{1,0:T(8,128)(2,1)S(1)} %pad_maximum_fusion.1.after), channel_id=1, source_target_pairs={{0,5},{1,4},{2,7},{3,6},{4,1},{5,0},{6,3},{7,2},{8,13},{9,12},{10,... | collective-permute-start | bytes 196616 | tf_op jit(solution)/shard_map/ppermute | solution.py:34
  19.9 4.8 %collective-permute-start.7 = (bf16[16,1280]{1,0:T(8,128)(2,1)S(1)}, bf16[16,1280]{1,0:T(8,128)(2,1)S(1)}, u32[]{:S(2)}, u32[]{:S(2)}) collective-permute-start(bf16[16,1280]{1,0:T(8,128)(2,1)S(1)} %get-tuple-element.85), channel_id=1, source_target_pairs={{0,9},{1,8},{2,11},{3,10},{4,13},{5,12},{6,15},{7,14},{8,1},{9,0},... | collective-permute-start | bytes 122888 | tf_op jit(solution)/shard_map/ppermute | solution.py:34
  24.8 3.6 %collective-permute-start.9 = (bf16[16,1280]{1,0:T(8,128)(2,1)S(1)}, bf16[16,1280]{1,0:T(8,128)(2,1)S(1)}, u32[]{:S(2)}, u32[]{:S(2)}) collective-permute-start(bf16[16,1280]{1,0:T(8,128)(2,1)S(1)} %get-tuple-element.64), channel_id=1, source_target_pairs={{0,3},{1,2},{2,1},{3,0},{4,7},{5,6},{6,5},{7,4},{8,11},{9,10},{10,... | collective-permute-start | bytes 122888 | tf_op jit(solution)/shard_map/ppermute | solution.py:34
  26.4 6.5 %collective-permute-start.11 = (bf16[16,4096]{1,0:T(8,128)(2,1)S(1)}, bf16[16,4096]{1,0:T(8,128)(2,1)S(1)}, u32[]{:S(2)}, u32[]{:S(2)}) collective-permute-start(bf16[16,4096]{1,0:T(8,128)(2,1)S(1)} %pad_maximum_fusion.after), channel_id=1, source_target_pairs={{0,3},{1,2},{2,1},{3,0},{4,7},{5,6},{6,5},{7,4},{8,11},{9,10},{10,... | collective-permute-start | bytes 393224 | tf_op jit(solution)/shard_map/ppermute | solution.py:34
  28.6 1.3 %collective-permute-start.10 = (bf16[16,1280]{1,0:T(8,128)(2,1)S(1)}, bf16[16,1280]{1,0:T(8,128)(2,1)S(1)}, u32[]{:S(2)}, u32[]{:S(2)}) collective-permute-start(bf16[16,1280]{1,0:T(8,128)(2,1)S(1)} %shard_map.170.post), channel_id=1, source_target_pairs={{0,1},{1,0},{2,3},{3,2},{4,5},{5,4},{6,7},{7,6},{8,9},{9,8},{10,11... | collective-permute-start | bytes 122888 | tf_op jit(solution)/shard_map/ppermute | solution.py:34
  30.1 5.1 %collective-permute-start.12 = (bf16[1,32,256]{2,1,0:T(8,128)(2,1)S(1)}, bf16[1,32,256]{2,1,0:T(8,128)(2,1)S(1)}, u32[]{:S(2)}, u32[]{:S(2)}) collective-permute-start(bf16[1,32,256]{2,1,0:T(8,128)(2,1)S(1)} %shard_map.171.carried), channel_id=1, source_target_pairs={{0,9},{1,8},{2,11},{3,10},{4,13},{5,12},{6,15},{7,14},{8,1},{9,0},... | collective-permute-start | bytes 49160 | tf_op jit(solution)/shard_map/ppermute | solution.py:34
  32.9 11.3 %collective-permute-start.16 = (bf16[32,4096]{1,0:T(8,128)(2,1)S(1)}, bf16[32,4096]{1,0:T(8,128)(2,1)S(1)}, u32[]{:S(2)}, u32[]{:S(2)}) collective-permute-start(bf16[32,4096]{1,0:T(8,128)(2,1)S(1)} %constant_dynamic-update-slice_fusion.4.after.prompts), channel_id=1, source_target_pairs={{0,1},{1,0},{2,3},{3,2},{4,5},{5,4},{6,7},{7,6},{8,9},{9,8},{10,11... | collective-permute-start | bytes 786440 | tf_op jit(solution)/shard_map/ppermute | solution.py:34
  35.2 3.6 %collective-permute-start.13 = (bf16[2,32,256]{2,1,0:T(8,128)(2,1)S(1)}, bf16[2,32,256]{2,1,0:T(8,128)(2,1)S(1)}, u32[]{:S(2)}, u32[]{:S(2)}) collective-permute-start(bf16[2,32,256]{2,1,0:T(8,128)(2,1)S(1)} %constant_dynamic-update-slice_fusion.6.carried.after), channel_id=1, source_target_pairs={{0,5},{1,4},{2,7},{3,6},{4,1},{5,0},{6,3},{7,2},{8,13},{9,12},{10,... | collective-permute-start | bytes 98312 | tf_op jit(solution)/shard_map/ppermute | solution.py:34
  38.7 4.1 %collective-permute-start.14 = (bf16[4,32,256]{2,1,0:T(8,128)(2,1)S(1)}, bf16[4,32,256]{2,1,0:T(8,128)(2,1)S(1)}, u32[]{:S(2)}, u32[]{:S(2)}) collective-permute-start(bf16[4,32,256]{2,1,0:T(8,128)(2,1)S(1)} %constant_dynamic-update-slice_fusion.8.carried.after), channel_id=1, source_target_pairs={{0,3},{1,2},{2,1},{3,0},{4,7},{5,6},{6,5},{7,4},{8,11},{9,10},{10,... | collective-permute-start | bytes 196616 | tf_op jit(solution)/shard_map/ppermute | solution.py:34
  42.9 1.3 %collective-permute-start.15 = (bf16[8,32,256]{2,1,0:T(8,128)(2,1)S(1)}, bf16[8,32,256]{2,1,0:T(8,128)(2,1)S(1)}, u32[]{:S(2)}, u32[]{:S(2)}) collective-permute-start(bf16[8,32,256]{2,1,0:T(8,128)(2,1)S(1)} %constant_dynamic-update-slice_fusion.10.near), channel_id=1, source_target_pairs={{0,1},{1,0},{2,3},{3,2},{4,5},{5,4},{6,7},{7,6},{8,9},{9,8},{10,11... | collective-permute-start | bytes 393224 | tf_op jit(solution)/shard_map/ppermute | solution.py:34
  48.9 1.6 %collective-permute-start.17 = (bf16[32,4096]{1,0:T(8,128)(2,1)S(1)}, bf16[32,4096]{1,0:T(8,128)(2,1)S(1)}, u32[]{:S(2)}, u32[]{:S(2)}) collective-permute-start(bf16[32,4096]{1,0:T(8,128)(2,1)S(1)} %get-tuple-element.82), channel_id=1, source_target_pairs={{0,1},{1,0},{2,3},{3,2},{4,5},{5,4},{6,7},{7,6},{8,9},{9,8},{10,11... | collective-permute-start | bytes 786440 | tf_op jit(solution)/shard_map/ppermute | solution.py:34
  50.6 5.6 %collective-permute-start.18 = (bf16[16,4096]{1,0:T(8,128)(2,1)S(1)}, bf16[16,4096]{1,0:T(8,128)(2,1)S(1)}, u32[]{:S(2)}, u32[]{:S(2)}) collective-permute-start(bf16[16,4096]{1,0:T(8,128)(2,1)S(1)} %slice.41), channel_id=1, source_target_pairs={{0,3},{1,2},{2,1},{3,0},{4,7},{5,6},{6,5},{7,4},{8,11},{9,10},{10,... | collective-permute-start | bytes 393224 | tf_op jit(solution)/shard_map/ppermute | solution.py:34
  56.2 4.0 %collective-permute-start.19 = (bf16[8,4096]{1,0:T(8,128)(2,1)S(1)}, bf16[8,4096]{1,0:T(8,128)(2,1)S(1)}, u32[]{:S(2)}, u32[]{:S(2)}) collective-permute-start(bf16[8,4096]{1,0:T(8,128)(2,1)S(1)} %slice.42), channel_id=1, source_target_pairs={{0,5},{1,4},{2,7},{3,6},{4,1},{5,0},{6,3},{7,2},{8,13},{9,12},{10,... | collective-permute-start | bytes 196616 | tf_op jit(solution)/shard_map/ppermute | solution.py:34
  60.3 4.3 %collective-permute-start.20 = (bf16[4,4096]{1,0:T(4,128)(2,1)S(1)}, bf16[4,4096]{1,0:T(4,128)(2,1)S(1)}, u32[]{:S(2)}, u32[]{:S(2)}) collective-permute-start(bf16[4,4096]{1,0:T(4,128)(2,1)S(1)} %slice.43), channel_id=1, source_target_pairs={{0,9},{1,8},{2,11},{3,10},{4,13},{5,12},{6,15},{7,14},{8,1},{9,0},... | collective-permute-start | bytes 98312 | tf_op jit(solution)/shard_map/ppermute | solution.py:34

commit v5 on v4

--- a/solution.py
+++ b/solution.py
@@ -55,55 +55,52 @@
     )
 
 
+def group_device(place, parity, bits):
+    return 2 * place + (parity ^ parity_of(place, bits))
+
+
 def encoder_kernel(
-    bits, frames, others, gain, shift, down_bias, bias, up, down, send, keep, base
+    bits, frames, gain, shift, down_bias, bias, bias_pair, up, up_pair, down, down_pair,
+    sums, base,
 ):
     me = lax.axis_index("tp")
-    first = frames.shape[0]
-    rows = 2 * first
+    rows = frames.shape[0]
     pooled = rows // 2
-    half = pooled // 2
-    own = rows >> bits
+    own = rows >> (bits - 1)
     out_row = lax.broadcasted_iota(jnp.int32, (rows, rows), 0)
     in_row = lax.broadcasted_iota(jnp.int32, (rows, rows), 1)
     frame = jnp.where(out_row < pooled, 2 * out_row, 2 * (out_row - pooled) + 1)
-    place = slot_of((frame // own) ^ me, bits) * own + frame % own
+    device = group_device(frame // own, parity_of(me, bits), bits)
+    place = slot_of(device ^ me, bits) * own + frame % own
     order = jnp.where(place == in_row, 1.0, 0.0).astype(jnp.bfloat16)
-    values = jnp.dot(
-        order, jnp.concatenate([frames[...], others[...]]), preferred_element_type=jnp.float32
-    )
+    values = jnp.dot(order, frames[...], preferred_element_type=jnp.float32)
     center = values - jnp.mean(values, axis=-1, keepdims=True)
     spread = jnp.mean(center * center, axis=-1, keepdims=True)
-    both = (values[:pooled] + values[pooled:]) * 0.5 + row(down_bias)
+    base[...] = (values[:pooled] + values[pooled:]) * 0.5 + row(down_bias)
     normed = (center * lax.rsqrt(spread + 1e-05) * row(gain) + row(shift)).astype(jnp.bfloat16)
-    pre_act = dot_last(normed, up[...]) + row(bias).astype(jnp.float32)
-    hidden = (0.5 * pre_act * (1.0 + lax.erf(pre_act * 0.7071067811865476))).astype(jnp.bfloat16)
-    result = jnp.dot(hidden, down[...], preferred_element_type=jnp.float32)
-    mine = (result[:pooled] + result[pooled:]) * 0.5
-    upper = parity_of(me, bits) == 1
-    keep[...] = jnp.where(upper, mine[half:], mine[:half])
-    send[...] = jnp.where(upper, mine[:half], mine[half:]).astype(jnp.bfloat16)
-    base[...] = jnp.where(upper, both[half:], both[:half])
-
-
-def encoder(halves, vectors, up, down, bits):
-    first, width = halves[0].shape
-    half = first // 2
+    result = 0.0
+    for weight, offset, back in ((up, bias, down), (up_pair, bias_pair, down_pair)):
+        pre_act = dot_last(normed, weight[...]) + row(offset).astype(jnp.float32)
+        hidden = 0.5 * pre_act * (1.0 + lax.erf(pre_act * 0.7071067811865476))
+        result += jnp.dot(
+            hidden.astype(jnp.bfloat16), back[...], preferred_element_type=jnp.float32
+        )
+    sums[...] = (result[:pooled] + result[pooled:]) * 0.5
+
+
+def encoder(frames, vectors, ups, downs, bits):
+    rows, width = frames.shape
     vmem = pl.BlockSpec(memory_space=pltpu.VMEM)
     return pl.pallas_call(
         functools.partial(encoder_kernel, bits),
-        out_shape=[
-            jax.ShapeDtypeStruct((half, width), jnp.bfloat16),
-            jax.ShapeDtypeStruct((half, width), jnp.float32),
-            jax.ShapeDtypeStruct((half, width), jnp.float32),
-        ],
-        in_specs=[vmem] * 8,
-        out_specs=[vmem] * 3,
+        out_shape=[jax.ShapeDtypeStruct((rows // 2, width), jnp.float32)] * 2,
+        in_specs=[vmem] * 10,
+        out_specs=[vmem] * 2,
         compiler_params=pltpu.CompilerParams(vmem_limit_bytes=8 * 2**20),
         cost_estimate=pl.CostEstimate(
-            flops=8 * first * up.size, bytes_accessed=4 * up.size, transcendentals=0
+            flops=8 * rows * ups[0].size, bytes_accessed=8 * ups[0].size, transcendentals=0
         ),
-    )(*halves, *vectors, up, down)
+    )(frames, *vectors, *ups, *downs)
 
 
 def post_kernel(total, arrived, base, gain, shift, after, post):
@@ -125,24 +122,23 @@
     )(total, arrived, base, gain, shift, after)
 
 
-def project_kernel(bits, post, other, weight, bias, out):
-    upper = parity_of(lax.axis_index("tp"), bits) == 1
-    low = jnp.where(upper, other[...], post[...])
-    high = jnp.where(upper, post[...], other[...])
-    every = jnp.concatenate([low, high])
-    result = jnp.dot(every, weight[...], preferred_element_type=jnp.float32) + row(bias)
-    out[0] = result.astype(out.dtype)
-
-
-def project(post, other, weight, bias, bits):
+def project_kernel(post, weight, weight_pair, bias, bias_pair, out):
+    for i, (shard, offset) in enumerate(((weight, bias), (weight_pair, bias_pair))):
+        result = jnp.dot(post[...], shard[...], preferred_element_type=jnp.float32)
+        out[0, i] = (result + row(offset)).astype(out.dtype)
+
+
+def project(post, weights, biases):
     vmem = pl.BlockSpec(memory_space=pltpu.VMEM)
     return pl.pallas_call(
-        functools.partial(project_kernel, bits),
-        out_shape=jax.ShapeDtypeStruct((1, 2 * post.shape[0], weight.shape[1]), jnp.bfloat16),
-        in_specs=[vmem] * 4,
+        project_kernel,
+        out_shape=jax.ShapeDtypeStruct(
+            (1, 2, post.shape[0], weights[0].shape[1]), jnp.bfloat16
+        ),
+        in_specs=[vmem] * 5,
         out_specs=vmem,
         compiler_params=pltpu.CompilerParams(vmem_limit_bytes=4 * 2**20),
-    )(post, other, weight, bias)
+    )(post, *weights, *biases)
 
 
 def stage_kernel(count, *refs):
@@ -206,8 +202,7 @@
     bits, near, far, source, prompts, others, gain, gate, up, down,
     send, keep, packed, normed,
 ):
-    count, audio, columns = near.shape
-    count = 2 * count
+    count, group, columns = 1 << bits, near.shape[2], near.shape[3]
     half, width = prompts.shape
     rows = 2 * half
     own = rows >> bits
@@ -216,7 +211,12 @@
     in_row = lax.broadcasted_iota(jnp.int32, (rows, rows), 1)
     place = (offset_of(out_row // own, bits) ^ me) * own + out_row % own
     order = jnp.where(place == in_row, 1.0, 0.0).astype(jnp.bfloat16)
-    wanted = lax.broadcasted_iota(jnp.int32, (audio, rows), 0)
+    parity = parity_of(me, bits)
+    audio = lax.broadcasted_iota(jnp.int32, (2 * group, rows), 0)
+    parities = jnp.where(audio < group, parity, 1 - parity)
+    audio = jnp.where(audio < group, audio, audio - group)
+    each = group >> (bits - 1)
+    wanted = group_device(audio // each, parities, bits) * each + audio % each
     chosen = jnp.where(row(source) == wanted, 1.0, 0.0).astype(jnp.bfloat16)
     pick = dot_last(order, chosen)
     audio_row = jnp.sum(pick, axis=1, keepdims=True) > 0.5
@@ -224,9 +224,10 @@
     squares = jnp.zeros((rows, columns), jnp.float32)
     for device in range(count):
         part = slice(device * columns, (device + 1) * columns)
-        slot = slot_of(me ^ device, bits)
-        place = slot & (count // 2 - 1)
-        piece = jnp.where(slot < count // 2, near[place], far[place])
+        differs = parity ^ parity_of(device, bits)
+        near_slot = slot_of(me ^ device ^ differs, bits)
+        far_slot = slot_of(me ^ device ^ differs, bits)
+        piece = jnp.concatenate([near[near_slot, differs], far[far_slot, 1 - differs]])
         found = jnp.dot(pick, piece, preferred_element_type=jnp.float32)
         prompt = jnp.concatenate([prompts[:, part], others[:, part]])
         value = jnp.where(audio_row, found, prompt.astype(jnp.float32))
@@ -375,6 +376,10 @@
     gate_rows, up_rows = gate_weight.T, up_weight.T
     arrived = swap(frames, bits - 1, count)
     prompts_arrived = swap(prompt_embeds, bits - 1, count)
+    up_pair, down_pair, bias_pair, proj_pair, proj_bias_pair = [
+        swap(value, 0, count)
+        for value in (enc_up, enc_down, enc_up_bias, proj_weight, proj_bias)
+    ]
     (
         block, prompts, enc_gain, enc_shift, enc_down_bias, enc_up_bias, enc_up, enc_down,
         post_gain, post_shift, proj_weight, proj_bias, rms_gain, slot_source,
@@ -393,16 +398,17 @@
             after = prompts if step else block
             gate, block = fetch(block, after, gate_rows, gate, step * part, part)
         block = jnp.concatenate([block, arrived])
-    send, total, base = encoder(
-        (block, swap(block, 0, count)),
-        (enc_gain, enc_shift, enc_down_bias, enc_up_bias),
-        enc_up,
-        enc_down,
+    total, base = encoder(
+        block,
+        (enc_gain, enc_shift, enc_down_bias, enc_up_bias, bias_pair),
+        (enc_up, up_pair),
+        (enc_down, down_pair),
         bits,
     )
-    arrived = swap(send, 0, count)
+    arrived = None
     for step, bit in enumerate((steps[1], steps[0], *steps[2:])):
-        total = total + arrived.astype(jnp.float32)
+        if arrived is not None:
+            total = total + arrived.astype(jnp.float32)
         outgoing = total.astype(jnp.bfloat16)
         if step != 1:
             outgoing, prompts = lax.optimization_barrier((outgoing, prompts))
@@ -415,14 +421,14 @@
         elif step < 3:
             up, total = fetch(total, total, up_rows, up, step // 2 * large, large)
     post = post_norm(total, arrived, base, post_gain, post_shift, early)
-    features = project(post, swap(post, 0, count), proj_weight, proj_bias, bits)
+    features = project(post, (proj_weight, proj_pair), (proj_bias, proj_bias_pair))
     for step, bit in enumerate(steps):
         arrived = swap(features, bit, count)
         if step == 1:
             left = width - 2 * large
             up, features = fetch(features, features, up_rows, up, 2 * large, left)
         elif step < 3:
-            after = features if step else prompts
+            after = prompts if step else features
             down, features = fetch(features, after, down_weight, down, step * part, 2 * part)
         features = jnp.concatenate([features, arrived])
     features = features, swap(features, 0, count)

time: 65.6 us -> 62.7 us (0.956)
  starting transfers between devices: 28.6 us -> 26.5 us
  waiting for transfers between devices: 14.7 us -> 13.5 us
    ppermute x21 -> x23, starting transfers between devices: 28.6 us -> 26.5 us  [swap(): return lax.ppermute(value, 'tp', pairs)]
    ppermute x21 -> x23, waiting for transfers between devices: 14.7 us -> 13.5 us  [swap(): return lax.ppermute(value, 'tp', pairs)]
  transfers between devices with their start and end apart: 21 -> 23, of which waited for: 14 -> 12; matrix products, arithmetic and copies ran while one was open for 0% -> 0% of each run, Pallas kernels for 23% -> 24%
where the time goes in v5:
time: 62.7 us; the launch traced here: 62.3 us
  starting transfers between devices  26.5 us (42%)
  Pallas kernels  21 us (33%)
  waiting for transfers between devices  13.5 us (22%)
  other arithmetic  0.85 us (1%)
    ppermute x23, starting transfers between devices, swap(): return lax.ppermute(value, 'tp', pairs)  26.5 us
    ppermute x23, waiting for transfers between devices, swap(): return lax.ppermute(value, 'tp', pairs)  13.5 us
    pallas_call x8, Pallas kernels, fetch(): pl.pallas_call(functools.partial(fetch_kernel, start, width), out_shape=[...  12.8 us
    pallas_call x1, Pallas kernels, language(): pl.pallas_call(functools.partial(language_kernel, bits), out_shape=[jax.S...  4.65 us
    pallas_call x1, Pallas kernels, stage(): pl.pallas_call(functools.partial(stage_kernel, count), out_shape=[pltpu.V...  1.82 us
  transfers between devices with their start and end apart: 23, of which 12 were waited for; matrix products, arithmetic and copies ran while one was open for 0% of the time, Pallas kernels for 24%

profile of v5, /device:TPU:0, one launch (start us, length us, event | category | flops | bytes accessed | tf_op | source)
XLA Modules:
  0.0 62.3 jit_solution(1146157228242925449)
XLA Ops:
  0.0 3.5 %collective-permute-start = (bf16[4,1280]{1,0:T(4,128)(2,1)}, bf16[4,1280]{1,0:T(4,128)(2,1)S(1)}, u32[]{:S(2)}, u32[]{:S(2)}) collective-permute-start(bf16[4,1280]{1,0:T(4,128)(2,1)} %refs_0_.1), channel_id=1, source_target_pairs={{0,9},{1,8},{2,11},{3,10},{4,13},{5,12},{6,15},{7,14},{8,1},{9,0},... | collective-permute-start | bytes 30728 | tf_op jit(solution)/shard_map/ppermute | solution.py:34
  3.5 0.0 collective-permute-start.2
  3.5 0.7 %collective-permute-start.5 = (bf16[320,1280]{1,0:T(8,128)(2,1)}, bf16[320,1280]{1,0:T(8,128)(2,1)S(1)}, u32[]{:S(2)}, u32[]{:S(2)}) collective-permute-start(bf16[320,1280]{1,0:T(8,128)(2,1)} %refs_6_.1), channel_id=1, source_target_pairs={{0,1},{1,0},{2,3},{3,2},{4,5},{5,4},{6,7},{7,6},{8,9},{9,8},{10,11... | collective-permute-start | bytes 2457608 | tf_op jit(solution)/shard_map/ppermute | solution.py:34
  4.2 0.0 collective-permute-start.6
  4.2 0.5 collective-permute-start.4
  4.7 1.8 %shard_map.163 = (bf16[4,1280]{1,0:T(4,128)(2,1)S(1)}, bf16[4,4096]{1,0:T(4,128)(2,1)S(1)}, f32[1280]{0:T(1024)S(1)}, f32[1280]{0:T(1024)S(1)}, f32[1280]{0:T(10...) custom-call(bf16[4,1280]{1,0:T(4,128)(2,1)} %refs_0_.1, ...), custom_call_target="tpu_custom_call" | custom-call | tf_op jit(solution)/shard_map/pallas_call | solution.py:157
  6.5 0.0 collective-permute-done
  6.6 1.7 %collective-permute-start.1 = (bf16[8,1280]{1,0:T(8,128)(2,1)S(1)}, bf16[8,1280]{1,0:T(8,128)(2,1)S(1)}, u32[]{:S(2)}, u32[]{:S(2)}) collective-permute-start(bf16[8,1280]{1,0:T(8,128)(2,1)S(1)} %pad_maximum_fusion.3.carried.after), channel_id=1, source_target_pairs={{0,5},{1,4},{2,7},{3,6},{4,1},{5,0},{6,3},{7,2},{8,13},{9,12},{10,... | collective-permute-start | bytes 61448 | tf_op jit(solution)/shard_map/ppermute | solution.py:34
  8.2 1.4 %shard_map.164 = (bf16[688,4096]{1,0:T(8,128)(2,1)S(1)}, bf16[8,1280]{1,0:T(8,128)(2,1)S(1)}) custom-call(bf16[8,1280]{1,0:T(8,128)(2,1)S(1)} %pad_maximum_fusion.3.carried.after, bf16[8,1280]{1,0:T(8,128)(2,1)S(1)} %pad_maximum_fusion.3.carried.after, bf16[688,4096]{1,0:T(8,128)(2,1)} %bitcast.2), custom_call_target="tpu_custom_call" | custom-call | bytes 1409024 | tf_op jit(solution)/shard_map/pallas_call | solution.py:179
  9.6 0.2 collective-permute-done.1
  9.9 1.5 %collective-permute-start.3 = (bf16[16,1280]{1,0:T(8,128)(2,1)S(1)}, bf16[16,1280]{1,0:T(8,128)(2,1)S(1)}, u32[]{:S(2)}, u32[]{:S(2)}) collective-permute-start(bf16[16,1280]{1,0:T(8,128)(2,1)S(1)} %constant_dynamic-update-slice_fusion.carried), channel_id=1, source_target_pairs={{0,3},{1,2},{2,1},{3,0},{4,7},{5,6},{6,5},{7,4},{8,11},{9,10},{10,... | collective-permute-start | bytes 122888 | tf_op jit(solution)/shard_map/ppermute | solution.py:34
  11.4 0.0 collective-permute-done.2
  11.4 0.0 copy-start
  11.5 0.0 copy-start.1
  11.5 1.4 %shard_map.165 = (bf16[688,4096]{1,0:T(8,128)(2,1)S(1)}, bf16[16,1280]{1,0:T(8,128)(2,1)S(1)}) custom-call(bf16[16,1280]{1,0:T(8,128)(2,1)S(1)} %constant_dynamic-update-slice_fusion.carried, bf16[8,4096]{1,0:T(8,128)(2,1)S(1)} %pad_maximum_fusion.2.after, bf16[688,4096]{1,0:T(8,128)(2,1)} %bitcast.3, ...), custom_call_target="tpu_custom_call", output_to_operand_aliasing={{0}: (3, {})} | custom-call | bytes 1409024 | tf_op jit(solution)/shard_map/pallas_call | solution.py:179
  12.9 0.5 collective-permute-done.3
  13.4 0.0 collective-permute-done.4.bias_pair
  13.4 0.0 collective-permute-done.5.up_pair
  13.5 0.0 collective-permute-done.6.down_pair
  13.5 1.3 %shard_map.166 = (f32[16,1280]{1,0:T(8,128)S(1)}, f32[16,1280]{1,0:T(8,128)S(1)}) custom-call(bf16[32,1280]{1,0:T(8,128)(2,1)S(1)} %pad_maximum_fusion.1.frames, f32[1280]{0:T(1024)S(1)} %get-tuple-element.48.gain, f32[1280]{0:T(1024)S(1)} %get-tuple-element.49.shift, f32[1280]{0:T(1024)S(1)} %get-tuple-element.50.down_bias, ...), custom_call_target="tpu_custom_call" | custom-call | flops 104857600 | bytes 3276800 | tf_op jit(solution)/shard_map/pallas_call | solution.py:94
  14.8 1.5 %collective-permute-start.7 = (bf16[16,1280]{1,0:T(8,128)(2,1)S(1)}, bf16[16,1280]{1,0:T(8,128)(2,1)S(1)}, u32[]{:S(2)}, u32[]{:S(2)}) collective-permute-start(bf16[16,1280]{1,0:T(8,128)(2,1)S(1)} %convert_element_type.33), channel_id=1, source_target_pairs={{0,5},{1,4},{2,7},{3,6},{4,1},{5,0},{6,3},{7,2},{8,13},{9,12},{10,... | collective-permute-start | bytes 122888 | tf_op jit(solution)/shard_map/ppermute | solution.py:34
  16.3 0.0 copy-done
  16.3 0.1 collective-permute-start.11
  16.3 0.0 copy-done.1
  16.3 0.4 collective-permute-start.12
  16.8 0.3 collective-permute-start.9
  17.1 1.6 %shard_map.167 = (bf16[688,4096]{1,0:T(8,128)(2,1)S(1)}, f32[16,1280]{1,0:T(8,128)S(1)}) custom-call(f32[16,1280]{1,0:T(8,128)S(1)} %get-tuple-element.54.carried.after, f32[16,1280]{1,0:T(8,128)S(1)} %get-tuple-element.54.carried.after, bf16[688,4096]{1,0:T(8,128)(2,1)} %bitcast.5), custom_call_target="tpu_custom_call" | custom-call | bytes 2113536 | tf_op jit(solution)/shard_map/pallas_call | solution.py:179
  18.7 0.0 collective-permute-done.7
  18.8 2.5 %collective-permute-start.8 = (bf16[16,1280]{1,0:T(8,128)(2,1)S(1)}, bf16[16,1280]{1,0:T(8,128)(2,1)S(1)}, u32[]{:S(2)}, u32[]{:S(2)}) collective-permute-start(bf16[16,1280]{1,0:T(8,128)(2,1)S(1)} %get-tuple-element.83), channel_id=1, source_target_pairs={{0,9},{1,8},{2,11},{3,10},{4,13},{5,12},{6,15},{7,14},{8,1},{9,0},... | collective-permute-start | bytes 122888 | tf_op jit(solution)/shard_map/ppermute | solution.py:34
  21.2 1.8 %shard_map.168 = (bf16[688,4096]{1,0:T(8,128)(2,1)S(1)}, f32[16,1280]{1,0:T(8,128)S(1)}) custom-call(f32[16,1280]{1,0:T(8,128)S(1)} %get-tuple-element.84.carried.after, f32[16,1280]{1,0:T(8,128)S(1)} %get-tuple-element.84.carried.after, bf16[688,4096]{1,0:T(8,128)(2,1)} %bitcast.4, ...), custom_call_target="tpu_custom_call", output_to_operand_aliasing={{0}: (3, {})} | custom-call | bytes 2818048 | tf_op jit(solution)/shard_map/pallas_call | solution.py:179
  23.0 0.0 collective-permute-done.9
  23.1 0.3 collective-permute-done.8
  23.3 1.3 %collective-permute-start.10 = (bf16[16,1280]{1,0:T(8,128)(2,1)S(1)}, bf16[16,1280]{1,0:T(8,128)(2,1)S(1)}, u32[]{:S(2)}, u32[]{:S(2)}) collective-permute-start(bf16[16,1280]{1,0:T(8,128)(2,1)S(1)} %get-tuple-element.62), channel_id=1, source_target_pairs={{0,3},{1,2},{2,1},{3,0},{4,7},{5,6},{6,5},{7,4},{8,11},{9,10},{10,... | collective-permute-start | bytes 122888 | tf_op jit(solution)/shard_map/ppermute | solution.py:34
  24.6 0.7 %collective-permute-start.15 = (bf16[16,4096]{1,0:T(8,128)(2,1)S(1)}, bf16[16,4096]{1,0:T(8,128)(2,1)S(1)}, u32[]{:S(2)}, u32[]{:S(2)}) collective-permute-start(bf16[16,4096]{1,0:T(8,128)(2,1)S(1)} %pad_maximum_fusion.after), channel_id=1, source_target_pairs={{0,3},{1,2},{2,1},{3,0},{4,7},{5,6},{6,5},{7,4},{8,11},{9,10},{10,... | collective-permute-start | bytes 393224 | tf_op jit(solution)/shard_map/ppermute | solution.py:34
  25.3 1.6 %shard_map.169 = (bf16[688,4096]{1,0:T(8,128)(2,1)S(1)}, f32[16,1280]{1,0:T(8,128)S(1)}) custom-call(f32[16,1280]{1,0:T(8,128)S(1)} %get-tuple-element.82.carried.after, f32[16,1280]{1,0:T(8,128)S(1)} %get-tuple-element.82.carried.after, bf16[688,4096]{1,0:T(8,128)(2,1)} %bitcast.6, ...), custom_call_target="tpu_custom_call", output_to_operand_aliasing={{0}: (3, {})} | custom-call | bytes 2113536 | tf_op jit(solution)/shard_map/pallas_call | solution.py:179
  26.9 0.1 collective-permute-done.10.arrived
  27.0 0.2 shard_map.170.post
  27.2 0.0 collective-permute-done.12.bias_pair
  27.2 0.0 collective-permute-done.11.weight_pair
  27.2 0.3 shard_map.171.carried.after
  27.5 2.1 %collective-permute-start.13 = (bf16[1,2,16,256]{3,2,1,0:T(8,128)(2,1)S(1)}, bf16[1,2,16,256]{3,2,1,0:T(8,128)(2,1)S(1)}, u32[]{:S(2)}, u32[]{:S(2)}) collective-permute-start(bf16[1,2,16,256]{3,2,1,0:T(8,128)(2,1)S(1)} %shard_map.171.carried.after), channel_id=1, source_target_pairs={{0,9},{1,8},{2,11},{3,10},{4,13},{5,12},{6,15},{7,14},{8,1},{9,0},... | collective-permute-start | bytes 49160 | tf_op jit(solution)/shard_map/ppermute | solution.py:34
  29.6 1.8 %shard_map.172 = (bf16[688,4096]{1,0:T(8,128)(2,1)S(1)}, bf16[1,2,16,256]{3,2,1,0:T(8,128)(2,1)S(1)}) custom-call(bf16[1,2,16,256]{3,2,1,0:T(8,128)(2,1)S(1)} %shard_map.171.carried.after, bf16[1,2,16,256]{3,2,1,0:T(8,128)(2,1)S(1)} %shard_map.171.carried.after, bf16[688,4096]{1,0:T(8,128)(2,1)} %source.3), custom_call_target="tpu_custom_call" | custom-call | bytes 2818048 | tf_op jit(solution)/shard_map/pallas_call | solution.py:179
  31.4 0.1 collective-permute-done.13
  31.6 2.3 %collective-permute-start.14 = (bf16[2,2,16,256]{3,2,1,0:T(8,128)(2,1)S(1)}, bf16[2,2,16,256]{3,2,1,0:T(8,128)(2,1)S(1)}, u32[]{:S(2)}, u32[]{:S(2)}) collective-permute-start(bf16[2,2,16,256]{3,2,1,0:T(8,128)(2,1)S(1)} %constant_dynamic-update-slice_fusion.2.carried.after), channel_id=1, source_target_pairs={{0,5},{1,4},{2,7},{3,6},{4,1},{5,0},{6,3},{7,2},{8,13},{9,12},{10,... | collective-permute-start | bytes 98312 | tf_op jit(solution)/shard_map/ppermute | solution.py:34
  33.9 1.4 %shard_map.173 = (bf16[688,4096]{1,0:T(8,128)(2,1)S(1)}, bf16[2,2,16,256]{3,2,1,0:T(8,128)(2,1)S(1)}) custom-call(bf16[2,2,16,256]{3,2,1,0:T(8,128)(2,1)S(1)} %constant_dynamic-update-slice_fusion.2.carried.after, bf16[2,2,16,256]{3,2,1,0:T(8,128)(2,1)S(1)} %constant_dynamic-update-slice_fusion.2.carried.after, ...), custom_call_target="tpu_custom_call", output_to_operand_aliasing={{0}: (3, {})} | custom-call | bytes 1409024 | tf_op jit(solution)/shard_map/pallas_call | solution.py:179
  35.3 0.3 collective-permute-done.14
  35.6 1.8 %collective-permute-start.16 = (bf16[4,2,16,256]{3,2,1,0:T(8,128)(2,1)S(1)}, bf16[4,2,16,256]{3,2,1,0:T(8,128)(2,1)S(1)}, u32[]{:S(2)}, u32[]{:S(2)}) collective-permute-start(bf16[4,2,16,256]{3,2,1,0:T(8,128)(2,1)S(1)} %constant_dynamic-update-slice_fusion.4.carried), channel_id=1, source_target_pairs={{0,3},{1,2},{2,1},{3,0},{4,7},{5,6},{6,5},{7,4},{8,11},{9,10},{10,... | collective-permute-start | bytes 196616 | tf_op jit(solution)/shard_map/ppermute | solution.py:34
  37.3 0.0 collective-permute-done.15
  37.3 0.1 collective-permute-start.18
  37.4 1.8 %shard_map.174 = (bf16[688,4096]{1,0:T(8,128)(2,1)S(1)}, bf16[4,2,16,256]{3,2,1,0:T(8,128)(2,1)S(1)}) custom-call(bf16[4,2,16,256]{3,2,1,0:T(8,128)(2,1)S(1)} %constant_dynamic-update-slice_fusion.4.carried, bf16[32,4096]{1,0:T(8,128)(2,1)S(1)} %constant_dynamic-update-slice_fusion.6.after.prompts, ...), custom_call_target="tpu_custom_call", output_to_operand_aliasing={{0}: (3, {})} | custom-call | bytes 2818048 | tf_op jit(solution)/shard_map/pallas_call | solution.py:179
  39.3 0.5 collective-permute-done.16
  39.7 0.1 collective-permute-start.17
  39.9 1.2 %collective-permute-done.17.far = bf16[8,2,16,256]{3,2,1,0:T(8,128)(2,1)S(1)} collective-permute-done((bf16[8,2,16,256]{3,2,1,0:T(8,128)(2,1)S(1)}, bf16[8,2,16,256]{3,2,1,0:T(8,128)(2,1)S(1)}, u32[]{:S(2)}, u32[]{:S(2)}) %collective-permute-start.17) | collective-permute-done | bytes 131104 | tf_op jit(solution)/shard_map/ppermute | solution.py:34
  41.1 0.0 collective-permute-done.18.others
  41.1 4.6 %shard_map.175 = (bf16[32,4096]{1,0:T(8,128)(2,1)S(1)}, f32[32,4096]{1,0:T(8,128)S(1)}) custom-call(bf16[8,2,16,256]{3,2,1,0:T(8,128)(2,1)S(1)} %constant_dynamic-update-slice_fusion.8.near, bf16[8,2,16,256]{3,2,1,0:T(8,128)(2,1)S(1)} %collective-permute-done.17.far, s32[64]{0:T(128)S(1)} %get-tuple-element.74.source, ...), custom_call_target="tpu_custom_call" | custom-call | flops 1082130432 | bytes 11272192 | tf_op jit(solution)/shard_map/pallas_call | solution.py:257
  45.7 0.2 collective-permute-start.19
  45.9 1.4 %collective-permute-done.19 = bf16[32,4096]{1,0:T(8,128)(2,1)S(1)} collective-permute-done((bf16[32,4096]{1,0:T(8,128)(2,1)S(1)}, bf16[32,4096]{1,0:T(8,128)(2,1)S(1)}, u32[]{:S(2)}, u32[]{:S(2)}) %collective-permute-start.19) | collective-permute-done | bytes 262176 | tf_op jit(solution)/shard_map/ppermute | solution.py:34
  47.4 1.4 %collective-permute-start.20 = (bf16[16,4096]{1,0:T(8,128)(2,1)S(1)}, bf16[16,4096]{1,0:T(8,128)(2,1)S(1)}, u32[]{:S(2)}, u32[]{:S(2)}) collective-permute-start(bf16[16,4096]{1,0:T(8,128)(2,1)S(1)} %slice.41), channel_id=1, source_target_pairs={{0,3},{1,2},{2,1},{3,0},{4,7},{5,6},{6,5},{7,4},{8,11},{9,10},{10,... | collective-permute-start | bytes 393224 | tf_op jit(solution)/shard_map/ppermute | solution.py:34
  48.8 4.2 %collective-permute-done.20 = bf16[16,4096]{1,0:T(8,128)(2,1)S(1)} collective-permute-done((bf16[16,4096]{1,0:T(8,128)(2,1)S(1)}, bf16[16,4096]{1,0:T(8,128)(2,1)S(1)}, u32[]{:S(2)}, u32[]{:S(2)}) %collective-permute-start.20) | collective-permute-done | bytes 131104 | tf_op jit(solution)/shard_map/ppermute | solution.py:34
  53.0 1.9 %collective-permute-start.21 = (bf16[8,4096]{1,0:T(8,128)(2,1)S(1)}, bf16[8,4096]{1,0:T(8,128)(2,1)S(1)}, u32[]{:S(2)}, u32[]{:S(2)}) collective-permute-start(bf16[8,4096]{1,0:T(8,128)(2,1)S(1)} %slice.42), channel_id=1, source_target_pairs={{0,5},{1,4},{2,7},{3,6},{4,1},{5,0},{6,3},{7,2},{8,13},{9,12},{10,... | collective-permute-start | bytes 196616 | tf_op jit(solution)/shard_map/ppermute | solution.py:34
  54.9 2.3 %collective-permute-done.21 = bf16[8,4096]{1,0:T(8,128)(2,1)S(1)} collective-permute-done((bf16[8,4096]{1,0:T(8,128)(2,1)S(1)}, bf16[8,4096]{1,0:T(8,128)(2,1)S(1)}, u32[]{:S(2)}, u32[]{:S(2)}) %collective-permute-start.21) | collective-permute-done | bytes 65568 | tf_op jit(solution)/shard_map/ppermute | solution.py:34
  57.3 1.9 %collective-permute-start.22 = (bf16[4,4096]{1,0:T(4,128)(2,1)S(1)}, bf16[4,4096]{1,0:T(4,128)(2,1)S(1)}, u32[]{:S(2)}, u32[]{:S(2)}) collective-permute-start(bf16[4,4096]{1,0:T(4,128)(2,1)S(1)} %slice.43), channel_id=1, source_target_pairs={{0,9},{1,8},{2,11},{3,10},{4,13},{5,12},{6,15},{7,14},{8,1},{9,0},... | collective-permute-start | bytes 98312 | tf_op jit(solution)/shard_map/ppermute | solution.py:34
  59.2 2.4 %collective-permute-done.22 = bf16[4,4096]{1,0:T(4,128)(2,1)S(1)} collective-permute-done((bf16[4,4096]{1,0:T(4,128)(2,1)S(1)}, bf16[4,4096]{1,0:T(4,128)(2,1)S(1)}, u32[]{:S(2)}, u32[]{:S(2)}) %collective-permute-start.22) | collective-permute-done | bytes 32800 | tf_op jit(solution)/shard_map/ppermute | solution.py:34
  61.6 0.6 %fusion = bf16[4,4096]{1,0:T(4,128)(2,1)} fusion(f32[8,4096]{1,0:T(8,128)S(1)} %slice_add_fusion.1, bf16[4,4096]{1,0:T(4,128)(2,1)S(1)} %collective-permute-done.22), kind=kLoop, calls=%fused_computation.11 | loop fusion | flops 49152 | bytes 131072 | tf_op jit(solution)/shard_map/convert_element_type | solution.py:442
  (23 shorter events, 0.3 us)
Async XLA Ops:
  0.0 6.5 %collective-permute-start = (bf16[4,1280]{1,0:T(4,128)(2,1)}, bf16[4,1280]{1,0:T(4,128)(2,1)S(1)}, u32[]{:S(2)}, u32[]{:S(2)}) collective-permute-start(bf16[4,1280]{1,0:T(4,128)(2,1)} %refs_0_.1), channel_id=1, source_target_pairs={{0,9},{1,8},{2,11},{3,10},{4,13},{5,12},{6,15},{7,14},{8,1},{9,0},... | collective-permute-start | bytes 30728 | tf_op jit(solution)/shard_map/ppermute | solution.py:34
  3.5 7.9 %collective-permute-start.2 = (bf16[4,4096]{1,0:T(4,128)(2,1)}, bf16[4,4096]{1,0:T(4,128)(2,1)S(1)}, u32[]{:S(2)}, u32[]{:S(2)}) collective-permute-start(bf16[4,4096]{1,0:T(4,128)(2,1)} %refs_1_.1), channel_id=1, source_target_pairs={{0,9},{1,8},{2,11},{3,10},{4,13},{5,12},{6,15},{7,14},{8,1},{9,0},... | collective-permute-start | bytes 98312 | tf_op jit(solution)/shard_map/ppermute | solution.py:34
  3.5 9.9 %collective-permute-start.5 = (bf16[320,1280]{1,0:T(8,128)(2,1)}, bf16[320,1280]{1,0:T(8,128)(2,1)S(1)}, u32[]{:S(2)}, u32[]{:S(2)}) collective-permute-start(bf16[320,1280]{1,0:T(8,128)(2,1)} %refs_6_.1), channel_id=1, source_target_pairs={{0,1},{1,0},{2,3},{3,2},{4,5},{5,4},{6,7},{7,6},{8,9},{9,8},{10,11... | collective-permute-start | bytes 2457608 | tf_op jit(solution)/shard_map/ppermute | solution.py:34
  4.2 9.3 %collective-permute-start.6 = (bf16[320,1280]{1,0:T(8,128)(2,1)}, bf16[320,1280]{1,0:T(8,128)(2,1)S(1)}, u32[]{:S(2)}, u32[]{:S(2)}) collective-permute-start(bf16[320,1280]{1,0:T(8,128)(2,1)} %refs_7_.1), channel_id=1, source_target_pairs={{0,1},{1,0},{2,3},{3,2},{4,5},{5,4},{6,7},{7,6},{8,9},{9,8},{10,11... | collective-permute-start | bytes 2457608 | tf_op jit(solution)/shard_map/ppermute | solution.py:34
  4.2 9.3 %collective-permute-start.4 = (bf16[320]{0:T(512)(128)(2,1)}, bf16[320]{0:T(512)(128)(2,1)S(1)}, u32[]{:S(2)}, u32[]{:S(2)}) collective-permute-start(bf16[320]{0:T(512)(128)(2,1)} %refs_5_.1), channel_id=1, source_target_pairs={{0,1},{1,0},{2,3},{3,2},{4,5},{5,4},{6,7},{7,6},{8,9},{9,8},{10,11... | collective-permute-start | bytes 1928 | tf_op jit(solution)/shard_map/ppermute | solution.py:34
  6.6 3.3 %collective-permute-start.1 = (bf16[8,1280]{1,0:T(8,128)(2,1)S(1)}, bf16[8,1280]{1,0:T(8,128)(2,1)S(1)}, u32[]{:S(2)}, u32[]{:S(2)}) collective-permute-start(bf16[8,1280]{1,0:T(8,128)(2,1)S(1)} %pad_maximum_fusion.3.carried.after), channel_id=1, source_target_pairs={{0,5},{1,4},{2,7},{3,6},{4,1},{5,0},{6,3},{7,2},{8,13},{9,12},{10,... | collective-permute-start | bytes 61448 | tf_op jit(solution)/shard_map/ppermute | solution.py:34
  9.9 3.6 %collective-permute-start.3 = (bf16[16,1280]{1,0:T(8,128)(2,1)S(1)}, bf16[16,1280]{1,0:T(8,128)(2,1)S(1)}, u32[]{:S(2)}, u32[]{:S(2)}) collective-permute-start(bf16[16,1280]{1,0:T(8,128)(2,1)S(1)} %constant_dynamic-update-slice_fusion.carried), channel_id=1, source_target_pairs={{0,3},{1,2},{2,1},{3,0},{4,7},{5,6},{6,5},{7,4},{8,11},{9,10},{10,... | collective-permute-start | bytes 122888 | tf_op jit(solution)/shard_map/ppermute | solution.py:34
  11.4 4.8 %copy-start = (bf16[1280,256]{1,0:T(8,128)(2,1)S(1)}, bf16[1280,256]{1,0:T(8,128)(2,1)}, u32[]{:S(2)}) copy-start(bf16[1280,256]{1,0:T(8,128)(2,1)} %refs_10_.1) | copy-start | bytes 1966084
  11.5 4.9 %copy-start.1 = (f32[256]{0:T(256)S(1)}, f32[256]{0:T(256)}, u32[]{:S(2)}) copy-start(f32[256]{0:T(256)} %refs_11_.1) | copy-start | bytes 3076
  14.8 4.0 %collective-permute-start.7 = (bf16[16,1280]{1,0:T(8,128)(2,1)S(1)}, bf16[16,1280]{1,0:T(8,128)(2,1)S(1)}, u32[]{:S(2)}, u32[]{:S(2)}) collective-permute-start(bf16[16,1280]{1,0:T(8,128)(2,1)S(1)} %convert_element_type.33), channel_id=1, source_target_pairs={{0,5},{1,4},{2,7},{3,6},{4,1},{5,0},{6,3},{7,2},{8,13},{9,12},{10,... | collective-permute-start | bytes 122888 | tf_op jit(solution)/shard_map/ppermute | solution.py:34
  16.3 10.9 %collective-permute-start.11 = (bf16[1280,256]{1,0:T(8,128)(2,1)S(1)}, bf16[1280,256]{1,0:T(8,128)(2,1)S(1)}, u32[]{:S(2)}, u32[]{:S(2)}) collective-permute-start(bf16[1280,256]{1,0:T(8,128)(2,1)S(1)} %copy-done), channel_id=1, source_target_pairs={{0,1},{1,0},{2,3},{3,2},{4,5},{5,4},{6,7},{7,6},{8,9},{9,8},{10,11... | collective-permute-start | bytes 1966088 | tf_op jit(solution)/shard_map/ppermute | solution.py:34
  16.3 10.8 %collective-permute-start.12 = (f32[256]{0:T(256)S(1)}, f32[256]{0:T(256)S(1)}, u32[]{:S(2)}, u32[]{:S(2)}) collective-permute-start(f32[256]{0:T(256)S(1)} %copy-done.1), channel_id=1, source_target_pairs={{0,1},{1,0},{2,3},{3,2},{4,5},{5,4},{6,7},{7,6},{8,9},{9,8},{10,11... | collective-permute-start | bytes 3080 | tf_op jit(solution)/shard_map/ppermute | solution.py:34
  16.8 6.3 %collective-permute-start.9 = (bf16[8,4096]{1,0:T(8,128)(2,1)S(1)}, bf16[8,4096]{1,0:T(8,128)(2,1)S(1)}, u32[]{:S(2)}, u32[]{:S(2)}) collective-permute-start(bf16[8,4096]{1,0:T(8,128)(2,1)S(1)} %pad_maximum_fusion.2.after), channel_id=1, source_target_pairs={{0,5},{1,4},{2,7},{3,6},{4,1},{5,0},{6,3},{7,2},{8,13},{9,12},{10,... | collective-permute-start | bytes 196616 | tf_op jit(solution)/shard_map/ppermute | solution.py:34
  18.8 4.6 %collective-permute-start.8 = (bf16[16,1280]{1,0:T(8,128)(2,1)S(1)}, bf16[16,1280]{1,0:T(8,128)(2,1)S(1)}, u32[]{:S(2)}, u32[]{:S(2)}) collective-permute-start(bf16[16,1280]{1,0:T(8,128)(2,1)S(1)} %get-tuple-element.83), channel_id=1, source_target_pairs={{0,9},{1,8},{2,11},{3,10},{4,13},{5,12},{6,15},{7,14},{8,1},{9,0},... | collective-permute-start | bytes 122888 | tf_op jit(solution)/shard_map/ppermute | solution.py:34
  23.3 3.6 %collective-permute-start.10 = (bf16[16,1280]{1,0:T(8,128)(2,1)S(1)}, bf16[16,1280]{1,0:T(8,128)(2,1)S(1)}, u32[]{:S(2)}, u32[]{:S(2)}) collective-permute-start(bf16[16,1280]{1,0:T(8,128)(2,1)S(1)} %get-tuple-element.62), channel_id=1, source_target_pairs={{0,3},{1,2},{2,1},{3,0},{4,7},{5,6},{6,5},{7,4},{8,11},{9,10},{10,... | collective-permute-start | bytes 122888 | tf_op jit(solution)/shard_map/ppermute | solution.py:34
  24.6 12.7 %collective-permute-start.15 = (bf16[16,4096]{1,0:T(8,128)(2,1)S(1)}, bf16[16,4096]{1,0:T(8,128)(2,1)S(1)}, u32[]{:S(2)}, u32[]{:S(2)}) collective-permute-start(bf16[16,4096]{1,0:T(8,128)(2,1)S(1)} %pad_maximum_fusion.after), channel_id=1, source_target_pairs={{0,3},{1,2},{2,1},{3,0},{4,7},{5,6},{6,5},{7,4},{8,11},{9,10},{10,... | collective-permute-start | bytes 393224 | tf_op jit(solution)/shard_map/ppermute | solution.py:34
  27.5 4.1 %collective-permute-start.13 = (bf16[1,2,16,256]{3,2,1,0:T(8,128)(2,1)S(1)}, bf16[1,2,16,256]{3,2,1,0:T(8,128)(2,1)S(1)}, u32[]{:S(2)}, u32[]{:S(2)}) collective-permute-start(bf16[1,2,16,256]{3,2,1,0:T(8,128)(2,1)S(1)} %shard_map.171.carried.after), channel_id=1, source_target_pairs={{0,9},{1,8},{2,11},{3,10},{4,13},{5,12},{6,15},{7,14},{8,1},{9,0},... | collective-permute-start | bytes 49160 | tf_op jit(solution)/shard_map/ppermute | solution.py:34
  31.6 4.0 %collective-permute-start.14 = (bf16[2,2,16,256]{3,2,1,0:T(8,128)(2,1)S(1)}, bf16[2,2,16,256]{3,2,1,0:T(8,128)(2,1)S(1)}, u32[]{:S(2)}, u32[]{:S(2)}) collective-permute-start(bf16[2,2,16,256]{3,2,1,0:T(8,128)(2,1)S(1)} %constant_dynamic-update-slice_fusion.2.carried.after), channel_id=1, source_target_pairs={{0,5},{1,4},{2,7},{3,6},{4,1},{5,0},{6,3},{7,2},{8,13},{9,12},{10,... | collective-permute-start | bytes 98312 | tf_op jit(solution)/shard_map/ppermute | solution.py:34
  35.6 4.2 %collective-permute-start.16 = (bf16[4,2,16,256]{3,2,1,0:T(8,128)(2,1)S(1)}, bf16[4,2,16,256]{3,2,1,0:T(8,128)(2,1)S(1)}, u32[]{:S(2)}, u32[]{:S(2)}) collective-permute-start(bf16[4,2,16,256]{3,2,1,0:T(8,128)(2,1)S(1)} %constant_dynamic-update-slice_fusion.4.carried), channel_id=1, source_target_pairs={{0,3},{1,2},{2,1},{3,0},{4,7},{5,6},{6,5},{7,4},{8,11},{9,10},{10,... | collective-permute-start | bytes 196616 | tf_op jit(solution)/shard_map/ppermute | solution.py:34
  37.3 3.7 %collective-permute-start.18 = (bf16[32,4096]{1,0:T(8,128)(2,1)S(1)}, bf16[32,4096]{1,0:T(8,128)(2,1)S(1)}, u32[]{:S(2)}, u32[]{:S(2)}) collective-permute-start(bf16[32,4096]{1,0:T(8,128)(2,1)S(1)} %constant_dynamic-update-slice_fusion.6.after.prompts), channel_id=1, source_target_pairs={{0,1},{1,0},{2,3},{3,2},{4,5},{5,4},{6,7},{7,6},{8,9},{9,8},{10,11... | collective-permute-start | bytes 786440 | tf_op jit(solution)/shard_map/ppermute | solution.py:34
  39.7 1.3 %collective-permute-start.17 = (bf16[8,2,16,256]{3,2,1,0:T(8,128)(2,1)S(1)}, bf16[8,2,16,256]{3,2,1,0:T(8,128)(2,1)S(1)}, u32[]{:S(2)}, u32[]{:S(2)}) collective-permute-start(bf16[8,2,16,256]{3,2,1,0:T(8,128)(2,1)S(1)} %constant_dynamic-update-slice_fusion.8.near), channel_id=1, source_target_pairs={{0,1},{1,0},{2,3},{3,2},{4,5},{5,4},{6,7},{7,6},{8,9},{9,8},{10,11... | collective-permute-start | bytes 393224 | tf_op jit(solution)/shard_map/ppermute | solution.py:34
  45.7 1.6 %collective-permute-start.19 = (bf16[32,4096]{1,0:T(8,128)(2,1)S(1)}, bf16[32,4096]{1,0:T(8,128)(2,1)S(1)}, u32[]{:S(2)}, u32[]{:S(2)}) collective-permute-start(bf16[32,4096]{1,0:T(8,128)(2,1)S(1)} %get-tuple-element.80), channel_id=1, source_target_pairs={{0,1},{1,0},{2,3},{3,2},{4,5},{5,4},{6,7},{7,6},{8,9},{9,8},{10,11... | collective-permute-start | bytes 786440 | tf_op jit(solution)/shard_map/ppermute | solution.py:34
  47.4 5.5 %collective-permute-start.20 = (bf16[16,4096]{1,0:T(8,128)(2,1)S(1)}, bf16[16,4096]{1,0:T(8,128)(2,1)S(1)}, u32[]{:S(2)}, u32[]{:S(2)}) collective-permute-start(bf16[16,4096]{1,0:T(8,128)(2,1)S(1)} %slice.41), channel_id=1, source_target_pairs={{0,3},{1,2},{2,1},{3,0},{4,7},{5,6},{6,5},{7,4},{8,11},{9,10},{10,... | collective-permute-start | bytes 393224 | tf_op jit(solution)/shard_map/ppermute | solution.py:34
  53.0 4.3 %collective-permute-start.21 = (bf16[8,4096]{1,0:T(8,128)(2,1)S(1)}, bf16[8,4096]{1,0:T(8,128)(2,1)S(1)}, u32[]{:S(2)}, u32[]{:S(2)}) collective-permute-start(bf16[8,4096]{1,0:T(8,128)(2,1)S(1)} %slice.42), channel_id=1, source_target_pairs={{0,5},{1,4},{2,7},{3,6},{4,1},{5,0},{6,3},{7,2},{8,13},{9,12},{10,... | collective-permute-start | bytes 196616 | tf_op jit(solution)/shard_map/ppermute | solution.py:34
  57.3 4.3 %collective-permute-start.22 = (bf16[4,4096]{1,0:T(4,128)(2,1)S(1)}, bf16[4,4096]{1,0:T(4,128)(2,1)S(1)}, u32[]{:S(2)}, u32[]{:S(2)}) collective-permute-start(bf16[4,4096]{1,0:T(4,128)(2,1)S(1)} %slice.43), channel_id=1, source_target_pairs={{0,9},{1,8},{2,11},{3,10},{4,13},{5,12},{6,15},{7,14},{8,1},{9,0},... | collective-permute-start | bytes 98312 | tf_op jit(solution)/shard_map/ppermute | solution.py:34

commit v6 on v5

--- a/solution.py
+++ b/solution.py
@@ -141,27 +141,38 @@
     )(post, *weights, *biases)
 
 
-def stage_kernel(count, *refs):
-    sems = refs[2 * count]
+def stage_kernel(count, extra, carry, *refs):
+    sources, sems = refs[:count], refs[-1]
+    targets = refs[count + extra + carry :][:count]
     copies = [
-        pltpu.make_async_copy(refs[i], refs[count + i], sems.at[i]) for i in range(count)
+        pltpu.make_async_copy(source, target, sems.at[i])
+        for i, (source, target) in enumerate(zip(sources, targets))
     ]
     for copy in copies:
         copy.start()
+    if carry:
+        refs[-2][...] = refs[count][...]
     for copy in copies:
         copy.wait()
 
 
-def stage(*values):
-    count = len(values)
+def stage(values, *carried, after=()):
+    count, carry = len(values), len(carried)
+    vmem = pl.BlockSpec(memory_space=pltpu.VMEM)
     return pl.pallas_call(
-        functools.partial(stage_kernel, count),
-        out_shape=[pltpu.VMEM(value.shape, value.dtype) for value in values],
-        in_specs=[pl.BlockSpec(memory_space=pltpu.HBM)] * count,
-        out_specs=[pl.BlockSpec(memory_space=pltpu.VMEM)] * count,
+        functools.partial(stage_kernel, count, len(after), carry),
+        out_shape=[pltpu.VMEM(value.shape, value.dtype) for value in values]
+        + [jax.ShapeDtypeStruct(value.shape, value.dtype) for value in carried],
+        in_specs=[pl.BlockSpec(memory_space=pltpu.HBM)] * count
+        + [vmem] * carry
+        + [pl.BlockSpec(memory_space=pl.ANY)] * len(after),
+        out_specs=[vmem] * (count + carry),
         scratch_shapes=[pltpu.SemaphoreType.DMA((count,))],
         compiler_params=pltpu.CompilerParams(vmem_limit_bytes=2 * 2**20),
-    )(*[in_hbm(value) for value in values])
+        cost_estimate=pl.CostEstimate(
+            flops=0, bytes_accessed=2 * sum(value.size for value in values), transcendentals=0
+        ),
+    )(*[in_hbm(value) for value in values], *carried, *after)
 
 
 def fetch_kernel(start, width, carried, after, source, *refs):
@@ -199,11 +210,14 @@
 
 
 def language_kernel(
-    bits, near, far, source, prompts, others, gain, gate, up, down,
-    send, keep, packed, normed,
+    bits, near, far, source, prompts, others, gain, gate, up, down, down_hbm,
+    send, keep, packed, normed, rest, sem,
 ):
     count, group, columns = 1 << bits, near.shape[2], near.shape[3]
     half, width = prompts.shape
+    cut = width // 2
+    copy = pltpu.make_async_copy(down_hbm.at[:, pl.ds(cut, cut)], rest, sem)
+    copy.start()
     rows = 2 * half
     own = rows >> bits
     me = lax.axis_index("tp")
@@ -244,14 +258,20 @@
     pieces = 4
     for piece in range(pieces):
         part = slice(piece * width // pieces, (piece + 1) * width // pieces)
-        result = jnp.dot(hidden, down[:, part], preferred_element_type=jnp.float32)
+        if part.start == cut:
+            copy.wait()
+        if part.start < cut:
+            weight = down[:, part]
+        else:
+            weight = rest[:, part.start - cut : part.stop - cut]
+        result = jnp.dot(hidden, weight, preferred_element_type=jnp.float32)
         send[:, part] = result[half:].astype(jnp.bfloat16)
         keep[:, part] = result[:half] + jnp.where(
             held, packed[:half, part].astype(jnp.float32), 0.0
         )
 
 
-def language(features, source, prompts, gain, gate, up, down, bits):
+def language(features, source, prompts, gain, gate, up, down, down_weight, bits):
     half, width = prompts[0].shape
     vmem = pl.BlockSpec(memory_space=pltpu.VMEM)
     return pl.pallas_call(
@@ -260,14 +280,15 @@
             jax.ShapeDtypeStruct((half, width), jnp.bfloat16),
             jax.ShapeDtypeStruct((half, width), jnp.float32),
         ],
-        in_specs=[vmem] * 9,
+        in_specs=[vmem] * 9 + [pl.BlockSpec(memory_space=pltpu.HBM)],
         out_specs=[vmem] * 2,
-        scratch_shapes=[pltpu.VMEM((2 * half, width), jnp.bfloat16)] * 2,
+        scratch_shapes=[pltpu.VMEM((2 * half, width), jnp.bfloat16)] * 2
+        + [pltpu.VMEM((down.shape[0], width // 2), down.dtype), pltpu.SemaphoreType.DMA],
         compiler_params=pltpu.CompilerParams(vmem_limit_bytes=12 * 2**20),
         cost_estimate=pl.CostEstimate(
             flops=12 * half * up.size, bytes_accessed=4 * up.size, transcendentals=0
         ),
-    )(*features, source, *prompts, gain, gate, up, down)
+    )(*features, source, *prompts, gain, gate, up, down, in_hbm(down_weight))
 
 
 def layer_norm(values, gain, shift):
@@ -380,13 +401,7 @@
         swap(value, 0, count)
         for value in (enc_up, enc_down, enc_up_bias, proj_weight, proj_bias)
     ]
-    (
-        block, prompts, enc_gain, enc_shift, enc_down_bias, enc_up_bias, enc_up, enc_down,
-        post_gain, post_shift, proj_weight, proj_bias, rms_gain, slot_source,
-    ) = stage(
-        frames, prompt_embeds, enc_gain, enc_shift, enc_down_bias, enc_up_bias, enc_up, enc_down,
-        post_gain, post_shift, proj_weight, proj_bias, rms_gain, slot_source,
-    )
+    block, prompts, enc_gain, enc_shift = stage((frames, prompt_embeds, enc_gain, enc_shift))
     gate = up = down = None
     part = width // 4
     large = width // 2 - width // 8
@@ -394,9 +409,20 @@
     prompts = jnp.concatenate([prompts, prompts_arrived])
     for step, bit in enumerate(steps[1:]):
         arrived = swap(block, bit, count)
-        if step < 2:
-            after = prompts if step else block
-            gate, block = fetch(block, after, gate_rows, gate, step * part, part)
+        if step == 0:
+            gate, block = fetch(block, block, gate_rows, gate, 0, part)
+        elif step == 1:
+            (
+                enc_down_bias, enc_up_bias, enc_up, enc_down,
+                post_gain, post_shift, proj_weight, proj_bias, rms_gain, slot_source, block,
+            ) = stage(
+                (
+                    enc_down_bias, enc_up_bias, enc_up, enc_down,
+                    post_gain, post_shift, proj_weight, proj_bias, rms_gain, slot_source,
+                ),
+                block,
+                after=(prompts, proj_pair, proj_bias_pair),
+            )
         block = jnp.concatenate([block, arrived])
     total, base = encoder(
         block,
@@ -427,13 +453,14 @@
         if step == 1:
             left = width - 2 * large
             up, features = fetch(features, features, up_rows, up, 2 * large, left)
-        elif step < 3:
-            after = prompts if step else features
-            down, features = fetch(features, after, down_weight, down, step * part, 2 * part)
+        elif step == 0:
+            down, features = fetch(features, features, down_weight, down, 0, 2 * part)
+        elif step == 2:
+            gate, features = fetch(features, prompts, gate_rows, gate, part, part)
         features = jnp.concatenate([features, arrived])
     features = features, swap(features, 0, count)
     prompts = prompts, swap(prompts, 0, count)
-    send, total = language(features, slot_source, prompts, rms_gain, gate, up, down, bits)
+    send, total = language(features, slot_source, prompts, rms_gain, gate, up, down, down_weight, bits)
     total = total + swap(send, 0, count).astype(jnp.float32)
     for bit in range(1, bits):
         half = total.shape[0] // 2

time: 62.7 us -> 62.5 us (level)
  starting transfers between devices: 26.5 us -> 28.2 us
  Pallas kernels: 21 us -> 20 us
  waiting for transfers between devices: 13.5 us -> 12.7 us
    pallas_call x8 -> x7, Pallas kernels: 12.8 us -> 10.9 us  [fetch(): pl.pallas_call(functools.partial(fetch_kernel, start, width), out_shape=[...]
    ppermute x23, starting transfers between devices: 26.5 us -> 28.2 us  [swap(): return lax.ppermute(value, 'tp', pairs)]
    ppermute x23, waiting for transfers between devices: 13.5 us -> 12.7 us  [swap(): return lax.ppermute(value, 'tp', pairs)]
    pallas_call x1 -> x2, Pallas kernels: 1.82 us -> 2.55 us  [stage(): pl.pallas_call(functools.partial(stage_kernel, count, len(after), carry),...]
  transfers between devices with their start and end apart: 23 -> 23, of which waited for: 12 -> 9; matrix products, arithmetic and copies ran while one was open for 0% -> 0% of each run, Pallas kernels for 24% -> 22%
where the time goes in v6:
time: 62.5 us; the launch traced here: 62.1 us
  starting transfers between devices  28.2 us (45%)
  Pallas kernels  20 us (32%)
  waiting for transfers between devices  12.7 us (20%)
  other arithmetic  0.84 us (1%)
    ppermute x23, starting transfers between devices, swap(): return lax.ppermute(value, 'tp', pairs)  28.2 us
    ppermute x23, waiting for transfers between devices, swap(): return lax.ppermute(value, 'tp', pairs)  12.7 us
    pallas_call x7, Pallas kernels, fetch(): pl.pallas_call(functools.partial(fetch_kernel, start, width), out_shape=[...  10.9 us
    pallas_call x1, Pallas kernels, language(): pl.pallas_call(functools.partial(language_kernel, bits), out_shape=[jax.S...  4.79 us
    pallas_call x2, Pallas kernels, stage(): pl.pallas_call(functools.partial(stage_kernel, count, len(after), carry),...  2.55 us
    pallas_call x1, Pallas kernels, encoder(): pl.pallas_call(functools.partial(encoder_kernel, bits), out_shape=[jax.Sh...  1.25 us
  transfers between devices with their start and end apart: 23, of which 9 were waited for; matrix products, arithmetic and copies ran while one was open for 0% of the time, Pallas kernels for 22%

profile of v6, /device:TPU:0, one launch (start us, length us, event | category | flops | bytes accessed | tf_op | source)
XLA Modules:
  0.0 62.1 jit_solution(18101145187630129594)
XLA Ops:
  0.0 0.0 copy-start
  0.0 0.0 copy-start.1
  0.0 3.5 %collective-permute-start = (bf16[4,1280]{1,0:T(4,128)(2,1)}, bf16[4,1280]{1,0:T(4,128)(2,1)S(1)}, u32[]{:S(2)}, u32[]{:S(2)}) collective-permute-start(bf16[4,1280]{1,0:T(4,128)(2,1)} %refs_0_.2), channel_id=1, source_target_pairs={{0,9},{1,8},{2,11},{3,10},{4,13},{5,12},{6,15},{7,14},{8,1},{9,0},... | collective-permute-start | bytes 30728 | tf_op jit(solution)/shard_map/ppermute | solution.py:34
  3.5 0.1 collective-permute-start.2
  3.6 0.7 %collective-permute-start.3 = (bf16[1280,256]{1,0:T(8,128)(2,1)}, bf16[1280,256]{1,0:T(8,128)(2,1)S(1)}, u32[]{:S(2)}, u32[]{:S(2)}) collective-permute-start(bf16[1280,256]{1,0:T(8,128)(2,1)} %refs_6_.1), channel_id=1, source_target_pairs={{0,1},{1,0},{2,3},{3,2},{4,5},{5,4},{6,7},{7,6},{8,9},{9,8},{10,11... | collective-permute-start | bytes 1966088 | tf_op jit(solution)/shard_map/ppermute | solution.py:34
  4.2 0.0 collective-permute-start.4
  4.2 0.5 collective-permute-start.7
  4.7 0.8 %shard_map.163 = (bf16[4,1280]{1,0:T(4,128)(2,1)S(1)}, bf16[4,4096]{1,0:T(4,128)(2,1)S(1)}, f32[1280]{0:T(1024)S(1)}, f32[1280]{0:T(1024)S(1)}) custom-call(bf16[4,1280]{1,0:T(4,128)(2,1)} %refs_0_.2, bf16[4,4096]{1,0:T(4,128)(2,1)} %refs_1_.2, f32[1280]{0:T(1024)} %refs_2_.2, f32[1280]{0:T(1024)} %refs_3_.2), custom_call_target="tpu_custom_call" | custom-call | bytes 48128 | tf_op jit(solution)/shard_map/pallas_call | solution.py:162
  5.6 0.0 collective-permute-done
  5.6 1.6 %collective-permute-start.1 = (bf16[8,1280]{1,0:T(8,128)(2,1)S(1)}, bf16[8,1280]{1,0:T(8,128)(2,1)S(1)}, u32[]{:S(2)}, u32[]{:S(2)}) collective-permute-start(bf16[8,1280]{1,0:T(8,128)(2,1)S(1)} %pad_maximum_fusion.3.carried.after), channel_id=1, source_target_pairs={{0,5},{1,4},{2,7},{3,6},{4,1},{5,0},{6,3},{7,2},{8,13},{9,12},{10,... | collective-permute-start | bytes 61448 | tf_op jit(solution)/shard_map/ppermute | solution.py:34
  7.2 1.4 %shard_map.164 = (bf16[688,4096]{1,0:T(8,128)(2,1)S(1)}, bf16[8,1280]{1,0:T(8,128)(2,1)S(1)}) custom-call(bf16[8,1280]{1,0:T(8,128)(2,1)S(1)} %pad_maximum_fusion.3.carried.after, bf16[8,1280]{1,0:T(8,128)(2,1)S(1)} %pad_maximum_fusion.3.carried.after, bf16[688,4096]{1,0:T(8,128)(2,1)} %bitcast.5), custom_call_target="tpu_custom_call" | custom-call | bytes 1409024 | tf_op jit(solution)/shard_map/pallas_call | solution.py:190
  8.6 0.3 collective-permute-done.1
  8.9 0.0 copy-done
  8.9 0.2 collective-permute-start.8
  9.1 0.0 collective-permute-done.2
  9.1 1.5 %collective-permute-start.5 = (bf16[16,1280]{1,0:T(8,128)(2,1)S(1)}, bf16[16,1280]{1,0:T(8,128)(2,1)S(1)}, u32[]{:S(2)}, u32[]{:S(2)}) collective-permute-start(bf16[16,1280]{1,0:T(8,128)(2,1)S(1)} %constant_dynamic-update-slice_fusion.refs_10_), channel_id=1, source_target_pairs={{0,3},{1,2},{2,1},{3,0},{4,7},{5,6},{6,5},{7,4},{8,11},{9,10},{10,... | collective-permute-start | bytes 122888 | tf_op jit(solution)/shard_map/ppermute | solution.py:34
  10.6 0.0 collective-permute-done.4.refs_13_.bias_pair
  10.6 0.0 copy-done.1
  10.7 0.4 collective-permute-start.6
  11.0 0.0 collective-permute-done.3.refs_12_.weight_pair
  11.0 1.7 %shard_map.165 = (f32[1280]{0:T(1024)S(1)}, bf16[320]{0:T(512)(128)(2,1)S(1)}, bf16[320,1280]{1,0:T(8,128)(2,1)S(1)}, bf16[320,1280]{1,0:T(8,128)(2,1)S(1)}, f32...) custom-call(f32[1280]{0:T(1024)} %refs_0_.3, ...), custom_call_target="tpu_custom_call" | custom-call | bytes 2310912 | tf_op jit(solution)/shard_map/pallas_call | solution.py:162
  12.8 0.0 collective-permute-done.5
  12.8 0.0 collective-permute-done.6.bias_pair
  12.8 0.0 collective-permute-done.7.up_pair
  12.8 0.0 collective-permute-done.8.down_pair
  12.8 1.2 %shard_map.166 = (f32[16,1280]{1,0:T(8,128)S(1)}, f32[16,1280]{1,0:T(8,128)S(1)}) custom-call(bf16[32,1280]{1,0:T(8,128)(2,1)S(1)} %pad_maximum_fusion.1.frames, f32[1280]{0:T(1024)S(1)} %get-tuple-element.46.gain, f32[1280]{0:T(1024)S(1)} %get-tuple-element.47.shift, f32[1280]{0:T(1024)S(1)} %get-tuple-element.48.down_bias, ...), custom_call_target="tpu_custom_call" | custom-call | flops 104857600 | bytes 3276800 | tf_op jit(solution)/shard_map/pallas_call | solution.py:94
  14.1 1.5 %collective-permute-start.9 = (bf16[16,1280]{1,0:T(8,128)(2,1)S(1)}, bf16[16,1280]{1,0:T(8,128)(2,1)S(1)}, u32[]{:S(2)}, u32[]{:S(2)}) collective-permute-start(bf16[16,1280]{1,0:T(8,128)(2,1)S(1)} %convert_element_type.33), channel_id=1, source_target_pairs={{0,5},{1,4},{2,7},{3,6},{4,1},{5,0},{6,3},{7,2},{8,13},{9,12},{10,... | collective-permute-start | bytes 122888 | tf_op jit(solution)/shard_map/ppermute | solution.py:34
  15.6 1.6 %shard_map.167 = (bf16[688,4096]{1,0:T(8,128)(2,1)S(1)}, f32[16,1280]{1,0:T(8,128)S(1)}) custom-call(f32[16,1280]{1,0:T(8,128)S(1)} %get-tuple-element.52.carried.after, f32[16,1280]{1,0:T(8,128)S(1)} %get-tuple-element.52.carried.after, bf16[688,4096]{1,0:T(8,128)(2,1)} %bitcast.2), custom_call_target="tpu_custom_call" | custom-call | bytes 2113536 | tf_op jit(solution)/shard_map/pallas_call | solution.py:190
  17.2 0.4 collective-permute-start.11
  17.6 0.1 collective-permute-done.9
  17.7 3.0 %collective-permute-start.10 = (bf16[16,1280]{1,0:T(8,128)(2,1)S(1)}, bf16[16,1280]{1,0:T(8,128)(2,1)S(1)}, u32[]{:S(2)}, u32[]{:S(2)}) collective-permute-start(bf16[16,1280]{1,0:T(8,128)(2,1)S(1)} %get-tuple-element.81), channel_id=1, source_target_pairs={{0,9},{1,8},{2,11},{3,10},{4,13},{5,12},{6,15},{7,14},{8,1},{9,0},... | collective-permute-start | bytes 122888 | tf_op jit(solution)/shard_map/ppermute | solution.py:34
  20.7 1.8 %shard_map.168 = (bf16[688,4096]{1,0:T(8,128)(2,1)S(1)}, f32[16,1280]{1,0:T(8,128)S(1)}) custom-call(f32[16,1280]{1,0:T(8,128)S(1)} %get-tuple-element.82.carried.after, f32[16,1280]{1,0:T(8,128)S(1)} %get-tuple-element.82.carried.after, bf16[688,4096]{1,0:T(8,128)(2,1)} %bitcast.6, ...), custom_call_target="tpu_custom_call", output_to_operand_aliasing={{0}: (3, {})} | custom-call | bytes 2818048 | tf_op jit(solution)/shard_map/pallas_call | solution.py:190
  22.5 0.0 collective-permute-done.11
  22.6 0.0 collective-permute-done.10
  22.6 1.6 %collective-permute-start.12 = (bf16[16,1280]{1,0:T(8,128)(2,1)S(1)}, bf16[16,1280]{1,0:T(8,128)(2,1)S(1)}, u32[]{:S(2)}, u32[]{:S(2)}) collective-permute-start(bf16[16,1280]{1,0:T(8,128)(2,1)S(1)} %get-tuple-element.60), channel_id=1, source_target_pairs={{0,3},{1,2},{2,1},{3,0},{4,7},{5,6},{6,5},{7,4},{8,11},{9,10},{10,... | collective-permute-start | bytes 122888 | tf_op jit(solution)/shard_map/ppermute | solution.py:34
  24.2 0.3 collective-permute-start.15
  24.5 1.6 %shard_map.169 = (bf16[688,4096]{1,0:T(8,128)(2,1)S(1)}, f32[16,1280]{1,0:T(8,128)S(1)}) custom-call(f32[16,1280]{1,0:T(8,128)S(1)} %get-tuple-element.80.carried.after, f32[16,1280]{1,0:T(8,128)S(1)} %get-tuple-element.80.carried.after, bf16[688,4096]{1,0:T(8,128)(2,1)} %bitcast.3, ...), custom_call_target="tpu_custom_call", output_to_operand_aliasing={{0}: (3, {})} | custom-call | bytes 2113536 | tf_op jit(solution)/shard_map/pallas_call | solution.py:190
  26.1 0.0 collective-permute-done.12.arrived
  26.1 0.2 shard_map.170.post
  26.3 0.3 shard_map.171.carried.after
  26.6 2.7 %collective-permute-start.13 = (bf16[1,2,16,256]{3,2,1,0:T(8,128)(2,1)S(1)}, bf16[1,2,16,256]{3,2,1,0:T(8,128)(2,1)S(1)}, u32[]{:S(2)}, u32[]{:S(2)}) collective-permute-start(bf16[1,2,16,256]{3,2,1,0:T(8,128)(2,1)S(1)} %shard_map.171.carried.after), channel_id=1, source_target_pairs={{0,9},{1,8},{2,11},{3,10},{4,13},{5,12},{6,15},{7,14},{8,1},{9,0},... | collective-permute-start | bytes 49160 | tf_op jit(solution)/shard_map/ppermute | solution.py:34
  29.4 1.8 %shard_map.172 = (bf16[688,4096]{1,0:T(8,128)(2,1)S(1)}, bf16[1,2,16,256]{3,2,1,0:T(8,128)(2,1)S(1)}) custom-call(bf16[1,2,16,256]{3,2,1,0:T(8,128)(2,1)S(1)} %shard_map.171.carried.after, bf16[1,2,16,256]{3,2,1,0:T(8,128)(2,1)S(1)} %shard_map.171.carried.after, bf16[688,4096]{1,0:T(8,128)(2,1)} %down_hbm.1), custom_call_target="tpu_custom_call" | custom-call | bytes 2818048 | tf_op jit(solution)/shard_map/pallas_call | solution.py:190
  31.2 0.0 collective-permute-done.13
  31.2 2.6 %collective-permute-start.14 = (bf16[2,2,16,256]{3,2,1,0:T(8,128)(2,1)S(1)}, bf16[2,2,16,256]{3,2,1,0:T(8,128)(2,1)S(1)}, u32[]{:S(2)}, u32[]{:S(2)}) collective-permute-start(bf16[2,2,16,256]{3,2,1,0:T(8,128)(2,1)S(1)} %constant_dynamic-update-slice_fusion.2.carried.after), channel_id=1, source_target_pairs={{0,5},{1,4},{2,7},{3,6},{4,1},{5,0},{6,3},{7,2},{8,13},{9,12},{10,... | collective-permute-start | bytes 98312 | tf_op jit(solution)/shard_map/ppermute | solution.py:34
  33.8 1.4 %shard_map.173 = (bf16[688,4096]{1,0:T(8,128)(2,1)S(1)}, bf16[2,2,16,256]{3,2,1,0:T(8,128)(2,1)S(1)}) custom-call(bf16[2,2,16,256]{3,2,1,0:T(8,128)(2,1)S(1)} %constant_dynamic-update-slice_fusion.2.carried.after, bf16[2,2,16,256]{3,2,1,0:T(8,128)(2,1)S(1)} %constant_dynamic-update-slice_fusion.2.carried.after, ...), custom_call_target="tpu_custom_call", output_to_operand_aliasing={{0}: (3, {})} | custom-call | bytes 1409024 | tf_op jit(solution)/shard_map/pallas_call | solution.py:190
  35.2 0.2 collective-permute-done.14
  35.4 1.8 %collective-permute-start.16 = (bf16[4,2,16,256]{3,2,1,0:T(8,128)(2,1)S(1)}, bf16[4,2,16,256]{3,2,1,0:T(8,128)(2,1)S(1)}, u32[]{:S(2)}, u32[]{:S(2)}) collective-permute-start(bf16[4,2,16,256]{3,2,1,0:T(8,128)(2,1)S(1)} %constant_dynamic-update-slice_fusion.4.carried), channel_id=1, source_target_pairs={{0,3},{1,2},{2,1},{3,0},{4,7},{5,6},{6,5},{7,4},{8,11},{9,10},{10,... | collective-permute-start | bytes 196616 | tf_op jit(solution)/shard_map/ppermute | solution.py:34
  37.3 0.0 collective-permute-done.15
  37.3 0.1 collective-permute-start.18
  37.4 1.4 %shard_map.174 = (bf16[688,4096]{1,0:T(8,128)(2,1)S(1)}, bf16[4,2,16,256]{3,2,1,0:T(8,128)(2,1)S(1)}) custom-call(bf16[4,2,16,256]{3,2,1,0:T(8,128)(2,1)S(1)} %constant_dynamic-update-slice_fusion.4.carried, bf16[32,4096]{1,0:T(8,128)(2,1)S(1)} %constant_dynamic-update-slice_fusion.6.after.prompts, ...), custom_call_target="tpu_custom_call", output_to_operand_aliasing={{0}: (3, {})} | custom-call | bytes 1409024 | tf_op jit(solution)/shard_map/pallas_call | solution.py:190
  38.8 0.9 %collective-permute-done.16 = bf16[4,2,16,256]{3,2,1,0:T(8,128)(2,1)S(1)} collective-permute-done((bf16[4,2,16,256]{3,2,1,0:T(8,128)(2,1)S(1)}, bf16[4,2,16,256]{3,2,1,0:T(8,128)(2,1)S(1)}, u32[]{:S(2)}, u32[]{:S(2)}) %collective-permute-start.16) | collective-permute-done | bytes 65568 | tf_op jit(solution)/shard_map/ppermute | solution.py:34
  39.6 0.1 collective-permute-start.17
  39.7 1.2 %collective-permute-done.17.far = bf16[8,2,16,256]{3,2,1,0:T(8,128)(2,1)S(1)} collective-permute-done((bf16[8,2,16,256]{3,2,1,0:T(8,128)(2,1)S(1)}, bf16[8,2,16,256]{3,2,1,0:T(8,128)(2,1)S(1)}, u32[]{:S(2)}, u32[]{:S(2)}) %collective-permute-start.17) | collective-permute-done | bytes 131104 | tf_op jit(solution)/shard_map/ppermute | solution.py:34
  41.0 0.0 collective-permute-done.18.others
  41.0 4.8 %shard_map.175 = (bf16[32,4096]{1,0:T(8,128)(2,1)S(1)}, f32[32,4096]{1,0:T(8,128)S(1)}) custom-call(bf16[8,2,16,256]{3,2,1,0:T(8,128)(2,1)S(1)} %constant_dynamic-update-slice_fusion.8.near, bf16[8,2,16,256]{3,2,1,0:T(8,128)(2,1)S(1)} %collective-permute-done.17.far, s32[64]{0:T(128)S(1)} %get-tuple-element.72.source, ...), custom_call_target="tpu_custom_call" | custom-call | flops 1082130432 | bytes 11272192 | tf_op jit(solution)/shard_map/pallas_call | solution.py:277
  45.8 0.2 collective-permute-start.19
  46.0 1.4 %collective-permute-done.19 = bf16[32,4096]{1,0:T(8,128)(2,1)S(1)} collective-permute-done((bf16[32,4096]{1,0:T(8,128)(2,1)S(1)}, bf16[32,4096]{1,0:T(8,128)(2,1)S(1)}, u32[]{:S(2)}, u32[]{:S(2)}) %collective-permute-start.19) | collective-permute-done | bytes 262176 | tf_op jit(solution)/shard_map/ppermute | solution.py:34
  47.4 1.5 %collective-permute-start.20 = (bf16[16,4096]{1,0:T(8,128)(2,1)S(1)}, bf16[16,4096]{1,0:T(8,128)(2,1)S(1)}, u32[]{:S(2)}, u32[]{:S(2)}) collective-permute-start(bf16[16,4096]{1,0:T(8,128)(2,1)S(1)} %slice.41), channel_id=1, source_target_pairs={{0,3},{1,2},{2,1},{3,0},{4,7},{5,6},{6,5},{7,4},{8,11},{9,10},{10,... | collective-permute-start | bytes 393224 | tf_op jit(solution)/shard_map/ppermute | solution.py:34
  48.9 4.1 %collective-permute-done.20 = bf16[16,4096]{1,0:T(8,128)(2,1)S(1)} collective-permute-done((bf16[16,4096]{1,0:T(8,128)(2,1)S(1)}, bf16[16,4096]{1,0:T(8,128)(2,1)S(1)}, u32[]{:S(2)}, u32[]{:S(2)}) %collective-permute-start.20) | collective-permute-done | bytes 131104 | tf_op jit(solution)/shard_map/ppermute | solution.py:34
  53.0 1.8 %collective-permute-start.21 = (bf16[8,4096]{1,0:T(8,128)(2,1)S(1)}, bf16[8,4096]{1,0:T(8,128)(2,1)S(1)}, u32[]{:S(2)}, u32[]{:S(2)}) collective-permute-start(bf16[8,4096]{1,0:T(8,128)(2,1)S(1)} %slice.42), channel_id=1, source_target_pairs={{0,5},{1,4},{2,7},{3,6},{4,1},{5,0},{6,3},{7,2},{8,13},{9,12},{10,... | collective-permute-start | bytes 196616 | tf_op jit(solution)/shard_map/ppermute | solution.py:34
  54.8 2.4 %collective-permute-done.21 = bf16[8,4096]{1,0:T(8,128)(2,1)S(1)} collective-permute-done((bf16[8,4096]{1,0:T(8,128)(2,1)S(1)}, bf16[8,4096]{1,0:T(8,128)(2,1)S(1)}, u32[]{:S(2)}, u32[]{:S(2)}) %collective-permute-start.21) | collective-permute-done | bytes 65568 | tf_op jit(solution)/shard_map/ppermute | solution.py:34
  57.2 2.2 %collective-permute-start.22 = (bf16[4,4096]{1,0:T(4,128)(2,1)S(1)}, bf16[4,4096]{1,0:T(4,128)(2,1)S(1)}, u32[]{:S(2)}, u32[]{:S(2)}) collective-permute-start(bf16[4,4096]{1,0:T(4,128)(2,1)S(1)} %slice.43), channel_id=1, source_target_pairs={{0,9},{1,8},{2,11},{3,10},{4,13},{5,12},{6,15},{7,14},{8,1},{9,0},... | collective-permute-start | bytes 98312 | tf_op jit(solution)/shard_map/ppermute | solution.py:34
  59.4 2.1 %collective-permute-done.22 = bf16[4,4096]{1,0:T(4,128)(2,1)S(1)} collective-permute-done((bf16[4,4096]{1,0:T(4,128)(2,1)S(1)}, bf16[4,4096]{1,0:T(4,128)(2,1)S(1)}, u32[]{:S(2)}, u32[]{:S(2)}) %collective-permute-start.22) | collective-permute-done | bytes 32800 | tf_op jit(solution)/shard_map/ppermute | solution.py:34
  61.5 0.6 %fusion = bf16[4,4096]{1,0:T(4,128)(2,1)} fusion(f32[8,4096]{1,0:T(8,128)S(1)} %slice_add_fusion.1, bf16[4,4096]{1,0:T(4,128)(2,1)S(1)} %collective-permute-done.22), kind=kLoop, calls=%fused_computation.11 | loop fusion | flops 49152 | bytes 131072 | tf_op jit(solution)/shard_map/convert_element_type | solution.py:469
  (23 shorter events, 0.3 us)
Async XLA Ops:
  0.0 8.9 %copy-start = (bf16[320,1280]{1,0:T(8,128)(2,1)S(1)}, bf16[320,1280]{1,0:T(8,128)(2,1)}, u32[]{:S(2)}) copy-start(bf16[320,1280]{1,0:T(8,128)(2,1)} %refs_3_.3) | copy-start | bytes 2457604
  0.0 10.6 %copy-start.1 = (bf16[320]{0:T(512)(128)(2,1)S(1)}, bf16[320]{0:T(512)(128)(2,1)}, u32[]{:S(2)}) copy-start(bf16[320]{0:T(512)(128)(2,1)} %refs_1_.3) | copy-start | bytes 1924
  0.0 5.6 %collective-permute-start = (bf16[4,1280]{1,0:T(4,128)(2,1)}, bf16[4,1280]{1,0:T(4,128)(2,1)S(1)}, u32[]{:S(2)}, u32[]{:S(2)}) collective-permute-start(bf16[4,1280]{1,0:T(4,128)(2,1)} %refs_0_.2), channel_id=1, source_target_pairs={{0,9},{1,8},{2,11},{3,10},{4,13},{5,12},{6,15},{7,14},{8,1},{9,0},... | collective-permute-start | bytes 30728 | tf_op jit(solution)/shard_map/ppermute | solution.py:34
  3.5 5.6 %collective-permute-start.2 = (bf16[4,4096]{1,0:T(4,128)(2,1)}, bf16[4,4096]{1,0:T(4,128)(2,1)S(1)}, u32[]{:S(2)}, u32[]{:S(2)}) collective-permute-start(bf16[4,4096]{1,0:T(4,128)(2,1)} %refs_1_.2), channel_id=1, source_target_pairs={{0,9},{1,8},{2,11},{3,10},{4,13},{5,12},{6,15},{7,14},{8,1},{9,0},... | collective-permute-start | bytes 98312 | tf_op jit(solution)/shard_map/ppermute | solution.py:34
  3.6 7.5 %collective-permute-start.3 = (bf16[1280,256]{1,0:T(8,128)(2,1)}, bf16[1280,256]{1,0:T(8,128)(2,1)S(1)}, u32[]{:S(2)}, u32[]{:S(2)}) collective-permute-start(bf16[1280,256]{1,0:T(8,128)(2,1)} %refs_6_.1), channel_id=1, source_target_pairs={{0,1},{1,0},{2,3},{3,2},{4,5},{5,4},{6,7},{7,6},{8,9},{9,8},{10,11... | collective-permute-start | bytes 1966088 | tf_op jit(solution)/shard_map/ppermute | solution.py:34
  4.2 6.4 %collective-permute-start.4 = (f32[256]{0:T(256)}, f32[256]{0:T(256)S(1)}, u32[]{:S(2)}, u32[]{:S(2)}) collective-permute-start(f32[256]{0:T(256)} %refs_7_.1), channel_id=1, source_target_pairs={{0,1},{1,0},{2,3},{3,2},{4,5},{5,4},{6,7},{7,6},{8,9},{9,8},{10,11... | collective-permute-start | bytes 3080 | tf_op jit(solution)/shard_map/ppermute | solution.py:34
  4.2 8.6 %collective-permute-start.7 = (bf16[320,1280]{1,0:T(8,128)(2,1)}, bf16[320,1280]{1,0:T(8,128)(2,1)S(1)}, u32[]{:S(2)}, u32[]{:S(2)}) collective-permute-start(bf16[320,1280]{1,0:T(8,128)(2,1)} %refs_2_.3), channel_id=1, source_target_pairs={{0,1},{1,0},{2,3},{3,2},{4,5},{5,4},{6,7},{7,6},{8,9},{9,8},{10,11... | collective-permute-start | bytes 2457608 | tf_op jit(solution)/shard_map/ppermute | solution.py:34
  5.6 3.3 %collective-permute-start.1 = (bf16[8,1280]{1,0:T(8,128)(2,1)S(1)}, bf16[8,1280]{1,0:T(8,128)(2,1)S(1)}, u32[]{:S(2)}, u32[]{:S(2)}) collective-permute-start(bf16[8,1280]{1,0:T(8,128)(2,1)S(1)} %pad_maximum_fusion.3.carried.after), channel_id=1, source_target_pairs={{0,5},{1,4},{2,7},{3,6},{4,1},{5,0},{6,3},{7,2},{8,13},{9,12},{10,... | collective-permute-start | bytes 61448 | tf_op jit(solution)/shard_map/ppermute | solution.py:34
  8.9 3.9 %collective-permute-start.8 = (bf16[320,1280]{1,0:T(8,128)(2,1)S(1)}, bf16[320,1280]{1,0:T(8,128)(2,1)S(1)}, u32[]{:S(2)}, u32[]{:S(2)}) collective-permute-start(bf16[320,1280]{1,0:T(8,128)(2,1)S(1)} %copy-done), channel_id=1, source_target_pairs={{0,1},{1,0},{2,3},{3,2},{4,5},{5,4},{6,7},{7,6},{8,9},{9,8},{10,11... | collective-permute-start | bytes 2457608 | tf_op jit(solution)/shard_map/ppermute | solution.py:34
  9.1 3.7 %collective-permute-start.5 = (bf16[16,1280]{1,0:T(8,128)(2,1)S(1)}, bf16[16,1280]{1,0:T(8,128)(2,1)S(1)}, u32[]{:S(2)}, u32[]{:S(2)}) collective-permute-start(bf16[16,1280]{1,0:T(8,128)(2,1)S(1)} %constant_dynamic-update-slice_fusion.refs_10_), channel_id=1, source_target_pairs={{0,3},{1,2},{2,1},{3,0},{4,7},{5,6},{6,5},{7,4},{8,11},{9,10},{10,... | collective-permute-start | bytes 122888 | tf_op jit(solution)/shard_map/ppermute | solution.py:34
  10.7 2.1 %collective-permute-start.6 = (bf16[320]{0:T(512)(128)(2,1)S(1)}, bf16[320]{0:T(512)(128)(2,1)S(1)}, u32[]{:S(2)}, u32[]{:S(2)}) collective-permute-start(bf16[320]{0:T(512)(128)(2,1)S(1)} %copy-done.1), channel_id=1, source_target_pairs={{0,1},{1,0},{2,3},{3,2},{4,5},{5,4},{6,7},{7,6},{8,9},{9,8},{10,11... | collective-permute-start | bytes 1928 | tf_op jit(solution)/shard_map/ppermute | solution.py:34
  14.1 3.6 %collective-permute-start.9 = (bf16[16,1280]{1,0:T(8,128)(2,1)S(1)}, bf16[16,1280]{1,0:T(8,128)(2,1)S(1)}, u32[]{:S(2)}, u32[]{:S(2)}) collective-permute-start(bf16[16,1280]{1,0:T(8,128)(2,1)S(1)} %convert_element_type.33), channel_id=1, source_target_pairs={{0,5},{1,4},{2,7},{3,6},{4,1},{5,0},{6,3},{7,2},{8,13},{9,12},{10,... | collective-permute-start | bytes 122888 | tf_op jit(solution)/shard_map/ppermute | solution.py:34
  17.2 5.4 %collective-permute-start.11 = (bf16[8,4096]{1,0:T(8,128)(2,1)S(1)}, bf16[8,4096]{1,0:T(8,128)(2,1)S(1)}, u32[]{:S(2)}, u32[]{:S(2)}) collective-permute-start(bf16[8,4096]{1,0:T(8,128)(2,1)S(1)} %pad_maximum_fusion.2.refs_11_), channel_id=1, source_target_pairs={{0,5},{1,4},{2,7},{3,6},{4,1},{5,0},{6,3},{7,2},{8,13},{9,12},{10,... | collective-permute-start | bytes 196616 | tf_op jit(solution)/shard_map/ppermute | solution.py:34
  17.7 4.8 %collective-permute-start.10 = (bf16[16,1280]{1,0:T(8,128)(2,1)S(1)}, bf16[16,1280]{1,0:T(8,128)(2,1)S(1)}, u32[]{:S(2)}, u32[]{:S(2)}) collective-permute-start(bf16[16,1280]{1,0:T(8,128)(2,1)S(1)} %get-tuple-element.81), channel_id=1, source_target_pairs={{0,9},{1,8},{2,11},{3,10},{4,13},{5,12},{6,15},{7,14},{8,1},{9,0},... | collective-permute-start | bytes 122888 | tf_op jit(solution)/shard_map/ppermute | solution.py:34
  22.6 3.5 %collective-permute-start.12 = (bf16[16,1280]{1,0:T(8,128)(2,1)S(1)}, bf16[16,1280]{1,0:T(8,128)(2,1)S(1)}, u32[]{:S(2)}, u32[]{:S(2)}) collective-permute-start(bf16[16,1280]{1,0:T(8,128)(2,1)S(1)} %get-tuple-element.60), channel_id=1, source_target_pairs={{0,3},{1,2},{2,1},{3,0},{4,7},{5,6},{6,5},{7,4},{8,11},{9,10},{10,... | collective-permute-start | bytes 122888 | tf_op jit(solution)/shard_map/ppermute | solution.py:34
  24.2 13.1 %collective-permute-start.15 = (bf16[16,4096]{1,0:T(8,128)(2,1)S(1)}, bf16[16,4096]{1,0:T(8,128)(2,1)S(1)}, u32[]{:S(2)}, u32[]{:S(2)}) collective-permute-start(bf16[16,4096]{1,0:T(8,128)(2,1)S(1)} %pad_maximum_fusion.after), channel_id=1, source_target_pairs={{0,3},{1,2},{2,1},{3,0},{4,7},{5,6},{6,5},{7,4},{8,11},{9,10},{10,... | collective-permute-start | bytes 393224 | tf_op jit(solution)/shard_map/ppermute | solution.py:34
  26.6 4.6 %collective-permute-start.13 = (bf16[1,2,16,256]{3,2,1,0:T(8,128)(2,1)S(1)}, bf16[1,2,16,256]{3,2,1,0:T(8,128)(2,1)S(1)}, u32[]{:S(2)}, u32[]{:S(2)}) collective-permute-start(bf16[1,2,16,256]{3,2,1,0:T(8,128)(2,1)S(1)} %shard_map.171.carried.after), channel_id=1, source_target_pairs={{0,9},{1,8},{2,11},{3,10},{4,13},{5,12},{6,15},{7,14},{8,1},{9,0},... | collective-permute-start | bytes 49160 | tf_op jit(solution)/shard_map/ppermute | solution.py:34
  31.2 4.2 %collective-permute-start.14 = (bf16[2,2,16,256]{3,2,1,0:T(8,128)(2,1)S(1)}, bf16[2,2,16,256]{3,2,1,0:T(8,128)(2,1)S(1)}, u32[]{:S(2)}, u32[]{:S(2)}) collective-permute-start(bf16[2,2,16,256]{3,2,1,0:T(8,128)(2,1)S(1)} %constant_dynamic-update-slice_fusion.2.carried.after), channel_id=1, source_target_pairs={{0,5},{1,4},{2,7},{3,6},{4,1},{5,0},{6,3},{7,2},{8,13},{9,12},{10,... | collective-permute-start | bytes 98312 | tf_op jit(solution)/shard_map/ppermute | solution.py:34
  35.4 4.2 %collective-permute-start.16 = (bf16[4,2,16,256]{3,2,1,0:T(8,128)(2,1)S(1)}, bf16[4,2,16,256]{3,2,1,0:T(8,128)(2,1)S(1)}, u32[]{:S(2)}, u32[]{:S(2)}) collective-permute-start(bf16[4,2,16,256]{3,2,1,0:T(8,128)(2,1)S(1)} %constant_dynamic-update-slice_fusion.4.carried), channel_id=1, source_target_pairs={{0,3},{1,2},{2,1},{3,0},{4,7},{5,6},{6,5},{7,4},{8,11},{9,10},{10,... | collective-permute-start | bytes 196616 | tf_op jit(solution)/shard_map/ppermute | solution.py:34
  37.3 3.7 %collective-permute-start.18 = (bf16[32,4096]{1,0:T(8,128)(2,1)S(1)}, bf16[32,4096]{1,0:T(8,128)(2,1)S(1)}, u32[]{:S(2)}, u32[]{:S(2)}) collective-permute-start(bf16[32,4096]{1,0:T(8,128)(2,1)S(1)} %constant_dynamic-update-slice_fusion.6.after.prompts), channel_id=1, source_target_pairs={{0,1},{1,0},{2,3},{3,2},{4,5},{5,4},{6,7},{7,6},{8,9},{9,8},{10,11... | collective-permute-start | bytes 786440 | tf_op jit(solution)/shard_map/ppermute | solution.py:34
  39.6 1.3 %collective-permute-start.17 = (bf16[8,2,16,256]{3,2,1,0:T(8,128)(2,1)S(1)}, bf16[8,2,16,256]{3,2,1,0:T(8,128)(2,1)S(1)}, u32[]{:S(2)}, u32[]{:S(2)}) collective-permute-start(bf16[8,2,16,256]{3,2,1,0:T(8,128)(2,1)S(1)} %constant_dynamic-update-slice_fusion.8.near), channel_id=1, source_target_pairs={{0,1},{1,0},{2,3},{3,2},{4,5},{5,4},{6,7},{7,6},{8,9},{9,8},{10,11... | collective-permute-start | bytes 393224 | tf_op jit(solution)/shard_map/ppermute | solution.py:34
  45.8 1.6 %collective-permute-start.19 = (bf16[32,4096]{1,0:T(8,128)(2,1)S(1)}, bf16[32,4096]{1,0:T(8,128)(2,1)S(1)}, u32[]{:S(2)}, u32[]{:S(2)}) collective-permute-start(bf16[32,4096]{1,0:T(8,128)(2,1)S(1)} %get-tuple-element.78), channel_id=1, source_target_pairs={{0,1},{1,0},{2,3},{3,2},{4,5},{5,4},{6,7},{7,6},{8,9},{9,8},{10,11... | collective-permute-start | bytes 786440 | tf_op jit(solution)/shard_map/ppermute | solution.py:34
  47.4 5.5 %collective-permute-start.20 = (bf16[16,4096]{1,0:T(8,128)(2,1)S(1)}, bf16[16,4096]{1,0:T(8,128)(2,1)S(1)}, u32[]{:S(2)}, u32[]{:S(2)}) collective-permute-start(bf16[16,4096]{1,0:T(8,128)(2,1)S(1)} %slice.41), channel_id=1, source_target_pairs={{0,3},{1,2},{2,1},{3,0},{4,7},{5,6},{6,5},{7,4},{8,11},{9,10},{10,... | collective-permute-start | bytes 393224 | tf_op jit(solution)/shard_map/ppermute | solution.py:34
  53.0 4.1 %collective-permute-start.21 = (bf16[8,4096]{1,0:T(8,128)(2,1)S(1)}, bf16[8,4096]{1,0:T(8,128)(2,1)S(1)}, u32[]{:S(2)}, u32[]{:S(2)}) collective-permute-start(bf16[8,4096]{1,0:T(8,128)(2,1)S(1)} %slice.42), channel_id=1, source_target_pairs={{0,5},{1,4},{2,7},{3,6},{4,1},{5,0},{6,3},{7,2},{8,13},{9,12},{10,... | collective-permute-start | bytes 196616 | tf_op jit(solution)/shard_map/ppermute | solution.py:34
  57.2 4.3 %collective-permute-start.22 = (bf16[4,4096]{1,0:T(4,128)(2,1)S(1)}, bf16[4,4096]{1,0:T(4,128)(2,1)S(1)}, u32[]{:S(2)}, u32[]{:S(2)}) collective-permute-start(bf16[4,4096]{1,0:T(4,128)(2,1)S(1)} %slice.43), channel_id=1, source_target_pairs={{0,9},{1,8},{2,11},{3,10},{4,13},{5,12},{6,15},{7,14},{8,1},{9,0},... | collective-permute-start | bytes 98312 | tf_op jit(solution)/shard_map/ppermute | solution.py:34

commit v7 on v6

--- a/solution.py
+++ b/solution.py
@@ -12,33 +12,44 @@
     return (1 << bit) | 1 if bit else 1
 
 
-def slot_of(offset, bits):
-    parity = offset & 1
-    slot = 0
-    for bit in range(1, bits):
-        one = (offset >> bit) & 1
-        parity = parity ^ one
-        slot = slot + (one << (bits - 1 - bit))
-    return slot + (parity << (bits - 1))
-
-
-def offset_of(slot, bits):
-    offset = (slot >> (bits - 1)) & 1
-    for bit in range(1, bits):
-        offset = offset ^ (((slot >> (bits - 1 - bit)) & 1) * mask_of(bit))
-    return offset
-
-
-def swap(value, bit, count):
-    pairs = [(i, i ^ mask_of(bit)) for i in range(count)]
-    return lax.ppermute(value, "tp", pairs)
-
-
 def parity_of(index, bits):
     parity = index
     for bit in range(1, bits):
         parity = parity ^ (index >> bit)
     return parity & 1
+
+
+def exchanged(flags, odd):
+    differ = (flags[1] ^ flags[2]) & odd
+    return [flags[0], flags[1] ^ differ, flags[2] ^ differ, *flags[3:]]
+
+
+def slot_of(offset, bits, parity):
+    across = parity_of(offset, bits)
+    flags = exchanged([(offset >> bit) & 1 for bit in range(bits)], parity ^ across)
+    slot = across << (bits - 1)
+    for bit in range(1, bits):
+        slot = slot + (flags[bit] << (bits - 1 - bit))
+    return slot
+
+
+def offset_of(slot, bits, parity):
+    across = (slot >> (bits - 1)) & 1
+    flags = [(slot >> (bits - 1 - bit)) & 1 for bit in range(bits)]
+    flags = exchanged(flags, parity ^ across)
+    offset = across
+    for bit in range(1, bits):
+        offset = offset ^ (flags[bit] * mask_of(bit))
+    return offset
+
+
+def swap(value, bit, count):
+    bits = count.bit_length() - 1
+    pairs = []
+    for i in range(count):
+        across = 3 - bit if bit in (1, 2) and parity_of(i, bits) else bit
+        pairs.append((i, i ^ mask_of(across)))
+    return lax.ppermute(value, "tp", pairs)
 
 
 def in_hbm(value):
@@ -71,7 +82,7 @@
     in_row = lax.broadcasted_iota(jnp.int32, (rows, rows), 1)
     frame = jnp.where(out_row < pooled, 2 * out_row, 2 * (out_row - pooled) + 1)
     device = group_device(frame // own, parity_of(me, bits), bits)
-    place = slot_of(device ^ me, bits) * own + frame % own
+    place = slot_of(device ^ me, bits, parity_of(me, bits)) * own + frame % own
     order = jnp.where(place == in_row, 1.0, 0.0).astype(jnp.bfloat16)
     values = jnp.dot(order, frames[...], preferred_element_type=jnp.float32)
     center = values - jnp.mean(values, axis=-1, keepdims=True)
@@ -223,7 +234,7 @@
     me = lax.axis_index("tp")
     out_row = lax.broadcasted_iota(jnp.int32, (rows, rows), 0)
     in_row = lax.broadcasted_iota(jnp.int32, (rows, rows), 1)
-    place = (offset_of(out_row // own, bits) ^ me) * own + out_row % own
+    place = (offset_of(out_row // own, bits, parity_of(me, bits)) ^ me) * own + out_row % own
     order = jnp.where(place == in_row, 1.0, 0.0).astype(jnp.bfloat16)
     parity = parity_of(me, bits)
     audio = lax.broadcasted_iota(jnp.int32, (2 * group, rows), 0)
@@ -239,8 +250,8 @@
     for device in range(count):
         part = slice(device * columns, (device + 1) * columns)
         differs = parity ^ parity_of(device, bits)
-        near_slot = slot_of(me ^ device ^ differs, bits)
-        far_slot = slot_of(me ^ device ^ differs, bits)
+        near_slot = slot_of(me ^ device ^ differs, bits, parity)
+        far_slot = slot_of(me ^ device ^ differs, bits, 1 - parity)
         piece = jnp.concatenate([near[near_slot, differs], far[far_slot, 1 - differs]])
         found = jnp.dot(pick, piece, preferred_element_type=jnp.float32)
         prompt = jnp.concatenate([prompts[:, part], others[:, part]])

time: 62.5 us -> 60.4 us (0.966)
  waiting for transfers between devices: 12.7 us -> 10.2 us
    ppermute x23, waiting for transfers between devices: 12.7 us -> 10.2 us  [swap(): return lax.ppermute(value, 'tp', pairs)]
  transfers between devices with their start and end apart: 23 -> 23, of which waited for: 9 -> 9; matrix products, arithmetic and copies ran while one was open for 0% -> 0% of each run, Pallas kernels for 22% -> 23%
where the time goes in v7:
time: 60.4 us; the launch traced here: 59.9 us
  starting transfers between devices  28.5 us (47%)
  Pallas kernels  20 us (33%)
  waiting for transfers between devices  10.2 us (17%)
  other arithmetic  0.84 us (1%)
    ppermute x23, starting transfers between devices, swap(): return lax.ppermute(value, 'tp', pairs)  28.5 us
    pallas_call x7, Pallas kernels, fetch(): pl.pallas_call(functools.partial(fetch_kernel, start, width), out_shape=[...  10.9 us
    ppermute x23, waiting for transfers between devices, swap(): return lax.ppermute(value, 'tp', pairs)  10.2 us
    pallas_call x1, Pallas kernels, language(): pl.pallas_call(functools.partial(language_kernel, bits), out_shape=[jax.S...  4.8 us
    pallas_call x2, Pallas kernels, stage(): pl.pallas_call(functools.partial(stage_kernel, count, len(after), carry),...  2.55 us
    pallas_call x1, Pallas kernels, encoder(): pl.pallas_call(functools.partial(encoder_kernel, bits), out_shape=[jax.Sh...  1.26 us
  transfers between devices with their start and end apart: 23, of which 9 were waited for; matrix products, arithmetic and copies ran while one was open for 0% of the time, Pallas kernels for 23%

profile of v7, /device:TPU:0, one launch (start us, length us, event | category | flops | bytes accessed | tf_op | source)
XLA Modules:
  0.0 59.9 jit_solution(9367909502356482404)
XLA Ops:
  0.0 0.0 copy-start
  0.0 0.0 copy-start.1
  0.0 3.5 %collective-permute-start = (bf16[4,1280]{1,0:T(4,128)(2,1)}, bf16[4,1280]{1,0:T(4,128)(2,1)S(1)}, u32[]{:S(2)}, u32[]{:S(2)}) collective-permute-start(bf16[4,1280]{1,0:T(4,128)(2,1)} %refs_0_.2), channel_id=1, source_target_pairs={{0,9},{1,8},{2,11},{3,10},{4,13},{5,12},{6,15},{7,14},{8,1},{9,0},... | collective-permute-start | bytes 30728 | tf_op jit(solution)/shard_map/ppermute | solution.py:52
  3.5 0.1 collective-permute-start.2
  3.6 0.7 %collective-permute-start.3 = (bf16[1280,256]{1,0:T(8,128)(2,1)}, bf16[1280,256]{1,0:T(8,128)(2,1)S(1)}, u32[]{:S(2)}, u32[]{:S(2)}) collective-permute-start(bf16[1280,256]{1,0:T(8,128)(2,1)} %refs_6_.1), channel_id=1, source_target_pairs={{0,1},{1,0},{2,3},{3,2},{4,5},{5,4},{6,7},{7,6},{8,9},{9,8},{10,11... | collective-permute-start | bytes 1966088 | tf_op jit(solution)/shard_map/ppermute | solution.py:52
  4.2 0.0 collective-permute-start.4
  4.2 0.5 collective-permute-start.7
  4.7 0.8 %shard_map.163 = (bf16[4,1280]{1,0:T(4,128)(2,1)S(1)}, bf16[4,4096]{1,0:T(4,128)(2,1)S(1)}, f32[1280]{0:T(1024)S(1)}, f32[1280]{0:T(1024)S(1)}) custom-call(bf16[4,1280]{1,0:T(4,128)(2,1)} %refs_0_.2, bf16[4,4096]{1,0:T(4,128)(2,1)} %refs_1_.2, f32[1280]{0:T(1024)} %refs_2_.2, f32[1280]{0:T(1024)} %refs_3_.2), custom_call_target="tpu_custom_call" | custom-call | bytes 48128 | tf_op jit(solution)/shard_map/pallas_call | solution.py:173
  5.6 0.0 collective-permute-done
  5.6 1.6 %collective-permute-start.1 = (bf16[8,1280]{1,0:T(8,128)(2,1)S(1)}, bf16[8,1280]{1,0:T(8,128)(2,1)S(1)}, u32[]{:S(2)}, u32[]{:S(2)}) collective-permute-start(bf16[8,1280]{1,0:T(8,128)(2,1)S(1)} %pad_maximum_fusion.3.carried.after), channel_id=1, source_target_pairs={{0,5},{1,2},{2,1},{3,6},{4,7},{5,0},{6,3},{7,4},{8,11},{9,12},{10,... | collective-permute-start | bytes 61448 | tf_op jit(solution)/shard_map/ppermute | solution.py:52
  7.2 1.4 %shard_map.164 = (bf16[688,4096]{1,0:T(8,128)(2,1)S(1)}, bf16[8,1280]{1,0:T(8,128)(2,1)S(1)}) custom-call(bf16[8,1280]{1,0:T(8,128)(2,1)S(1)} %pad_maximum_fusion.3.carried.after, bf16[8,1280]{1,0:T(8,128)(2,1)S(1)} %pad_maximum_fusion.3.carried.after, bf16[688,4096]{1,0:T(8,128)(2,1)} %bitcast.5), custom_call_target="tpu_custom_call" | custom-call | bytes 1409024 | tf_op jit(solution)/shard_map/pallas_call | solution.py:201
  8.6 0.3 collective-permute-done.1
  8.9 0.0 copy-done
  8.9 0.1 collective-permute-start.8
  9.0 0.0 collective-permute-done.2
  9.0 1.5 %collective-permute-start.5 = (bf16[16,1280]{1,0:T(8,128)(2,1)S(1)}, bf16[16,1280]{1,0:T(8,128)(2,1)S(1)}, u32[]{:S(2)}, u32[]{:S(2)}) collective-permute-start(bf16[16,1280]{1,0:T(8,128)(2,1)S(1)} %constant_dynamic-update-slice_fusion.refs_10_), channel_id=1, source_target_pairs={{0,3},{1,4},{2,7},{3,0},{4,1},{5,6},{6,5},{7,2},{8,13},{9,10},{10,... | collective-permute-start | bytes 122888 | tf_op jit(solution)/shard_map/ppermute | solution.py:52
  10.6 0.0 collective-permute-done.4.refs_13_.bias_pair
  10.6 0.0 copy-done.1
  10.7 0.4 collective-permute-start.6
  11.1 0.0 collective-permute-done.3.refs_12_.weight_pair
  11.1 1.7 %shard_map.165 = (f32[1280]{0:T(1024)S(1)}, bf16[320]{0:T(512)(128)(2,1)S(1)}, bf16[320,1280]{1,0:T(8,128)(2,1)S(1)}, bf16[320,1280]{1,0:T(8,128)(2,1)S(1)}, f32...) custom-call(f32[1280]{0:T(1024)} %refs_0_.3, ...), custom_call_target="tpu_custom_call" | custom-call | bytes 2310912 | tf_op jit(solution)/shard_map/pallas_call | solution.py:173
  12.8 0.0 collective-permute-done.5
  12.8 0.0 collective-permute-done.6.bias_pair
  12.9 0.0 collective-permute-done.7.up_pair
  12.9 0.0 collective-permute-done.8.down_pair
  12.9 1.3 %shard_map.166 = (f32[16,1280]{1,0:T(8,128)S(1)}, f32[16,1280]{1,0:T(8,128)S(1)}) custom-call(bf16[32,1280]{1,0:T(8,128)(2,1)S(1)} %pad_maximum_fusion.1.frames, f32[1280]{0:T(1024)S(1)} %get-tuple-element.46.gain, f32[1280]{0:T(1024)S(1)} %get-tuple-element.47.shift, f32[1280]{0:T(1024)S(1)} %get-tuple-element.48.down_bias, ...), custom_call_target="tpu_custom_call" | custom-call | flops 104857600 | bytes 3276800 | tf_op jit(solution)/shard_map/pallas_call | solution.py:105
  14.2 1.3 %collective-permute-start.9 = (bf16[16,1280]{1,0:T(8,128)(2,1)S(1)}, bf16[16,1280]{1,0:T(8,128)(2,1)S(1)}, u32[]{:S(2)}, u32[]{:S(2)}) collective-permute-start(bf16[16,1280]{1,0:T(8,128)(2,1)S(1)} %convert_element_type.33), channel_id=1, source_target_pairs={{0,5},{1,2},{2,1},{3,6},{4,7},{5,0},{6,3},{7,4},{8,11},{9,12},{10,... | collective-permute-start | bytes 122888 | tf_op jit(solution)/shard_map/ppermute | solution.py:52
  15.5 1.6 %shard_map.167 = (bf16[688,4096]{1,0:T(8,128)(2,1)S(1)}, f32[16,1280]{1,0:T(8,128)S(1)}) custom-call(f32[16,1280]{1,0:T(8,128)S(1)} %get-tuple-element.52.carried.after, f32[16,1280]{1,0:T(8,128)S(1)} %get-tuple-element.52.carried.after, bf16[688,4096]{1,0:T(8,128)(2,1)} %bitcast.2), custom_call_target="tpu_custom_call" | custom-call | bytes 2113536 | tf_op jit(solution)/shard_map/pallas_call | solution.py:201
  17.1 0.6 collective-permute-start.11
  17.7 0.0 collective-permute-done.9
  17.7 3.4 %collective-permute-start.10 = (bf16[16,1280]{1,0:T(8,128)(2,1)S(1)}, bf16[16,1280]{1,0:T(8,128)(2,1)S(1)}, u32[]{:S(2)}, u32[]{:S(2)}) collective-permute-start(bf16[16,1280]{1,0:T(8,128)(2,1)S(1)} %get-tuple-element.81), channel_id=1, source_target_pairs={{0,9},{1,8},{2,11},{3,10},{4,13},{5,12},{6,15},{7,14},{8,1},{9,0},... | collective-permute-start | bytes 122888 | tf_op jit(solution)/shard_map/ppermute | solution.py:52
  21.1 1.8 %shard_map.168 = (bf16[688,4096]{1,0:T(8,128)(2,1)S(1)}, f32[16,1280]{1,0:T(8,128)S(1)}) custom-call(f32[16,1280]{1,0:T(8,128)S(1)} %get-tuple-element.82.carried.after, f32[16,1280]{1,0:T(8,128)S(1)} %get-tuple-element.82.carried.after, bf16[688,4096]{1,0:T(8,128)(2,1)} %bitcast.6, ...), custom_call_target="tpu_custom_call", output_to_operand_aliasing={{0}: (3, {})} | custom-call | bytes 2818048 | tf_op jit(solution)/shard_map/pallas_call | solution.py:201
  22.9 0.0 collective-permute-done.11
  22.9 0.1 collective-permute-done.10
  23.0 1.3 %collective-permute-start.12 = (bf16[16,1280]{1,0:T(8,128)(2,1)S(1)}, bf16[16,1280]{1,0:T(8,128)(2,1)S(1)}, u32[]{:S(2)}, u32[]{:S(2)}) collective-permute-start(bf16[16,1280]{1,0:T(8,128)(2,1)S(1)} %get-tuple-element.60), channel_id=1, source_target_pairs={{0,3},{1,4},{2,7},{3,0},{4,1},{5,6},{6,5},{7,2},{8,13},{9,10},{10,... | collective-permute-start | bytes 122888 | tf_op jit(solution)/shard_map/ppermute | solution.py:52
  24.3 0.6 %collective-permute-start.15 = (bf16[16,4096]{1,0:T(8,128)(2,1)S(1)}, bf16[16,4096]{1,0:T(8,128)(2,1)S(1)}, u32[]{:S(2)}, u32[]{:S(2)}) collective-permute-start(bf16[16,4096]{1,0:T(8,128)(2,1)S(1)} %pad_maximum_fusion.after), channel_id=1, source_target_pairs={{0,3},{1,4},{2,7},{3,0},{4,1},{5,6},{6,5},{7,2},{8,13},{9,10},{10,... | collective-permute-start | bytes 393224 | tf_op jit(solution)/shard_map/ppermute | solution.py:52
  24.9 1.6 %shard_map.169 = (bf16[688,4096]{1,0:T(8,128)(2,1)S(1)}, f32[16,1280]{1,0:T(8,128)S(1)}) custom-call(f32[16,1280]{1,0:T(8,128)S(1)} %get-tuple-element.80.carried.after, f32[16,1280]{1,0:T(8,128)S(1)} %get-tuple-element.80.carried.after, bf16[688,4096]{1,0:T(8,128)(2,1)} %bitcast.3, ...), custom_call_target="tpu_custom_call", output_to_operand_aliasing={{0}: (3, {})} | custom-call | bytes 2113536 | tf_op jit(solution)/shard_map/pallas_call | solution.py:201
  26.5 0.0 collective-permute-done.12.arrived
  26.5 0.2 shard_map.170.post
  26.7 0.3 shard_map.171.carried.after
  27.0 2.6 %collective-permute-start.13 = (bf16[1,2,16,256]{3,2,1,0:T(8,128)(2,1)S(1)}, bf16[1,2,16,256]{3,2,1,0:T(8,128)(2,1)S(1)}, u32[]{:S(2)}, u32[]{:S(2)}) collective-permute-start(bf16[1,2,16,256]{3,2,1,0:T(8,128)(2,1)S(1)} %shard_map.171.carried.after), channel_id=1, source_target_pairs={{0,9},{1,8},{2,11},{3,10},{4,13},{5,12},{6,15},{7,14},{8,1},{9,0},... | collective-permute-start | bytes 49160 | tf_op jit(solution)/shard_map/ppermute | solution.py:52
  29.6 1.8 %shard_map.172 = (bf16[688,4096]{1,0:T(8,128)(2,1)S(1)}, bf16[1,2,16,256]{3,2,1,0:T(8,128)(2,1)S(1)}) custom-call(bf16[1,2,16,256]{3,2,1,0:T(8,128)(2,1)S(1)} %shard_map.171.carried.after, bf16[1,2,16,256]{3,2,1,0:T(8,128)(2,1)S(1)} %shard_map.171.carried.after, bf16[688,4096]{1,0:T(8,128)(2,1)} %down_hbm.1), custom_call_target="tpu_custom_call" | custom-call | bytes 2818048 | tf_op jit(solution)/shard_map/pallas_call | solution.py:201
  31.4 0.0 collective-permute-done.13
  31.4 2.1 %collective-permute-start.14 = (bf16[2,2,16,256]{3,2,1,0:T(8,128)(2,1)S(1)}, bf16[2,2,16,256]{3,2,1,0:T(8,128)(2,1)S(1)}, u32[]{:S(2)}, u32[]{:S(2)}) collective-permute-start(bf16[2,2,16,256]{3,2,1,0:T(8,128)(2,1)S(1)} %constant_dynamic-update-slice_fusion.2.carried.after), channel_id=1, source_target_pairs={{0,5},{1,2},{2,1},{3,6},{4,7},{5,0},{6,3},{7,4},{8,11},{9,12},{10,... | collective-permute-start | bytes 98312 | tf_op jit(solution)/shard_map/ppermute | solution.py:52
  33.5 1.4 %shard_map.173 = (bf16[688,4096]{1,0:T(8,128)(2,1)S(1)}, bf16[2,2,16,256]{3,2,1,0:T(8,128)(2,1)S(1)}) custom-call(bf16[2,2,16,256]{3,2,1,0:T(8,128)(2,1)S(1)} %constant_dynamic-update-slice_fusion.2.carried.after, bf16[2,2,16,256]{3,2,1,0:T(8,128)(2,1)S(1)} %constant_dynamic-update-slice_fusion.2.carried.after, ...), custom_call_target="tpu_custom_call", output_to_operand_aliasing={{0}: (3, {})} | custom-call | bytes 1409024 | tf_op jit(solution)/shard_map/pallas_call | solution.py:201
  34.9 0.2 collective-permute-done.14
  35.1 1.6 %collective-permute-start.16 = (bf16[4,2,16,256]{3,2,1,0:T(8,128)(2,1)S(1)}, bf16[4,2,16,256]{3,2,1,0:T(8,128)(2,1)S(1)}, u32[]{:S(2)}, u32[]{:S(2)}) collective-permute-start(bf16[4,2,16,256]{3,2,1,0:T(8,128)(2,1)S(1)} %constant_dynamic-update-slice_fusion.4.carried), channel_id=1, source_target_pairs={{0,3},{1,4},{2,7},{3,0},{4,1},{5,6},{6,5},{7,2},{8,13},{9,10},{10,... | collective-permute-start | bytes 196616 | tf_op jit(solution)/shard_map/ppermute | solution.py:52
  36.7 0.0 collective-permute-done.15
  36.8 0.3 collective-permute-start.18
  37.1 1.4 %shard_map.174 = (bf16[688,4096]{1,0:T(8,128)(2,1)S(1)}, bf16[4,2,16,256]{3,2,1,0:T(8,128)(2,1)S(1)}) custom-call(bf16[4,2,16,256]{3,2,1,0:T(8,128)(2,1)S(1)} %constant_dynamic-update-slice_fusion.4.carried, bf16[32,4096]{1,0:T(8,128)(2,1)S(1)} %constant_dynamic-update-slice_fusion.6.after.prompts, ...), custom_call_target="tpu_custom_call", output_to_operand_aliasing={{0}: (3, {})} | custom-call | bytes 1409024 | tf_op jit(solution)/shard_map/pallas_call | solution.py:201
  38.5 0.4 collective-permute-done.16
  38.8 0.3 collective-permute-start.17
  39.1 1.1 %collective-permute-done.17.far = bf16[8,2,16,256]{3,2,1,0:T(8,128)(2,1)S(1)} collective-permute-done((bf16[8,2,16,256]{3,2,1,0:T(8,128)(2,1)S(1)}, bf16[8,2,16,256]{3,2,1,0:T(8,128)(2,1)S(1)}, u32[]{:S(2)}, u32[]{:S(2)}) %collective-permute-start.17) | collective-permute-done | bytes 131104 | tf_op jit(solution)/shard_map/ppermute | solution.py:52
  40.2 0.0 collective-permute-done.18.others
  40.2 4.8 %shard_map.175 = (bf16[32,4096]{1,0:T(8,128)(2,1)S(1)}, f32[32,4096]{1,0:T(8,128)S(1)}) custom-call(bf16[8,2,16,256]{3,2,1,0:T(8,128)(2,1)S(1)} %constant_dynamic-update-slice_fusion.8.near, bf16[8,2,16,256]{3,2,1,0:T(8,128)(2,1)S(1)} %collective-permute-done.17.far, s32[64]{0:T(128)S(1)} %get-tuple-element.72.source, ...), custom_call_target="tpu_custom_call" | custom-call | flops 1082130432 | bytes 11272192 | tf_op jit(solution)/shard_map/pallas_call | solution.py:288
  45.0 0.3 collective-permute-start.19
  45.3 1.3 %collective-permute-done.19 = bf16[32,4096]{1,0:T(8,128)(2,1)S(1)} collective-permute-done((bf16[32,4096]{1,0:T(8,128)(2,1)S(1)}, bf16[32,4096]{1,0:T(8,128)(2,1)S(1)}, u32[]{:S(2)}, u32[]{:S(2)}) %collective-permute-start.19) | collective-permute-done | bytes 262176 | tf_op jit(solution)/shard_map/ppermute | solution.py:52
  46.7 1.7 %collective-permute-start.20 = (bf16[16,4096]{1,0:T(8,128)(2,1)S(1)}, bf16[16,4096]{1,0:T(8,128)(2,1)S(1)}, u32[]{:S(2)}, u32[]{:S(2)}) collective-permute-start(bf16[16,4096]{1,0:T(8,128)(2,1)S(1)} %slice.41), channel_id=1, source_target_pairs={{0,3},{1,4},{2,7},{3,0},{4,1},{5,6},{6,5},{7,2},{8,13},{9,10},{10,... | collective-permute-start | bytes 393224 | tf_op jit(solution)/shard_map/ppermute | solution.py:52
  48.4 2.7 %collective-permute-done.20 = bf16[16,4096]{1,0:T(8,128)(2,1)S(1)} collective-permute-done((bf16[16,4096]{1,0:T(8,128)(2,1)S(1)}, bf16[16,4096]{1,0:T(8,128)(2,1)S(1)}, u32[]{:S(2)}, u32[]{:S(2)}) %collective-permute-start.20) | collective-permute-done | bytes 131104 | tf_op jit(solution)/shard_map/ppermute | solution.py:52
  51.2 1.8 %collective-permute-start.21 = (bf16[8,4096]{1,0:T(8,128)(2,1)S(1)}, bf16[8,4096]{1,0:T(8,128)(2,1)S(1)}, u32[]{:S(2)}, u32[]{:S(2)}) collective-permute-start(bf16[8,4096]{1,0:T(8,128)(2,1)S(1)} %slice.42), channel_id=1, source_target_pairs={{0,5},{1,2},{2,1},{3,6},{4,7},{5,0},{6,3},{7,4},{8,11},{9,12},{10,... | collective-permute-start | bytes 196616 | tf_op jit(solution)/shard_map/ppermute | solution.py:52
  53.0 2.0 %collective-permute-done.21 = bf16[8,4096]{1,0:T(8,128)(2,1)S(1)} collective-permute-done((bf16[8,4096]{1,0:T(8,128)(2,1)S(1)}, bf16[8,4096]{1,0:T(8,128)(2,1)S(1)}, u32[]{:S(2)}, u32[]{:S(2)}) %collective-permute-start.21) | collective-permute-done | bytes 65568 | tf_op jit(solution)/shard_map/ppermute | solution.py:52
  55.0 2.2 %collective-permute-start.22 = (bf16[4,4096]{1,0:T(4,128)(2,1)S(1)}, bf16[4,4096]{1,0:T(4,128)(2,1)S(1)}, u32[]{:S(2)}, u32[]{:S(2)}) collective-permute-start(bf16[4,4096]{1,0:T(4,128)(2,1)S(1)} %slice.43), channel_id=1, source_target_pairs={{0,9},{1,8},{2,11},{3,10},{4,13},{5,12},{6,15},{7,14},{8,1},{9,0},... | collective-permute-start | bytes 98312 | tf_op jit(solution)/shard_map/ppermute | solution.py:52
  57.2 2.1 %collective-permute-done.22 = bf16[4,4096]{1,0:T(4,128)(2,1)S(1)} collective-permute-done((bf16[4,4096]{1,0:T(4,128)(2,1)S(1)}, bf16[4,4096]{1,0:T(4,128)(2,1)S(1)}, u32[]{:S(2)}, u32[]{:S(2)}) %collective-permute-start.22) | collective-permute-done | bytes 32800 | tf_op jit(solution)/shard_map/ppermute | solution.py:52
  59.3 0.6 %fusion = bf16[4,4096]{1,0:T(4,128)(2,1)} fusion(f32[8,4096]{1,0:T(8,128)S(1)} %slice_add_fusion.1, bf16[4,4096]{1,0:T(4,128)(2,1)S(1)} %collective-permute-done.22), kind=kLoop, calls=%fused_computation.11 | loop fusion | flops 49152 | bytes 131072 | tf_op jit(solution)/shard_map/convert_element_type | solution.py:480
  (23 shorter events, 0.3 us)
Async XLA Ops:
  0.0 8.9 %copy-start = (bf16[320,1280]{1,0:T(8,128)(2,1)S(1)}, bf16[320,1280]{1,0:T(8,128)(2,1)}, u32[]{:S(2)}) copy-start(bf16[320,1280]{1,0:T(8,128)(2,1)} %refs_3_.3) | copy-start | bytes 2457604
  0.0 10.6 %copy-start.1 = (bf16[320]{0:T(512)(128)(2,1)S(1)}, bf16[320]{0:T(512)(128)(2,1)}, u32[]{:S(2)}) copy-start(bf16[320]{0:T(512)(128)(2,1)} %refs_1_.3) | copy-start | bytes 1924
  0.0 5.6 %collective-permute-start = (bf16[4,1280]{1,0:T(4,128)(2,1)}, bf16[4,1280]{1,0:T(4,128)(2,1)S(1)}, u32[]{:S(2)}, u32[]{:S(2)}) collective-permute-start(bf16[4,1280]{1,0:T(4,128)(2,1)} %refs_0_.2), channel_id=1, source_target_pairs={{0,9},{1,8},{2,11},{3,10},{4,13},{5,12},{6,15},{7,14},{8,1},{9,0},... | collective-permute-start | bytes 30728 | tf_op jit(solution)/shard_map/ppermute | solution.py:52
  3.5 5.6 %collective-permute-start.2 = (bf16[4,4096]{1,0:T(4,128)(2,1)}, bf16[4,4096]{1,0:T(4,128)(2,1)S(1)}, u32[]{:S(2)}, u32[]{:S(2)}) collective-permute-start(bf16[4,4096]{1,0:T(4,128)(2,1)} %refs_1_.2), channel_id=1, source_target_pairs={{0,9},{1,8},{2,11},{3,10},{4,13},{5,12},{6,15},{7,14},{8,1},{9,0},... | collective-permute-start | bytes 98312 | tf_op jit(solution)/shard_map/ppermute | solution.py:52
  3.6 7.5 %collective-permute-start.3 = (bf16[1280,256]{1,0:T(8,128)(2,1)}, bf16[1280,256]{1,0:T(8,128)(2,1)S(1)}, u32[]{:S(2)}, u32[]{:S(2)}) collective-permute-start(bf16[1280,256]{1,0:T(8,128)(2,1)} %refs_6_.1), channel_id=1, source_target_pairs={{0,1},{1,0},{2,3},{3,2},{4,5},{5,4},{6,7},{7,6},{8,9},{9,8},{10,11... | collective-permute-start | bytes 1966088 | tf_op jit(solution)/shard_map/ppermute | solution.py:52
  4.2 6.4 %collective-permute-start.4 = (f32[256]{0:T(256)}, f32[256]{0:T(256)S(1)}, u32[]{:S(2)}, u32[]{:S(2)}) collective-permute-start(f32[256]{0:T(256)} %refs_7_.1), channel_id=1, source_target_pairs={{0,1},{1,0},{2,3},{3,2},{4,5},{5,4},{6,7},{7,6},{8,9},{9,8},{10,11... | collective-permute-start | bytes 3080 | tf_op jit(solution)/shard_map/ppermute | solution.py:52
  4.2 8.6 %collective-permute-start.7 = (bf16[320,1280]{1,0:T(8,128)(2,1)}, bf16[320,1280]{1,0:T(8,128)(2,1)S(1)}, u32[]{:S(2)}, u32[]{:S(2)}) collective-permute-start(bf16[320,1280]{1,0:T(8,128)(2,1)} %refs_2_.3), channel_id=1, source_target_pairs={{0,1},{1,0},{2,3},{3,2},{4,5},{5,4},{6,7},{7,6},{8,9},{9,8},{10,11... | collective-permute-start | bytes 2457608 | tf_op jit(solution)/shard_map/ppermute | solution.py:52
  5.6 3.3 %collective-permute-start.1 = (bf16[8,1280]{1,0:T(8,128)(2,1)S(1)}, bf16[8,1280]{1,0:T(8,128)(2,1)S(1)}, u32[]{:S(2)}, u32[]{:S(2)}) collective-permute-start(bf16[8,1280]{1,0:T(8,128)(2,1)S(1)} %pad_maximum_fusion.3.carried.after), channel_id=1, source_target_pairs={{0,5},{1,2},{2,1},{3,6},{4,7},{5,0},{6,3},{7,4},{8,11},{9,12},{10,... | collective-permute-start | bytes 61448 | tf_op jit(solution)/shard_map/ppermute | solution.py:52
  8.9 3.9 %collective-permute-start.8 = (bf16[320,1280]{1,0:T(8,128)(2,1)S(1)}, bf16[320,1280]{1,0:T(8,128)(2,1)S(1)}, u32[]{:S(2)}, u32[]{:S(2)}) collective-permute-start(bf16[320,1280]{1,0:T(8,128)(2,1)S(1)} %copy-done), channel_id=1, source_target_pairs={{0,1},{1,0},{2,3},{3,2},{4,5},{5,4},{6,7},{7,6},{8,9},{9,8},{10,11... | collective-permute-start | bytes 2457608 | tf_op jit(solution)/shard_map/ppermute | solution.py:52
  9.0 3.8 %collective-permute-start.5 = (bf16[16,1280]{1,0:T(8,128)(2,1)S(1)}, bf16[16,1280]{1,0:T(8,128)(2,1)S(1)}, u32[]{:S(2)}, u32[]{:S(2)}) collective-permute-start(bf16[16,1280]{1,0:T(8,128)(2,1)S(1)} %constant_dynamic-update-slice_fusion.refs_10_), channel_id=1, source_target_pairs={{0,3},{1,4},{2,7},{3,0},{4,1},{5,6},{6,5},{7,2},{8,13},{9,10},{10,... | collective-permute-start | bytes 122888 | tf_op jit(solution)/shard_map/ppermute | solution.py:52
  10.7 2.2 %collective-permute-start.6 = (bf16[320]{0:T(512)(128)(2,1)S(1)}, bf16[320]{0:T(512)(128)(2,1)S(1)}, u32[]{:S(2)}, u32[]{:S(2)}) collective-permute-start(bf16[320]{0:T(512)(128)(2,1)S(1)} %copy-done.1), channel_id=1, source_target_pairs={{0,1},{1,0},{2,3},{3,2},{4,5},{5,4},{6,7},{7,6},{8,9},{9,8},{10,11... | collective-permute-start | bytes 1928 | tf_op jit(solution)/shard_map/ppermute | solution.py:52
  14.2 3.5 %collective-permute-start.9 = (bf16[16,1280]{1,0:T(8,128)(2,1)S(1)}, bf16[16,1280]{1,0:T(8,128)(2,1)S(1)}, u32[]{:S(2)}, u32[]{:S(2)}) collective-permute-start(bf16[16,1280]{1,0:T(8,128)(2,1)S(1)} %convert_element_type.33), channel_id=1, source_target_pairs={{0,5},{1,2},{2,1},{3,6},{4,7},{5,0},{6,3},{7,4},{8,11},{9,12},{10,... | collective-permute-start | bytes 122888 | tf_op jit(solution)/shard_map/ppermute | solution.py:52
  17.1 5.8 %collective-permute-start.11 = (bf16[8,4096]{1,0:T(8,128)(2,1)S(1)}, bf16[8,4096]{1,0:T(8,128)(2,1)S(1)}, u32[]{:S(2)}, u32[]{:S(2)}) collective-permute-start(bf16[8,4096]{1,0:T(8,128)(2,1)S(1)} %pad_maximum_fusion.2.refs_11_), channel_id=1, source_target_pairs={{0,5},{1,2},{2,1},{3,6},{4,7},{5,0},{6,3},{7,4},{8,11},{9,12},{10,... | collective-permute-start | bytes 196616 | tf_op jit(solution)/shard_map/ppermute | solution.py:52
  17.7 5.3 %collective-permute-start.10 = (bf16[16,1280]{1,0:T(8,128)(2,1)S(1)}, bf16[16,1280]{1,0:T(8,128)(2,1)S(1)}, u32[]{:S(2)}, u32[]{:S(2)}) collective-permute-start(bf16[16,1280]{1,0:T(8,128)(2,1)S(1)} %get-tuple-element.81), channel_id=1, source_target_pairs={{0,9},{1,8},{2,11},{3,10},{4,13},{5,12},{6,15},{7,14},{8,1},{9,0},... | collective-permute-start | bytes 122888 | tf_op jit(solution)/shard_map/ppermute | solution.py:52
  23.0 3.5 %collective-permute-start.12 = (bf16[16,1280]{1,0:T(8,128)(2,1)S(1)}, bf16[16,1280]{1,0:T(8,128)(2,1)S(1)}, u32[]{:S(2)}, u32[]{:S(2)}) collective-permute-start(bf16[16,1280]{1,0:T(8,128)(2,1)S(1)} %get-tuple-element.60), channel_id=1, source_target_pairs={{0,3},{1,4},{2,7},{3,0},{4,1},{5,6},{6,5},{7,2},{8,13},{9,10},{10,... | collective-permute-start | bytes 122888 | tf_op jit(solution)/shard_map/ppermute | solution.py:52
  24.3 12.5 %collective-permute-start.15 = (bf16[16,4096]{1,0:T(8,128)(2,1)S(1)}, bf16[16,4096]{1,0:T(8,128)(2,1)S(1)}, u32[]{:S(2)}, u32[]{:S(2)}) collective-permute-start(bf16[16,4096]{1,0:T(8,128)(2,1)S(1)} %pad_maximum_fusion.after), channel_id=1, source_target_pairs={{0,3},{1,4},{2,7},{3,0},{4,1},{5,6},{6,5},{7,2},{8,13},{9,10},{10,... | collective-permute-start | bytes 393224 | tf_op jit(solution)/shard_map/ppermute | solution.py:52
  27.0 4.4 %collective-permute-start.13 = (bf16[1,2,16,256]{3,2,1,0:T(8,128)(2,1)S(1)}, bf16[1,2,16,256]{3,2,1,0:T(8,128)(2,1)S(1)}, u32[]{:S(2)}, u32[]{:S(2)}) collective-permute-start(bf16[1,2,16,256]{3,2,1,0:T(8,128)(2,1)S(1)} %shard_map.171.carried.after), channel_id=1, source_target_pairs={{0,9},{1,8},{2,11},{3,10},{4,13},{5,12},{6,15},{7,14},{8,1},{9,0},... | collective-permute-start | bytes 49160 | tf_op jit(solution)/shard_map/ppermute | solution.py:52
  31.4 3.7 %collective-permute-start.14 = (bf16[2,2,16,256]{3,2,1,0:T(8,128)(2,1)S(1)}, bf16[2,2,16,256]{3,2,1,0:T(8,128)(2,1)S(1)}, u32[]{:S(2)}, u32[]{:S(2)}) collective-permute-start(bf16[2,2,16,256]{3,2,1,0:T(8,128)(2,1)S(1)} %constant_dynamic-update-slice_fusion.2.carried.after), channel_id=1, source_target_pairs={{0,5},{1,2},{2,1},{3,6},{4,7},{5,0},{6,3},{7,4},{8,11},{9,12},{10,... | collective-permute-start | bytes 98312 | tf_op jit(solution)/shard_map/ppermute | solution.py:52
  35.1 3.7 %collective-permute-start.16 = (bf16[4,2,16,256]{3,2,1,0:T(8,128)(2,1)S(1)}, bf16[4,2,16,256]{3,2,1,0:T(8,128)(2,1)S(1)}, u32[]{:S(2)}, u32[]{:S(2)}) collective-permute-start(bf16[4,2,16,256]{3,2,1,0:T(8,128)(2,1)S(1)} %constant_dynamic-update-slice_fusion.4.carried), channel_id=1, source_target_pairs={{0,3},{1,4},{2,7},{3,0},{4,1},{5,6},{6,5},{7,2},{8,13},{9,10},{10,... | collective-permute-start | bytes 196616 | tf_op jit(solution)/shard_map/ppermute | solution.py:52
  36.8 3.4 %collective-permute-start.18 = (bf16[32,4096]{1,0:T(8,128)(2,1)S(1)}, bf16[32,4096]{1,0:T(8,128)(2,1)S(1)}, u32[]{:S(2)}, u32[]{:S(2)}) collective-permute-start(bf16[32,4096]{1,0:T(8,128)(2,1)S(1)} %constant_dynamic-update-slice_fusion.6.after.prompts), channel_id=1, source_target_pairs={{0,1},{1,0},{2,3},{3,2},{4,5},{5,4},{6,7},{7,6},{8,9},{9,8},{10,11... | collective-permute-start | bytes 786440 | tf_op jit(solution)/shard_map/ppermute | solution.py:52
  38.8 1.3 %collective-permute-start.17 = (bf16[8,2,16,256]{3,2,1,0:T(8,128)(2,1)S(1)}, bf16[8,2,16,256]{3,2,1,0:T(8,128)(2,1)S(1)}, u32[]{:S(2)}, u32[]{:S(2)}) collective-permute-start(bf16[8,2,16,256]{3,2,1,0:T(8,128)(2,1)S(1)} %constant_dynamic-update-slice_fusion.8.near), channel_id=1, source_target_pairs={{0,1},{1,0},{2,3},{3,2},{4,5},{5,4},{6,7},{7,6},{8,9},{9,8},{10,11... | collective-permute-start | bytes 393224 | tf_op jit(solution)/shard_map/ppermute | solution.py:52
  45.0 1.6 %collective-permute-start.19 = (bf16[32,4096]{1,0:T(8,128)(2,1)S(1)}, bf16[32,4096]{1,0:T(8,128)(2,1)S(1)}, u32[]{:S(2)}, u32[]{:S(2)}) collective-permute-start(bf16[32,4096]{1,0:T(8,128)(2,1)S(1)} %get-tuple-element.78), channel_id=1, source_target_pairs={{0,1},{1,0},{2,3},{3,2},{4,5},{5,4},{6,7},{7,6},{8,9},{9,8},{10,11... | collective-permute-start | bytes 786440 | tf_op jit(solution)/shard_map/ppermute | solution.py:52
  46.7 4.5 %collective-permute-start.20 = (bf16[16,4096]{1,0:T(8,128)(2,1)S(1)}, bf16[16,4096]{1,0:T(8,128)(2,1)S(1)}, u32[]{:S(2)}, u32[]{:S(2)}) collective-permute-start(bf16[16,4096]{1,0:T(8,128)(2,1)S(1)} %slice.41), channel_id=1, source_target_pairs={{0,3},{1,4},{2,7},{3,0},{4,1},{5,6},{6,5},{7,2},{8,13},{9,10},{10,... | collective-permute-start | bytes 393224 | tf_op jit(solution)/shard_map/ppermute | solution.py:52
  51.2 3.8 %collective-permute-start.21 = (bf16[8,4096]{1,0:T(8,128)(2,1)S(1)}, bf16[8,4096]{1,0:T(8,128)(2,1)S(1)}, u32[]{:S(2)}, u32[]{:S(2)}) collective-permute-start(bf16[8,4096]{1,0:T(8,128)(2,1)S(1)} %slice.42), channel_id=1, source_target_pairs={{0,5},{1,2},{2,1},{3,6},{4,7},{5,0},{6,3},{7,4},{8,11},{9,12},{10,... | collective-permute-start | bytes 196616 | tf_op jit(solution)/shard_map/ppermute | solution.py:52
  55.0 4.3 %collective-permute-start.22 = (bf16[4,4096]{1,0:T(4,128)(2,1)S(1)}, bf16[4,4096]{1,0:T(4,128)(2,1)S(1)}, u32[]{:S(2)}, u32[]{:S(2)}) collective-permute-start(bf16[4,4096]{1,0:T(4,128)(2,1)S(1)} %slice.43), channel_id=1, source_target_pairs={{0,9},{1,8},{2,11},{3,10},{4,13},{5,12},{6,15},{7,14},{8,1},{9,0},... | collective-permute-start | bytes 98312 | tf_op jit(solution)/shard_map/ppermute | solution.py:52

commit v8 on v7

--- a/solution.py
+++ b/solution.py
@@ -258,12 +258,11 @@
         value = jnp.where(audio_row, found, prompt.astype(jnp.float32))
         squares += value * value
         packed[:, part] = value.astype(jnp.bfloat16)
+        normed[:, part] = (value * row(gain, part)).astype(jnp.bfloat16)
     scale = lax.rsqrt(jnp.sum(squares, axis=1, keepdims=True) / width + 1e-06)
-    for device in range(count):
-        part = slice(device * columns, (device + 1) * columns)
-        value = packed[:, part].astype(jnp.float32) * scale * row(gain, part)
-        normed[:, part] = value.astype(jnp.bfloat16)
+    scale = jnp.broadcast_to(scale, (rows, 128)).T[:1, :]
     gated, lifted = dot_last(gate[...], normed[...]), dot_last(up[...], normed[...])
+    gated, lifted = gated * scale, lifted * scale
     hidden = (gated * jax.nn.sigmoid(gated) * lifted).T.astype(jnp.bfloat16)
     held = lax.broadcasted_iota(jnp.int32, (half, 1), 0) < own
     pieces = 4

time: 60.4 us -> 60.2 us (level)
  no operation moved by 1% of the time
where the time goes in v8:
time: 60.2 us; the launch traced here: 59.7 us
  starting transfers between devices  28.5 us (47%)
  Pallas kernels  19.8 us (33%)
  waiting for transfers between devices  10.2 us (17%)
  other arithmetic  0.84 us (1%)
    ppermute x23, starting transfers between devices, swap(): return lax.ppermute(value, 'tp', pairs)  28.5 us
    pallas_call x7, Pallas kernels, fetch(): pl.pallas_call(functools.partial(fetch_kernel, start, width), out_shape=[...  10.9 us
    ppermute x23, waiting for transfers between devices, swap(): return lax.ppermute(value, 'tp', pairs)  10.2 us
    pallas_call x1, Pallas kernels, language(): pl.pallas_call(functools.partial(language_kernel, bits), out_shape=[jax.S...  4.62 us
    pallas_call x2, Pallas kernels, stage(): pl.pallas_call(functools.partial(stage_kernel, count, len(after), carry),...  2.55 us
    pallas_call x1, Pallas kernels, encoder(): pl.pallas_call(functools.partial(encoder_kernel, bits), out_shape=[jax.Sh...  1.26 us
  transfers between devices with their start and end apart: 23, of which 9 were waited for; matrix products, arithmetic and copies ran while one was open for 0% of the time, Pallas kernels for 23%

profile of v8, /device:TPU:0, one launch (start us, length us, event | category | flops | bytes accessed | tf_op | source)
XLA Modules:
  0.0 59.7 jit_solution(7341578588682013501)
XLA Ops:
  0.0 0.0 copy-start
  0.0 0.0 copy-start.1
  0.0 3.5 %collective-permute-start = (bf16[4,1280]{1,0:T(4,128)(2,1)}, bf16[4,1280]{1,0:T(4,128)(2,1)S(1)}, u32[]{:S(2)}, u32[]{:S(2)}) collective-permute-start(bf16[4,1280]{1,0:T(4,128)(2,1)} %refs_0_.2), channel_id=1, source_target_pairs={{0,9},{1,8},{2,11},{3,10},{4,13},{5,12},{6,15},{7,14},{8,1},{9,0},... | collective-permute-start | bytes 30728 | tf_op jit(solution)/shard_map/ppermute | solution.py:52
  3.5 0.1 collective-permute-start.2
  3.6 0.7 %collective-permute-start.3 = (bf16[1280,256]{1,0:T(8,128)(2,1)}, bf16[1280,256]{1,0:T(8,128)(2,1)S(1)}, u32[]{:S(2)}, u32[]{:S(2)}) collective-permute-start(bf16[1280,256]{1,0:T(8,128)(2,1)} %refs_6_.1), channel_id=1, source_target_pairs={{0,1},{1,0},{2,3},{3,2},{4,5},{5,4},{6,7},{7,6},{8,9},{9,8},{10,11... | collective-permute-start | bytes 1966088 | tf_op jit(solution)/shard_map/ppermute | solution.py:52
  4.2 0.0 collective-permute-start.4
  4.2 0.5 collective-permute-start.7
  4.7 0.8 %shard_map.163 = (bf16[4,1280]{1,0:T(4,128)(2,1)S(1)}, bf16[4,4096]{1,0:T(4,128)(2,1)S(1)}, f32[1280]{0:T(1024)S(1)}, f32[1280]{0:T(1024)S(1)}) custom-call(bf16[4,1280]{1,0:T(4,128)(2,1)} %refs_0_.2, bf16[4,4096]{1,0:T(4,128)(2,1)} %refs_1_.2, f32[1280]{0:T(1024)} %refs_2_.2, f32[1280]{0:T(1024)} %refs_3_.2), custom_call_target="tpu_custom_call" | custom-call | bytes 48128 | tf_op jit(solution)/shard_map/pallas_call | solution.py:173
  5.6 0.0 collective-permute-done
  5.6 1.6 %collective-permute-start.1 = (bf16[8,1280]{1,0:T(8,128)(2,1)S(1)}, bf16[8,1280]{1,0:T(8,128)(2,1)S(1)}, u32[]{:S(2)}, u32[]{:S(2)}) collective-permute-start(bf16[8,1280]{1,0:T(8,128)(2,1)S(1)} %pad_maximum_fusion.3.carried.after), channel_id=1, source_target_pairs={{0,5},{1,2},{2,1},{3,6},{4,7},{5,0},{6,3},{7,4},{8,11},{9,12},{10,... | collective-permute-start | bytes 61448 | tf_op jit(solution)/shard_map/ppermute | solution.py:52
  7.2 1.4 %shard_map.164 = (bf16[688,4096]{1,0:T(8,128)(2,1)S(1)}, bf16[8,1280]{1,0:T(8,128)(2,1)S(1)}) custom-call(bf16[8,1280]{1,0:T(8,128)(2,1)S(1)} %pad_maximum_fusion.3.carried.after, bf16[8,1280]{1,0:T(8,128)(2,1)S(1)} %pad_maximum_fusion.3.carried.after, bf16[688,4096]{1,0:T(8,128)(2,1)} %bitcast.5), custom_call_target="tpu_custom_call" | custom-call | bytes 1409024 | tf_op jit(solution)/shard_map/pallas_call | solution.py:201
  8.6 0.3 collective-permute-done.1
  8.9 0.0 copy-done
  8.9 0.1 collective-permute-start.8
  9.0 0.0 collective-permute-done.2
  9.0 1.5 %collective-permute-start.5 = (bf16[16,1280]{1,0:T(8,128)(2,1)S(1)}, bf16[16,1280]{1,0:T(8,128)(2,1)S(1)}, u32[]{:S(2)}, u32[]{:S(2)}) collective-permute-start(bf16[16,1280]{1,0:T(8,128)(2,1)S(1)} %constant_dynamic-update-slice_fusion.refs_10_), channel_id=1, source_target_pairs={{0,3},{1,4},{2,7},{3,0},{4,1},{5,6},{6,5},{7,2},{8,13},{9,10},{10,... | collective-permute-start | bytes 122888 | tf_op jit(solution)/shard_map/ppermute | solution.py:52
  10.6 0.0 collective-permute-done.4.refs_13_.bias_pair
  10.6 0.0 copy-done.1
  10.7 0.4 collective-permute-start.6
  11.1 0.0 collective-permute-done.3.refs_12_.weight_pair
  11.1 1.7 %shard_map.165 = (f32[1280]{0:T(1024)S(1)}, bf16[320]{0:T(512)(128)(2,1)S(1)}, bf16[320,1280]{1,0:T(8,128)(2,1)S(1)}, bf16[320,1280]{1,0:T(8,128)(2,1)S(1)}, f32...) custom-call(f32[1280]{0:T(1024)} %refs_0_.3, ...), custom_call_target="tpu_custom_call" | custom-call | bytes 2310912 | tf_op jit(solution)/shard_map/pallas_call | solution.py:173
  12.8 0.0 collective-permute-done.5
  12.8 0.0 collective-permute-done.6.bias_pair
  12.9 0.0 collective-permute-done.7.up_pair
  12.9 0.0 collective-permute-done.8.down_pair
  12.9 1.3 %shard_map.166 = (f32[16,1280]{1,0:T(8,128)S(1)}, f32[16,1280]{1,0:T(8,128)S(1)}) custom-call(bf16[32,1280]{1,0:T(8,128)(2,1)S(1)} %pad_maximum_fusion.1.frames, f32[1280]{0:T(1024)S(1)} %get-tuple-element.46.gain, f32[1280]{0:T(1024)S(1)} %get-tuple-element.47.shift, f32[1280]{0:T(1024)S(1)} %get-tuple-element.48.down_bias, ...), custom_call_target="tpu_custom_call" | custom-call | flops 104857600 | bytes 3276800 | tf_op jit(solution)/shard_map/pallas_call | solution.py:105
  14.2 1.3 %collective-permute-start.9 = (bf16[16,1280]{1,0:T(8,128)(2,1)S(1)}, bf16[16,1280]{1,0:T(8,128)(2,1)S(1)}, u32[]{:S(2)}, u32[]{:S(2)}) collective-permute-start(bf16[16,1280]{1,0:T(8,128)(2,1)S(1)} %convert_element_type.33), channel_id=1, source_target_pairs={{0,5},{1,2},{2,1},{3,6},{4,7},{5,0},{6,3},{7,4},{8,11},{9,12},{10,... | collective-permute-start | bytes 122888 | tf_op jit(solution)/shard_map/ppermute | solution.py:52
  15.5 1.6 %shard_map.167 = (bf16[688,4096]{1,0:T(8,128)(2,1)S(1)}, f32[16,1280]{1,0:T(8,128)S(1)}) custom-call(f32[16,1280]{1,0:T(8,128)S(1)} %get-tuple-element.52.carried.after, f32[16,1280]{1,0:T(8,128)S(1)} %get-tuple-element.52.carried.after, bf16[688,4096]{1,0:T(8,128)(2,1)} %bitcast.2), custom_call_target="tpu_custom_call" | custom-call | bytes 2113536 | tf_op jit(solution)/shard_map/pallas_call | solution.py:201
  17.1 0.6 collective-permute-start.11
  17.7 0.0 collective-permute-done.9
  17.7 3.4 %collective-permute-start.10 = (bf16[16,1280]{1,0:T(8,128)(2,1)S(1)}, bf16[16,1280]{1,0:T(8,128)(2,1)S(1)}, u32[]{:S(2)}, u32[]{:S(2)}) collective-permute-start(bf16[16,1280]{1,0:T(8,128)(2,1)S(1)} %get-tuple-element.81), channel_id=1, source_target_pairs={{0,9},{1,8},{2,11},{3,10},{4,13},{5,12},{6,15},{7,14},{8,1},{9,0},... | collective-permute-start | bytes 122888 | tf_op jit(solution)/shard_map/ppermute | solution.py:52
  21.1 1.8 %shard_map.168 = (bf16[688,4096]{1,0:T(8,128)(2,1)S(1)}, f32[16,1280]{1,0:T(8,128)S(1)}) custom-call(f32[16,1280]{1,0:T(8,128)S(1)} %get-tuple-element.82.carried.after, f32[16,1280]{1,0:T(8,128)S(1)} %get-tuple-element.82.carried.after, bf16[688,4096]{1,0:T(8,128)(2,1)} %bitcast.6, ...), custom_call_target="tpu_custom_call", output_to_operand_aliasing={{0}: (3, {})} | custom-call | bytes 2818048 | tf_op jit(solution)/shard_map/pallas_call | solution.py:201
  22.9 0.0 collective-permute-done.11
  22.9 0.1 collective-permute-done.10
  23.0 1.3 %collective-permute-start.12 = (bf16[16,1280]{1,0:T(8,128)(2,1)S(1)}, bf16[16,1280]{1,0:T(8,128)(2,1)S(1)}, u32[]{:S(2)}, u32[]{:S(2)}) collective-permute-start(bf16[16,1280]{1,0:T(8,128)(2,1)S(1)} %get-tuple-element.60), channel_id=1, source_target_pairs={{0,3},{1,4},{2,7},{3,0},{4,1},{5,6},{6,5},{7,2},{8,13},{9,10},{10,... | collective-permute-start | bytes 122888 | tf_op jit(solution)/shard_map/ppermute | solution.py:52
  24.3 0.6 %collective-permute-start.15 = (bf16[16,4096]{1,0:T(8,128)(2,1)S(1)}, bf16[16,4096]{1,0:T(8,128)(2,1)S(1)}, u32[]{:S(2)}, u32[]{:S(2)}) collective-permute-start(bf16[16,4096]{1,0:T(8,128)(2,1)S(1)} %pad_maximum_fusion.after), channel_id=1, source_target_pairs={{0,3},{1,4},{2,7},{3,0},{4,1},{5,6},{6,5},{7,2},{8,13},{9,10},{10,... | collective-permute-start | bytes 393224 | tf_op jit(solution)/shard_map/ppermute | solution.py:52
  24.9 1.6 %shard_map.169 = (bf16[688,4096]{1,0:T(8,128)(2,1)S(1)}, f32[16,1280]{1,0:T(8,128)S(1)}) custom-call(f32[16,1280]{1,0:T(8,128)S(1)} %get-tuple-element.80.carried.after, f32[16,1280]{1,0:T(8,128)S(1)} %get-tuple-element.80.carried.after, bf16[688,4096]{1,0:T(8,128)(2,1)} %bitcast.3, ...), custom_call_target="tpu_custom_call", output_to_operand_aliasing={{0}: (3, {})} | custom-call | bytes 2113536 | tf_op jit(solution)/shard_map/pallas_call | solution.py:201
  26.5 0.0 collective-permute-done.12.arrived
  26.5 0.2 shard_map.170.post
  26.7 0.3 shard_map.171.carried.after
  27.0 2.6 %collective-permute-start.13 = (bf16[1,2,16,256]{3,2,1,0:T(8,128)(2,1)S(1)}, bf16[1,2,16,256]{3,2,1,0:T(8,128)(2,1)S(1)}, u32[]{:S(2)}, u32[]{:S(2)}) collective-permute-start(bf16[1,2,16,256]{3,2,1,0:T(8,128)(2,1)S(1)} %shard_map.171.carried.after), channel_id=1, source_target_pairs={{0,9},{1,8},{2,11},{3,10},{4,13},{5,12},{6,15},{7,14},{8,1},{9,0},... | collective-permute-start | bytes 49160 | tf_op jit(solution)/shard_map/ppermute | solution.py:52
  29.6 1.8 %shard_map.172 = (bf16[688,4096]{1,0:T(8,128)(2,1)S(1)}, bf16[1,2,16,256]{3,2,1,0:T(8,128)(2,1)S(1)}) custom-call(bf16[1,2,16,256]{3,2,1,0:T(8,128)(2,1)S(1)} %shard_map.171.carried.after, bf16[1,2,16,256]{3,2,1,0:T(8,128)(2,1)S(1)} %shard_map.171.carried.after, bf16[688,4096]{1,0:T(8,128)(2,1)} %down_hbm.1), custom_call_target="tpu_custom_call" | custom-call | bytes 2818048 | tf_op jit(solution)/shard_map/pallas_call | solution.py:201
  31.4 0.0 collective-permute-done.13
  31.4 2.1 %collective-permute-start.14 = (bf16[2,2,16,256]{3,2,1,0:T(8,128)(2,1)S(1)}, bf16[2,2,16,256]{3,2,1,0:T(8,128)(2,1)S(1)}, u32[]{:S(2)}, u32[]{:S(2)}) collective-permute-start(bf16[2,2,16,256]{3,2,1,0:T(8,128)(2,1)S(1)} %constant_dynamic-update-slice_fusion.2.carried.after), channel_id=1, source_target_pairs={{0,5},{1,2},{2,1},{3,6},{4,7},{5,0},{6,3},{7,4},{8,11},{9,12},{10,... | collective-permute-start | bytes 98312 | tf_op jit(solution)/shard_map/ppermute | solution.py:52
  33.5 1.4 %shard_map.173 = (bf16[688,4096]{1,0:T(8,128)(2,1)S(1)}, bf16[2,2,16,256]{3,2,1,0:T(8,128)(2,1)S(1)}) custom-call(bf16[2,2,16,256]{3,2,1,0:T(8,128)(2,1)S(1)} %constant_dynamic-update-slice_fusion.2.carried.after, bf16[2,2,16,256]{3,2,1,0:T(8,128)(2,1)S(1)} %constant_dynamic-update-slice_fusion.2.carried.after, ...), custom_call_target="tpu_custom_call", output_to_operand_aliasing={{0}: (3, {})} | custom-call | bytes 1409024 | tf_op jit(solution)/shard_map/pallas_call | solution.py:201
  34.9 0.2 collective-permute-done.14
  35.1 1.6 %collective-permute-start.16 = (bf16[4,2,16,256]{3,2,1,0:T(8,128)(2,1)S(1)}, bf16[4,2,16,256]{3,2,1,0:T(8,128)(2,1)S(1)}, u32[]{:S(2)}, u32[]{:S(2)}) collective-permute-start(bf16[4,2,16,256]{3,2,1,0:T(8,128)(2,1)S(1)} %constant_dynamic-update-slice_fusion.4.carried), channel_id=1, source_target_pairs={{0,3},{1,4},{2,7},{3,0},{4,1},{5,6},{6,5},{7,2},{8,13},{9,10},{10,... | collective-permute-start | bytes 196616 | tf_op jit(solution)/shard_map/ppermute | solution.py:52
  36.7 0.0 collective-permute-done.15
  36.8 0.3 collective-permute-start.18
  37.1 1.4 %shard_map.174 = (bf16[688,4096]{1,0:T(8,128)(2,1)S(1)}, bf16[4,2,16,256]{3,2,1,0:T(8,128)(2,1)S(1)}) custom-call(bf16[4,2,16,256]{3,2,1,0:T(8,128)(2,1)S(1)} %constant_dynamic-update-slice_fusion.4.carried, bf16[32,4096]{1,0:T(8,128)(2,1)S(1)} %constant_dynamic-update-slice_fusion.6.after.prompts, ...), custom_call_target="tpu_custom_call", output_to_operand_aliasing={{0}: (3, {})} | custom-call | bytes 1409024 | tf_op jit(solution)/shard_map/pallas_call | solution.py:201
  38.5 0.4 collective-permute-done.16
  38.8 0.3 collective-permute-start.17
  39.1 1.1 %collective-permute-done.17.far = bf16[8,2,16,256]{3,2,1,0:T(8,128)(2,1)S(1)} collective-permute-done((bf16[8,2,16,256]{3,2,1,0:T(8,128)(2,1)S(1)}, bf16[8,2,16,256]{3,2,1,0:T(8,128)(2,1)S(1)}, u32[]{:S(2)}, u32[]{:S(2)}) %collective-permute-start.17) | collective-permute-done | bytes 131104 | tf_op jit(solution)/shard_map/ppermute | solution.py:52
  40.2 0.0 collective-permute-done.18.others
  40.2 4.6 %shard_map.175 = (bf16[32,4096]{1,0:T(8,128)(2,1)S(1)}, f32[32,4096]{1,0:T(8,128)S(1)}) custom-call(bf16[8,2,16,256]{3,2,1,0:T(8,128)(2,1)S(1)} %constant_dynamic-update-slice_fusion.8.near, bf16[8,2,16,256]{3,2,1,0:T(8,128)(2,1)S(1)} %collective-permute-done.17.far, s32[64]{0:T(128)S(1)} %get-tuple-element.72.source, ...), custom_call_target="tpu_custom_call" | custom-call | flops 1082130432 | bytes 11272192 | tf_op jit(solution)/shard_map/pallas_call | solution.py:287
  44.8 0.3 collective-permute-start.19
  45.2 1.3 %collective-permute-done.19 = bf16[32,4096]{1,0:T(8,128)(2,1)S(1)} collective-permute-done((bf16[32,4096]{1,0:T(8,128)(2,1)S(1)}, bf16[32,4096]{1,0:T(8,128)(2,1)S(1)}, u32[]{:S(2)}, u32[]{:S(2)}) %collective-permute-start.19) | collective-permute-done | bytes 262176 | tf_op jit(solution)/shard_map/ppermute | solution.py:52
  46.5 1.7 %collective-permute-start.20 = (bf16[16,4096]{1,0:T(8,128)(2,1)S(1)}, bf16[16,4096]{1,0:T(8,128)(2,1)S(1)}, u32[]{:S(2)}, u32[]{:S(2)}) collective-permute-start(bf16[16,4096]{1,0:T(8,128)(2,1)S(1)} %slice.41), channel_id=1, source_target_pairs={{0,3},{1,4},{2,7},{3,0},{4,1},{5,6},{6,5},{7,2},{8,13},{9,10},{10,... | collective-permute-start | bytes 393224 | tf_op jit(solution)/shard_map/ppermute | solution.py:52
  48.2 2.8 %collective-permute-done.20 = bf16[16,4096]{1,0:T(8,128)(2,1)S(1)} collective-permute-done((bf16[16,4096]{1,0:T(8,128)(2,1)S(1)}, bf16[16,4096]{1,0:T(8,128)(2,1)S(1)}, u32[]{:S(2)}, u32[]{:S(2)}) %collective-permute-start.20) | collective-permute-done | bytes 131104 | tf_op jit(solution)/shard_map/ppermute | solution.py:52
  51.0 1.8 %collective-permute-start.21 = (bf16[8,4096]{1,0:T(8,128)(2,1)S(1)}, bf16[8,4096]{1,0:T(8,128)(2,1)S(1)}, u32[]{:S(2)}, u32[]{:S(2)}) collective-permute-start(bf16[8,4096]{1,0:T(8,128)(2,1)S(1)} %slice.42), channel_id=1, source_target_pairs={{0,5},{1,2},{2,1},{3,6},{4,7},{5,0},{6,3},{7,4},{8,11},{9,12},{10,... | collective-permute-start | bytes 196616 | tf_op jit(solution)/shard_map/ppermute | solution.py:52
  52.8 2.0 %collective-permute-done.21 = bf16[8,4096]{1,0:T(8,128)(2,1)S(1)} collective-permute-done((bf16[8,4096]{1,0:T(8,128)(2,1)S(1)}, bf16[8,4096]{1,0:T(8,128)(2,1)S(1)}, u32[]{:S(2)}, u32[]{:S(2)}) %collective-permute-start.21) | collective-permute-done | bytes 65568 | tf_op jit(solution)/shard_map/ppermute | solution.py:52
  54.8 2.2 %collective-permute-start.22 = (bf16[4,4096]{1,0:T(4,128)(2,1)S(1)}, bf16[4,4096]{1,0:T(4,128)(2,1)S(1)}, u32[]{:S(2)}, u32[]{:S(2)}) collective-permute-start(bf16[4,4096]{1,0:T(4,128)(2,1)S(1)} %slice.43), channel_id=1, source_target_pairs={{0,9},{1,8},{2,11},{3,10},{4,13},{5,12},{6,15},{7,14},{8,1},{9,0},... | collective-permute-start | bytes 98312 | tf_op jit(solution)/shard_map/ppermute | solution.py:52
  57.0 2.1 %collective-permute-done.22 = bf16[4,4096]{1,0:T(4,128)(2,1)S(1)} collective-permute-done((bf16[4,4096]{1,0:T(4,128)(2,1)S(1)}, bf16[4,4096]{1,0:T(4,128)(2,1)S(1)}, u32[]{:S(2)}, u32[]{:S(2)}) %collective-permute-start.22) | collective-permute-done | bytes 32800 | tf_op jit(solution)/shard_map/ppermute | solution.py:52
  59.1 0.6 %fusion = bf16[4,4096]{1,0:T(4,128)(2,1)} fusion(f32[8,4096]{1,0:T(8,128)S(1)} %slice_add_fusion.1, bf16[4,4096]{1,0:T(4,128)(2,1)S(1)} %collective-permute-done.22), kind=kLoop, calls=%fused_computation.11 | loop fusion | flops 49152 | bytes 131072 | tf_op jit(solution)/shard_map/convert_element_type | solution.py:479
  (23 shorter events, 0.3 us)
Async XLA Ops:
  0.0 8.9 %copy-start = (bf16[320,1280]{1,0:T(8,128)(2,1)S(1)}, bf16[320,1280]{1,0:T(8,128)(2,1)}, u32[]{:S(2)}) copy-start(bf16[320,1280]{1,0:T(8,128)(2,1)} %refs_3_.3) | copy-start | bytes 2457604
  0.0 10.6 %copy-start.1 = (bf16[320]{0:T(512)(128)(2,1)S(1)}, bf16[320]{0:T(512)(128)(2,1)}, u32[]{:S(2)}) copy-start(bf16[320]{0:T(512)(128)(2,1)} %refs_1_.3) | copy-start | bytes 1924
  0.0 5.6 %collective-permute-start = (bf16[4,1280]{1,0:T(4,128)(2,1)}, bf16[4,1280]{1,0:T(4,128)(2,1)S(1)}, u32[]{:S(2)}, u32[]{:S(2)}) collective-permute-start(bf16[4,1280]{1,0:T(4,128)(2,1)} %refs_0_.2), channel_id=1, source_target_pairs={{0,9},{1,8},{2,11},{3,10},{4,13},{5,12},{6,15},{7,14},{8,1},{9,0},... | collective-permute-start | bytes 30728 | tf_op jit(solution)/shard_map/ppermute | solution.py:52
  3.5 5.6 %collective-permute-start.2 = (bf16[4,4096]{1,0:T(4,128)(2,1)}, bf16[4,4096]{1,0:T(4,128)(2,1)S(1)}, u32[]{:S(2)}, u32[]{:S(2)}) collective-permute-start(bf16[4,4096]{1,0:T(4,128)(2,1)} %refs_1_.2), channel_id=1, source_target_pairs={{0,9},{1,8},{2,11},{3,10},{4,13},{5,12},{6,15},{7,14},{8,1},{9,0},... | collective-permute-start | bytes 98312 | tf_op jit(solution)/shard_map/ppermute | solution.py:52
  3.6 7.5 %collective-permute-start.3 = (bf16[1280,256]{1,0:T(8,128)(2,1)}, bf16[1280,256]{1,0:T(8,128)(2,1)S(1)}, u32[]{:S(2)}, u32[]{:S(2)}) collective-permute-start(bf16[1280,256]{1,0:T(8,128)(2,1)} %refs_6_.1), channel_id=1, source_target_pairs={{0,1},{1,0},{2,3},{3,2},{4,5},{5,4},{6,7},{7,6},{8,9},{9,8},{10,11... | collective-permute-start | bytes 1966088 | tf_op jit(solution)/shard_map/ppermute | solution.py:52
  4.2 6.4 %collective-permute-start.4 = (f32[256]{0:T(256)}, f32[256]{0:T(256)S(1)}, u32[]{:S(2)}, u32[]{:S(2)}) collective-permute-start(f32[256]{0:T(256)} %refs_7_.1), channel_id=1, source_target_pairs={{0,1},{1,0},{2,3},{3,2},{4,5},{5,4},{6,7},{7,6},{8,9},{9,8},{10,11... | collective-permute-start | bytes 3080 | tf_op jit(solution)/shard_map/ppermute | solution.py:52
  4.2 8.6 %collective-permute-start.7 = (bf16[320,1280]{1,0:T(8,128)(2,1)}, bf16[320,1280]{1,0:T(8,128)(2,1)S(1)}, u32[]{:S(2)}, u32[]{:S(2)}) collective-permute-start(bf16[320,1280]{1,0:T(8,128)(2,1)} %refs_2_.3), channel_id=1, source_target_pairs={{0,1},{1,0},{2,3},{3,2},{4,5},{5,4},{6,7},{7,6},{8,9},{9,8},{10,11... | collective-permute-start | bytes 2457608 | tf_op jit(solution)/shard_map/ppermute | solution.py:52
  5.6 3.3 %collective-permute-start.1 = (bf16[8,1280]{1,0:T(8,128)(2,1)S(1)}, bf16[8,1280]{1,0:T(8,128)(2,1)S(1)}, u32[]{:S(2)}, u32[]{:S(2)}) collective-permute-start(bf16[8,1280]{1,0:T(8,128)(2,1)S(1)} %pad_maximum_fusion.3.carried.after), channel_id=1, source_target_pairs={{0,5},{1,2},{2,1},{3,6},{4,7},{5,0},{6,3},{7,4},{8,11},{9,12},{10,... | collective-permute-start | bytes 61448 | tf_op jit(solution)/shard_map/ppermute | solution.py:52
  8.9 3.9 %collective-permute-start.8 = (bf16[320,1280]{1,0:T(8,128)(2,1)S(1)}, bf16[320,1280]{1,0:T(8,128)(2,1)S(1)}, u32[]{:S(2)}, u32[]{:S(2)}) collective-permute-start(bf16[320,1280]{1,0:T(8,128)(2,1)S(1)} %copy-done), channel_id=1, source_target_pairs={{0,1},{1,0},{2,3},{3,2},{4,5},{5,4},{6,7},{7,6},{8,9},{9,8},{10,11... | collective-permute-start | bytes 2457608 | tf_op jit(solution)/shard_map/ppermute | solution.py:52
  9.0 3.8 %collective-permute-start.5 = (bf16[16,1280]{1,0:T(8,128)(2,1)S(1)}, bf16[16,1280]{1,0:T(8,128)(2,1)S(1)}, u32[]{:S(2)}, u32[]{:S(2)}) collective-permute-start(bf16[16,1280]{1,0:T(8,128)(2,1)S(1)} %constant_dynamic-update-slice_fusion.refs_10_), channel_id=1, source_target_pairs={{0,3},{1,4},{2,7},{3,0},{4,1},{5,6},{6,5},{7,2},{8,13},{9,10},{10,... | collective-permute-start | bytes 122888 | tf_op jit(solution)/shard_map/ppermute | solution.py:52
  10.7 2.2 %collective-permute-start.6 = (bf16[320]{0:T(512)(128)(2,1)S(1)}, bf16[320]{0:T(512)(128)(2,1)S(1)}, u32[]{:S(2)}, u32[]{:S(2)}) collective-permute-start(bf16[320]{0:T(512)(128)(2,1)S(1)} %copy-done.1), channel_id=1, source_target_pairs={{0,1},{1,0},{2,3},{3,2},{4,5},{5,4},{6,7},{7,6},{8,9},{9,8},{10,11... | collective-permute-start | bytes 1928 | tf_op jit(solution)/shard_map/ppermute | solution.py:52
  14.2 3.5 %collective-permute-start.9 = (bf16[16,1280]{1,0:T(8,128)(2,1)S(1)}, bf16[16,1280]{1,0:T(8,128)(2,1)S(1)}, u32[]{:S(2)}, u32[]{:S(2)}) collective-permute-start(bf16[16,1280]{1,0:T(8,128)(2,1)S(1)} %convert_element_type.33), channel_id=1, source_target_pairs={{0,5},{1,2},{2,1},{3,6},{4,7},{5,0},{6,3},{7,4},{8,11},{9,12},{10,... | collective-permute-start | bytes 122888 | tf_op jit(solution)/shard_map/ppermute | solution.py:52
  17.1 5.8 %collective-permute-start.11 = (bf16[8,4096]{1,0:T(8,128)(2,1)S(1)}, bf16[8,4096]{1,0:T(8,128)(2,1)S(1)}, u32[]{:S(2)}, u32[]{:S(2)}) collective-permute-start(bf16[8,4096]{1,0:T(8,128)(2,1)S(1)} %pad_maximum_fusion.2.refs_11_), channel_id=1, source_target_pairs={{0,5},{1,2},{2,1},{3,6},{4,7},{5,0},{6,3},{7,4},{8,11},{9,12},{10,... | collective-permute-start | bytes 196616 | tf_op jit(solution)/shard_map/ppermute | solution.py:52
  17.7 5.3 %collective-permute-start.10 = (bf16[16,1280]{1,0:T(8,128)(2,1)S(1)}, bf16[16,1280]{1,0:T(8,128)(2,1)S(1)}, u32[]{:S(2)}, u32[]{:S(2)}) collective-permute-start(bf16[16,1280]{1,0:T(8,128)(2,1)S(1)} %get-tuple-element.81), channel_id=1, source_target_pairs={{0,9},{1,8},{2,11},{3,10},{4,13},{5,12},{6,15},{7,14},{8,1},{9,0},... | collective-permute-start | bytes 122888 | tf_op jit(solution)/shard_map/ppermute | solution.py:52
  23.0 3.5 %collective-permute-start.12 = (bf16[16,1280]{1,0:T(8,128)(2,1)S(1)}, bf16[16,1280]{1,0:T(8,128)(2,1)S(1)}, u32[]{:S(2)}, u32[]{:S(2)}) collective-permute-start(bf16[16,1280]{1,0:T(8,128)(2,1)S(1)} %get-tuple-element.60), channel_id=1, source_target_pairs={{0,3},{1,4},{2,7},{3,0},{4,1},{5,6},{6,5},{7,2},{8,13},{9,10},{10,... | collective-permute-start | bytes 122888 | tf_op jit(solution)/shard_map/ppermute | solution.py:52
  24.3 12.5 %collective-permute-start.15 = (bf16[16,4096]{1,0:T(8,128)(2,1)S(1)}, bf16[16,4096]{1,0:T(8,128)(2,1)S(1)}, u32[]{:S(2)}, u32[]{:S(2)}) collective-permute-start(bf16[16,4096]{1,0:T(8,128)(2,1)S(1)} %pad_maximum_fusion.after), channel_id=1, source_target_pairs={{0,3},{1,4},{2,7},{3,0},{4,1},{5,6},{6,5},{7,2},{8,13},{9,10},{10,... | collective-permute-start | bytes 393224 | tf_op jit(solution)/shard_map/ppermute | solution.py:52
  27.0 4.4 %collective-permute-start.13 = (bf16[1,2,16,256]{3,2,1,0:T(8,128)(2,1)S(1)}, bf16[1,2,16,256]{3,2,1,0:T(8,128)(2,1)S(1)}, u32[]{:S(2)}, u32[]{:S(2)}) collective-permute-start(bf16[1,2,16,256]{3,2,1,0:T(8,128)(2,1)S(1)} %shard_map.171.carried.after), channel_id=1, source_target_pairs={{0,9},{1,8},{2,11},{3,10},{4,13},{5,12},{6,15},{7,14},{8,1},{9,0},... | collective-permute-start | bytes 49160 | tf_op jit(solution)/shard_map/ppermute | solution.py:52
  31.4 3.7 %collective-permute-start.14 = (bf16[2,2,16,256]{3,2,1,0:T(8,128)(2,1)S(1)}, bf16[2,2,16,256]{3,2,1,0:T(8,128)(2,1)S(1)}, u32[]{:S(2)}, u32[]{:S(2)}) collective-permute-start(bf16[2,2,16,256]{3,2,1,0:T(8,128)(2,1)S(1)} %constant_dynamic-update-slice_fusion.2.carried.after), channel_id=1, source_target_pairs={{0,5},{1,2},{2,1},{3,6},{4,7},{5,0},{6,3},{7,4},{8,11},{9,12},{10,... | collective-permute-start | bytes 98312 | tf_op jit(solution)/shard_map/ppermute | solution.py:52
  35.1 3.7 %collective-permute-start.16 = (bf16[4,2,16,256]{3,2,1,0:T(8,128)(2,1)S(1)}, bf16[4,2,16,256]{3,2,1,0:T(8,128)(2,1)S(1)}, u32[]{:S(2)}, u32[]{:S(2)}) collective-permute-start(bf16[4,2,16,256]{3,2,1,0:T(8,128)(2,1)S(1)} %constant_dynamic-update-slice_fusion.4.carried), channel_id=1, source_target_pairs={{0,3},{1,4},{2,7},{3,0},{4,1},{5,6},{6,5},{7,2},{8,13},{9,10},{10,... | collective-permute-start | bytes 196616 | tf_op jit(solution)/shard_map/ppermute | solution.py:52
  36.8 3.4 %collective-permute-start.18 = (bf16[32,4096]{1,0:T(8,128)(2,1)S(1)}, bf16[32,4096]{1,0:T(8,128)(2,1)S(1)}, u32[]{:S(2)}, u32[]{:S(2)}) collective-permute-start(bf16[32,4096]{1,0:T(8,128)(2,1)S(1)} %constant_dynamic-update-slice_fusion.6.after.prompts), channel_id=1, source_target_pairs={{0,1},{1,0},{2,3},{3,2},{4,5},{5,4},{6,7},{7,6},{8,9},{9,8},{10,11... | collective-permute-start | bytes 786440 | tf_op jit(solution)/shard_map/ppermute | solution.py:52
  38.8 1.3 %collective-permute-start.17 = (bf16[8,2,16,256]{3,2,1,0:T(8,128)(2,1)S(1)}, bf16[8,2,16,256]{3,2,1,0:T(8,128)(2,1)S(1)}, u32[]{:S(2)}, u32[]{:S(2)}) collective-permute-start(bf16[8,2,16,256]{3,2,1,0:T(8,128)(2,1)S(1)} %constant_dynamic-update-slice_fusion.8.near), channel_id=1, source_target_pairs={{0,1},{1,0},{2,3},{3,2},{4,5},{5,4},{6,7},{7,6},{8,9},{9,8},{10,11... | collective-permute-start | bytes 393224 | tf_op jit(solution)/shard_map/ppermute | solution.py:52
  44.8 1.6 %collective-permute-start.19 = (bf16[32,4096]{1,0:T(8,128)(2,1)S(1)}, bf16[32,4096]{1,0:T(8,128)(2,1)S(1)}, u32[]{:S(2)}, u32[]{:S(2)}) collective-permute-start(bf16[32,4096]{1,0:T(8,128)(2,1)S(1)} %get-tuple-element.78), channel_id=1, source_target_pairs={{0,1},{1,0},{2,3},{3,2},{4,5},{5,4},{6,7},{7,6},{8,9},{9,8},{10,11... | collective-permute-start | bytes 786440 | tf_op jit(solution)/shard_map/ppermute | solution.py:52
  46.5 4.5 %collective-permute-start.20 = (bf16[16,4096]{1,0:T(8,128)(2,1)S(1)}, bf16[16,4096]{1,0:T(8,128)(2,1)S(1)}, u32[]{:S(2)}, u32[]{:S(2)}) collective-permute-start(bf16[16,4096]{1,0:T(8,128)(2,1)S(1)} %slice.41), channel_id=1, source_target_pairs={{0,3},{1,4},{2,7},{3,0},{4,1},{5,6},{6,5},{7,2},{8,13},{9,10},{10,... | collective-permute-start | bytes 393224 | tf_op jit(solution)/shard_map/ppermute | solution.py:52
  51.0 3.8 %collective-permute-start.21 = (bf16[8,4096]{1,0:T(8,128)(2,1)S(1)}, bf16[8,4096]{1,0:T(8,128)(2,1)S(1)}, u32[]{:S(2)}, u32[]{:S(2)}) collective-permute-start(bf16[8,4096]{1,0:T(8,128)(2,1)S(1)} %slice.42), channel_id=1, source_target_pairs={{0,5},{1,2},{2,1},{3,6},{4,7},{5,0},{6,3},{7,4},{8,11},{9,12},{10,... | collective-permute-start | bytes 196616 | tf_op jit(solution)/shard_map/ppermute | solution.py:52
  54.8 4.3 %collective-permute-start.22 = (bf16[4,4096]{1,0:T(4,128)(2,1)S(1)}, bf16[4,4096]{1,0:T(4,128)(2,1)S(1)}, u32[]{:S(2)}, u32[]{:S(2)}) collective-permute-start(bf16[4,4096]{1,0:T(4,128)(2,1)S(1)} %slice.43), channel_id=1, source_target_pairs={{0,9},{1,8},{2,11},{3,10},{4,13},{5,12},{6,15},{7,14},{8,1},{9,0},... | collective-permute-start | bytes 98312 | tf_op jit(solution)/shard_map/ppermute | solution.py:52
